TPU v7x, 32 devices: a whole 2x2x4 slice. The times are simulated.
32 devices in a mesh: batch: 4 (over z), wide: 8 (over y, x, core).
Axes of the slice: x: 2, y: 2, z: 4, core: 2. Of those that a mesh axis runs over, the one named last changes fastest.
Arguments:
- hidden: bfloat16 [16384, 2048], P(('batch', 'wide')), may hold values from -6 to 6
- cotangent: bfloat16 [16384, 2048], P(('batch', 'wide')), may hold values from -6 to 6
- exit_layer: int32 [8, 2048], P('batch'), may hold values from 1 to 24, as said below
- ln1_gain: float32 [2048], replicated, may hold values from 0.1 to 1.9
- ln1_bias: float32 [2048], replicated, may hold values from -4 to 4
- qkv_weight: bfloat16 [6144, 2048], P('wide'), may hold values from -0.125 to 0.125
- query_bias: float32 [2048], replicated, may hold values from -6 to 6
- value_bias: float32 [2048], replicated, may hold values from -3 to 3
- out_weight: bfloat16 [2048, 2048], P('wide'), may hold values from -0.375 to 0.375
- out_bias: float32 [2048], replicated, may hold values from -4 to 4
- ln2_gain: float32 [2048], replicated, may hold values from 0.1 to 1.9
- ln2_bias: float32 [2048], replicated, may hold values from -4 to 4
- up_weight: bfloat16 [8192, 2048], P('wide'), may hold values from -0.125 to 0.125
- up_bias: float32 [8192], replicated, may hold values from -6 to 6
- down_weight: bfloat16 [8192, 2048], P('wide'), may hold values from -0.0625 to 0.0625
- down_bias: float32 [2048], replicated, may hold values from -4 to 4
Outputs:
- layer_output: bfloat16 [16384, 2048], P(('batch', 'wide'))
- input_grad: float32 [16384, 2048], P(('batch', 'wide'))
- ln1_gain_grad: float32 [2048], replicated
- ln1_bias_grad: float32 [2048], replicated
- qkv_weight_grad: float32 [6144, 2048], P('wide')
- query_bias_grad: float32 [2048], replicated
- value_bias_grad: float32 [2048], replicated
- out_weight_grad: float32 [2048, 2048], P('wide')
- out_bias_grad: float32 [2048], replicated
- ln2_gain_grad: float32 [2048], replicated
- ln2_bias_grad: float32 [2048], replicated
- up_weight_grad: float32 [8192, 2048], P('wide')
- up_bias_grad: float32 [8192], replicated
- down_weight_grad: float32 [8192, 2048], P('wide')
- down_bias_grad: float32 [2048], replicated
Inputs may be any that keep to these rules, and one draw needn't show every extreme that they name: `exit_layer`: along each sequence the exit layers fall linearly from its first position to its last (first value minus the floor of the difference times the position over 2048 - 1); every first value is at least 12; in each aligned group of 2 sequences on one index of batch one sequence has every exit layer at least 12.
All inputs are finite; a program needn't handle non-finite values.
Results may differ from a plain program's by a relative error of at most 0.013.
Values may be sent and summed in bfloat16 or wider, within the bound.
No kernel may reach another device: no remote copies, remote signals or barrier semaphores. Data moves between devices by JAX's collectives and lax.ppermute only.
A program may use at most 512 MiB of HBM per device.

v0:
```python
import functools

import jax
import jax.numpy as jnp
import numpy as np
from jax import lax
from jax.experimental import pallas as pl
from jax.experimental.pallas import tpu as pltpu
from jax.sharding import PartitionSpec as P

HEADS = 32
LAYER = 12
LANES = 128
TILE = 512
CHUNKS = 2
LOG2E = 1.4426950408889634

epsilon = 1e-05
VMEM_BYTES = 48 * 2**20


def cost(flops, size, exponentials=0):
    return pl.CostEstimate(flops=flops, bytes_accessed=size, transcendentals=exponentials)


def dot_nt(left, right):
    return lax.dot_general(
        left, right, (((1,), (1,)), ((), ())), preferred_element_type=jnp.float32
    )


def dot_nn(left, right):
    return lax.dot_general(
        left, right, (((1,), (0,)), ((), ())), preferred_element_type=jnp.float32
    )


def dot_tn(left, right):
    return lax.dot_general(
        left, right, (((0,), (0,)), ((), ())), preferred_element_type=jnp.float32
    )


def head_masks(head_size):
    lane = lax.broadcasted_iota(jnp.int32, (1, LANES), 1)
    return [
        (lane >= h * head_size) & (lane < (h + 1) * head_size)
        for h in range(LANES // head_size)
    ]


def fetch(sources, target, sems):
    size = target.shape[1]
    copies = []
    row = 0
    for source in sources:
        rows = source.shape[0]
        least = min(rows, size)
        for k in range(rows // least):
            place = target.at[row // size, pl.ds(row % size, least)]
            copies.append(
                pltpu.make_async_copy(source.at[pl.ds(k * least, least)], place, sems.at[len(copies)])
            )
            row += least

    @pl.when(pl.program_id(0) == 0)
    def _():
        for copy in copies:
            copy.start()
        for copy in copies:
            copy.wait()


def attend_kernel(head_size, blocks_in, counts, slots, *refs):
    sources = refs[:blocks_in]
    out_ref, log_ref, mixed_ref, key_own, value_own, sems = refs[blocks_in:]
    fetch(sources, mixed_ref, sems)
    length, lanes = out_ref.shape
    tile = mixed_ref.shape[1]
    pack = LANES // head_size
    scale = head_size ** (-0.5) * LOG2E
    sequence = pl.program_id(0)
    blocks = lax.div(counts[sequence] + (tile - 1), tile)
    masks = head_masks(head_size)
    out_ref[...] = jnp.zeros(out_ref.shape, out_ref.dtype)
    log_ref[...] = jnp.zeros(log_ref.shape, log_ref.dtype)
    row = lax.broadcasted_iota(jnp.int32, (tile, tile), 0)
    col = lax.broadcasted_iota(jnp.int32, (tile, tile), 1)
    for pair in range(lanes // LANES):
        base = pair * LANES
        for i in range(length // tile):
            slot = slots[sequence, i]
            keys = mixed_ref[slot, :, lanes + base : lanes + base + LANES]
            values = mixed_ref[slot, :, 2 * lanes + base : 2 * lanes + base + LANES]
            for h in range(pack):
                key_own[h, i * tile : (i + 1) * tile] = jnp.where(masks[h], keys, jnp.zeros_like(keys))
                value_own[h, i * tile : (i + 1) * tile] = jnp.where(
                    masks[h], values, jnp.zeros_like(values)
                )

        def query_block(i, _, pair=pair, base=base):
            start = pl.multiple_of(i * tile, tile)
            queries = mixed_ref[slots[sequence, i], :, base : base + LANES]

            def step(j, carry, diagonal=False):
                total, tops, sums = carry
                first = pl.multiple_of(j * tile, tile)
                new_tops, new_sums, shrinks, adds = [], [], [], []
                for h in range(pack):
                    scores = dot_nt(queries, key_own[h, pl.ds(first, tile)]) * scale
                    if diagonal:
                        scores = jnp.where(col <= row, scores, -1e30)
                    top = jnp.maximum(tops[h], jnp.max(scores, axis=1, keepdims=True))
                    terms = jnp.exp2(scores - top)
                    shrink = jnp.exp2(tops[h] - top)
                    new_tops.append(top)
                    new_sums.append(sums[h] * shrink + jnp.sum(terms, axis=1, keepdims=True))
                    shrinks.append(shrink)
                    adds.append(dot_nn(terms.astype(jnp.bfloat16), value_own[h, pl.ds(first, tile)]))
                shrink = shrinks[0]
                for h in range(1, pack):
                    shrink = jnp.where(masks[h], shrinks[h], shrink)
                total = total * shrink
                for add in adds:
                    total = total + add
                return total, tuple(new_tops), tuple(new_sums)

            carry = (
                jnp.zeros((tile, LANES), jnp.float32),
                tuple(jnp.full((tile, 1), -1e30, jnp.float32) for _ in range(pack)),
                tuple(jnp.zeros((tile, 1), jnp.float32) for _ in range(pack)),
            )
            carry = lax.fori_loop(0, i, step, carry)
            total, tops, sums = step(i, carry, diagonal=True)
            share = 1.0 / sums[0]
            for h in range(1, pack):
                share = jnp.where(masks[h], 1.0 / sums[h], share)
            out_ref[pl.ds(start, tile), base : base + LANES] = (total * share).astype(out_ref.dtype)
            for h in range(pack):
                logs = jnp.broadcast_to(tops[h] + jnp.log2(sums[h]), (tile, LANES))
                index = pair * pack + h
                log_ref[0, index : index + 1, pl.ds(start, tile)] = jnp.transpose(logs)[0:1]
            return 0

        lax.fori_loop(0, blocks, query_block, 0)


def attend(mixed, slots, counts, head_size):
    sequences = counts.shape[0]
    rows = sum(part.shape[0] for part in mixed)
    tile = rows // slots.size
    blocks = rows // tile
    lanes = mixed[0].shape[1] // 3
    length = rows // sequences
    heads = lanes // head_size
    pack = LANES // head_size
    return pl.pallas_call(
        functools.partial(attend_kernel, head_size, len(mixed)),
        grid_spec=pltpu.PrefetchScalarGridSpec(
            num_scalar_prefetch=2,
            grid=(sequences,),
            in_specs=[pl.BlockSpec(memory_space=pl.ANY)] * len(mixed),
            out_specs=[
                pl.BlockSpec((length, lanes), lambda s, *_: (s, 0)),
                pl.BlockSpec((1, heads, length), lambda s, *_: (s, 0, 0)),
            ],
            scratch_shapes=[
                pltpu.VMEM((blocks, tile, 3 * lanes), jnp.bfloat16),
                pltpu.VMEM((pack, length, LANES), jnp.bfloat16),
                pltpu.VMEM((pack, length, LANES), jnp.bfloat16),
                pltpu.SemaphoreType.DMA((blocks,)),
            ],
        ),
        out_shape=[
            jax.ShapeDtypeStruct((rows, lanes), jnp.bfloat16),
            jax.ShapeDtypeStruct((sequences, heads, length), jnp.float32),
        ],
        compiler_params=pltpu.CompilerParams(vmem_limit_bytes=VMEM_BYTES),
        cost_estimate=cost(rows * length * lanes * 2, rows * lanes * 8, rows * length * heads // 2),
    )(counts, slots, *mixed)


def attend_back_kernel(
    head_size,
    blocks_in,
    counts,
    slots,
    *refs,
):
    sources = refs[:blocks_in]
    grad_ref, out_ref, log_ref, own_ref, other_ref, mixed_ref = refs[blocks_in : blocks_in + 6]
    query_own, key_own, grad_own, delta, grad_query, grad_key, grad_value, back_ref, sems = refs[
        blocks_in + 6 :
    ]
    fetch(sources, mixed_ref, sems)
    length, lanes = out_ref.shape
    tile = mixed_ref.shape[1]
    pack = LANES // head_size
    scale = head_size ** (-0.5)
    sequence = pl.program_id(0)
    blocks = lax.div(counts[sequence] + (tile - 1), tile)
    masks = head_masks(head_size)
    for i in range(length // tile):
        back_ref[slots[sequence, i]] = jnp.zeros((tile, 3 * lanes), back_ref.dtype)
    key_row = lax.broadcasted_iota(jnp.int32, (tile, tile), 0)
    query_col = lax.broadcasted_iota(jnp.int32, (tile, tile), 1)
    for pair in range(lanes // LANES):
        base = pair * LANES
        for i in range(length // tile):
            span = slice(i * tile, (i + 1) * tile)
            slot = slots[sequence, i]
            queries = mixed_ref[slot, :, base : base + LANES]
            keys = mixed_ref[slot, :, lanes + base : lanes + base + LANES]
            grads = grad_ref[span, base : base + LANES]
            for h in range(pack):
                query_own[h, span] = jnp.where(masks[h], queries, jnp.zeros_like(queries))
                key_own[h, span] = jnp.where(masks[h], keys, jnp.zeros_like(keys))
                grad_own[h, span] = jnp.where(masks[h], grads, jnp.zeros_like(grads))
        grad_query[...] = jnp.zeros(grad_query.shape, jnp.float32)

        def deltas(i, _, base=base):
            start = pl.multiple_of(i * tile, tile)
            grads = grad_ref[pl.ds(start, tile), base : base + LANES].astype(jnp.float32)
            outs = out_ref[pl.ds(start, tile), base : base + LANES].astype(jnp.float32)
            products = jnp.transpose(grads * outs)
            for h in range(pack):
                delta[h : h + 1, pl.ds(start, tile)] = jnp.sum(
                    products[h * head_size : (h + 1) * head_size], axis=0, keepdims=True
                )
            return 0

        lax.fori_loop(0, blocks, deltas, 0)

        def key_block(j, _, pair=pair, base=base):
            first = pl.multiple_of(j * tile, tile)
            place = slots[sequence, j]
            keys = mixed_ref[place, :, lanes + base : lanes + base + LANES]
            values = mixed_ref[place, :, 2 * lanes + base : 2 * lanes + base + LANES]
            grad_key[...] = jnp.zeros(grad_key.shape, jnp.float32)
            grad_value[...] = jnp.zeros(grad_value.shape, jnp.float32)

            def step(i, diagonal=False):
                start = pl.multiple_of(i * tile, tile)
                add_query, add_key, add_value = [], [], []
                for h in range(pack):
                    index = pair * pack + h
                    query_head = query_own[h, pl.ds(start, tile)]
                    grad_head = grad_own[h, pl.ds(start, tile)]
                    scores = dot_nt(keys, query_head) * (scale * LOG2E)
                    probs = jnp.exp2(scores - log_ref[0, index : index + 1, pl.ds(start, tile)])
                    if diagonal:
                        probs = jnp.where(key_row <= query_col, probs, 0.0)
                    grad_probs = dot_nt(values, grad_head)
                    grad_scores = (
                        probs * (grad_probs - delta[h : h + 1, pl.ds(start, tile)])
                    ).astype(jnp.bfloat16)
                    add_value.append(dot_nn(probs.astype(jnp.bfloat16), grad_head))
                    add_key.append(dot_nn(grad_scores, query_head))
                    add_query.append(dot_tn(grad_scores, key_own[h, pl.ds(first, tile)]))
                grad_value[...] += functools.reduce(jnp.add, add_value)
                grad_key[...] += functools.reduce(jnp.add, add_key)
                grad_query[pl.ds(start, tile), :] += functools.reduce(jnp.add, add_query)

            def off_diagonal(i, _):
                step(i)
                return 0

            step(j, diagonal=True)
            lax.fori_loop(j + 1, blocks, off_diagonal, 0)
            back_ref[place, :, lanes + base : lanes + base + LANES] = (grad_key[...] * scale).astype(
                back_ref.dtype
            )
            back_ref[place, :, 2 * lanes + base : 2 * lanes + base + LANES] = grad_value[...].astype(
                back_ref.dtype
            )
            return 0

        lax.fori_loop(0, blocks, key_block, 0)
        for i in range(length // tile):
            back_ref[slots[sequence, i], :, base : base + LANES] = (
                grad_query[i * tile : (i + 1) * tile] * scale
            ).astype(back_ref.dtype)

    @pl.when(sequence == pl.num_programs(0) - 1)
    def _():
        half = back_ref.shape[0] // 2
        for k in range(half):
            own_ref[k * tile : (k + 1) * tile] = back_ref[k]
            other_ref[k * tile : (k + 1) * tile] = back_ref[half + k]


def attend_back(mixed, slots, grads, outs, logs, counts, head_size):
    sequences = counts.shape[0]
    rows, lanes = outs.shape
    length = rows // sequences
    heads = lanes // head_size
    pack = LANES // head_size
    tile = rows // slots.size
    blocks = rows // tile
    whole = pl.BlockSpec((rows // 2, 3 * lanes), lambda s, *_: (0, 0))
    return pl.pallas_call(
        functools.partial(attend_back_kernel, head_size, len(mixed)),
        grid_spec=pltpu.PrefetchScalarGridSpec(
            num_scalar_prefetch=2,
            grid=(sequences,),
            in_specs=[pl.BlockSpec(memory_space=pl.ANY)] * len(mixed)
            + [
                pl.BlockSpec((length, lanes), lambda s, *_: (s, 0)),
                pl.BlockSpec((length, lanes), lambda s, *_: (s, 0)),
                pl.BlockSpec((1, heads, length), lambda s, *_: (s, 0, 0)),
            ],
            out_specs=[whole, whole],
            scratch_shapes=[
                pltpu.VMEM((blocks, tile, 3 * lanes), jnp.bfloat16),
                pltpu.VMEM((pack, length, LANES), jnp.bfloat16),
                pltpu.VMEM((pack, length, LANES), jnp.bfloat16),
                pltpu.VMEM((pack, length, LANES), jnp.bfloat16),
                pltpu.VMEM((pack, length), jnp.float32),
                pltpu.VMEM((length, LANES), jnp.float32),
                pltpu.VMEM((tile, LANES), jnp.float32),
                pltpu.VMEM((tile, LANES), jnp.float32),
                pltpu.VMEM((blocks, tile, 3 * lanes), jnp.bfloat16),
                pltpu.SemaphoreType.DMA((blocks,)),
            ],
        ),
        out_shape=[jax.ShapeDtypeStruct((rows // 2, 3 * lanes), jnp.bfloat16)] * 2,
        compiler_params=pltpu.CompilerParams(vmem_limit_bytes=VMEM_BYTES),
        cost_estimate=cost(1, 1),
    )(counts, slots, *mixed, grads, outs, logs)


def ffn_kernel(block, x_parts, g_parts, counts, *refs):
    xs, refs = refs[:x_parts], refs[x_parts:]
    gs, refs = refs[:g_parts], refs[g_parts:]
    ups, downs, shifts = refs[0:2], refs[2:4], refs[4:6]
    units_ref, back_ref, out_ref, x, g, total, x_sems, g_sems = refs[-8:]
    fetch(xs, x, x_sems)
    fetch(gs, g, g_sems)
    blocks, size, model = x.shape
    width = ups[0].shape[0]
    step = pl.program_id(0)

    @pl.when(step == 0)
    def _():
        total[...] = jnp.zeros(total.shape, total.dtype)

    for k in range(blocks):
        rows = slice(k * size, (k + 1) * size)

        @pl.when(counts[block + k] != 0)
        def _(k=k, rows=rows):
            backs = []
            for side in range(2):
                span = slice(side * width, (side + 1) * width)
                pre = dot_nt(x[k], ups[side][...]) + shifts[side][...]
                grad_units = dot_nt(g[k], downs[side][...])
                size_of = jnp.abs(pre)
                bell = jnp.exp2(pre * pre * (-0.5 * LOG2E))
                denominator = 1.0 + (0.3275911 * 0.7071067811865476) * size_of
                t = pl.reciprocal(denominator, approx=True)
                t = t * (2.0 - denominator * t)
                tail = 0.5 * 1.061405429
                for factor in (-1.453152027, 1.421413741, -0.284496736, 0.254829592):
                    tail = tail * t + 0.5 * factor
                tail = tail * t
                units = jnp.maximum(pre, 0.0) - size_of * (tail * bell)
                units_ref[rows, span] = units.astype(units_ref.dtype)
                slope = (tail - size_of * 0.3989422804014327) * bell
                slope = jnp.where(pre < 0, slope, 1.0 - slope)
                backs.append((grad_units * slope).astype(back_ref.dtype))
                back_ref[rows, span] = backs[-1]
            total[rows] += dot_nn(backs[0], ups[0][...]) + dot_nn(backs[1], ups[1][...])

        @pl.when(counts[block + k] == 0)
        def _(rows=rows):
            units_ref[rows] = jnp.zeros((size, 2 * width), units_ref.dtype)
            back_ref[rows] = jnp.zeros((size, 2 * width), back_ref.dtype)

    @pl.when(step == pl.num_programs(0) - 1)
    def _():
        out_ref[...] = total[...].astype(out_ref.dtype)


def ffn_blocks(place, block, counts, xs, gs, ups, downs, shifts, kept):
    size, width = 512, 256
    model = xs[0].shape[1]
    rows = sum(x.shape[0] for x in xs)
    units = ups[0].shape[0]
    whole = pl.BlockSpec(memory_space=pl.ANY)
    weights = pl.BlockSpec((width, model), lambda u, *_: (u, 0))
    shift = pl.BlockSpec((1, width), lambda u, *_: (0, u))
    output = pl.BlockSpec((rows, 2 * width), lambda u, *_: (place, u))
    full = jax.ShapeDtypeStruct((4 * size, 2 * units), jnp.bfloat16)
    return pl.pallas_call(
        functools.partial(ffn_kernel, block, len(xs), len(gs)),
        grid_spec=pltpu.PrefetchScalarGridSpec(
            num_scalar_prefetch=1,
            grid=(units // width,),
            in_specs=[whole] * (len(xs) + len(gs))
            + [weights] * 4
            + [shift] * 2
            + [whole] * len(kept),
            out_specs=[output, output, pl.BlockSpec((rows, model), lambda u, *_: (0, 0))],
            scratch_shapes=[
                pltpu.VMEM((rows // size, size, model), jnp.bfloat16),
                pltpu.VMEM((rows // size, size, model), jnp.bfloat16),
                pltpu.VMEM((rows, model), jnp.float32),
                pltpu.SemaphoreType.DMA((len(xs),)),
                pltpu.SemaphoreType.DMA((len(gs),)),
            ],
        ),
        out_shape=[full, full, jax.ShapeDtypeStruct((rows, model), jnp.bfloat16)],
        input_output_aliases={len(xs) + len(gs) + 7 + k: k for k in range(len(kept))},
        compiler_params=pltpu.CompilerParams(vmem_limit_bytes=VMEM_BYTES),
        cost_estimate=cost(12 * rows * units * model, 8 * units * model + 8 * rows * model, 4 * rows * units),
    )(counts, *xs, *gs, *ups, *downs, *shifts, *kept)


def arrange(outs, total):
    to_x, to_y, rest = outs
    half = total.shape[0] // 2
    top, bottom = total[:half].astype(to_x.dtype), total[half:].astype(to_x.dtype)
    step = pl.program_id(0)

    @pl.when(step == 0)
    def _():
        to_x[:half] = top
        to_y[:half] = bottom

    @pl.when(step == 1)
    def _():
        to_x[half:] = top
        rest[half : 2 * half] = bottom

    @pl.when(step == 2)
    def _():
        rest[:half] = top
        to_y[half:] = bottom

    @pl.when(step == 3)
    def _():
        rest[2 * half : 3 * half] = top
        rest[3 * half :] = bottom


def arranged(rows, columns):
    sizes = (rows // 4, rows // 4, rows // 2)
    specs = [pl.BlockSpec((size, columns), lambda i, *_: (0, 0)) for size in sizes]
    return specs, [jax.ShapeDtypeStruct((size, columns), jnp.bfloat16) for size in sizes]


def products_kernel(width, order, active, left, own, other, *outs):
    here = active[order[pl.program_id(0)]] != 0

    @pl.when(here)
    def _():
        total = None
        for k in range(own.shape[0] // width):
            rows = slice(k * width, (k + 1) * width)
            for side, right in enumerate((own, other)):
                start = (2 * k + side) * width
                term = dot_nn(left[:, start : start + width], right[rows])
                total = term if total is None else total + term
        arrange(outs, total)

    @pl.when(jnp.logical_not(here))
    def _():
        arrange(outs, jnp.zeros((left.shape[0], own.shape[1]), jnp.float32))


def products(order, counts, left, own, other):
    blocks = counts.shape[0]
    rows, depth = left.shape
    columns = own.shape[1]
    specs, shapes = arranged(rows, columns)
    return pl.pallas_call(
        functools.partial(products_kernel, 256),
        grid_spec=pltpu.PrefetchScalarGridSpec(
            num_scalar_prefetch=2,
            grid=(blocks,),
            in_specs=[
                pl.BlockSpec((rows // blocks, depth), lambda i, order, *_: (order[i], 0)),
                pl.BlockSpec(own.shape, lambda i, *_: (0, 0)),
                pl.BlockSpec(own.shape, lambda i, *_: (0, 0)),
            ],
            out_specs=specs,
        ),
        out_shape=shapes,
        compiler_params=pltpu.CompilerParams(vmem_limit_bytes=VMEM_BYTES),
        cost_estimate=cost(1, 1),
    )(order, counts, left, own, other)


def attend_out_kernel(left, weight, bias, hidden, active, out_ref):
    out_ref[...] = hidden[...].astype(jnp.float32) + active[...] * (
        dot_nn(left[...], weight[...]) + bias[...]
    )


def attend_out(left, weight, bias, hidden, active):
    rows, depth = left.shape
    columns = weight.shape[1]
    width = 512
    column = pl.BlockSpec((rows, width), lambda j: (0, j))
    return pl.pallas_call(
        attend_out_kernel,
        grid=(columns // width,),
        in_specs=[
            pl.BlockSpec((rows, depth), lambda j: (0, 0)),
            pl.BlockSpec((depth, width), lambda j: (0, j)),
            pl.BlockSpec((1, width), lambda j: (0, j)),
            column,
            pl.BlockSpec((rows, 1), lambda j: (0, 0)),
        ],
        out_specs=column,
        out_shape=jax.ShapeDtypeStruct((rows, columns), jnp.float32),
        compiler_params=pltpu.CompilerParams(vmem_limit_bytes=VMEM_BYTES),
        cost_estimate=cost(2 * rows * depth * columns, 2 * depth * columns + 8 * rows * columns),
    )(left, weight, bias[None], hidden, active)


def attend_out_back_kernel(grad, weight, out_ref):
    out_ref[...] = dot_nt(grad[...], weight[...]).astype(out_ref.dtype)


def attend_out_back(grad, weight):
    rows, columns = grad.shape
    depth = weight.shape[0]
    width = 512
    return pl.pallas_call(
        attend_out_back_kernel,
        grid=(depth // width,),
        in_specs=[
            pl.BlockSpec((rows, columns), lambda j: (0, 0)),
            pl.BlockSpec((width, columns), lambda j: (j, 0)),
        ],
        out_specs=pl.BlockSpec((rows, width), lambda j: (0, j)),
        out_shape=jax.ShapeDtypeStruct((rows, depth), jnp.bfloat16),
        compiler_params=pltpu.CompilerParams(vmem_limit_bytes=VMEM_BYTES),
        cost_estimate=cost(1, 1),
    )(grad, weight)


def project_kernel(inputs, side, parts, *refs):
    xs = refs[:inputs]
    weights, shift, out_ref = refs[inputs:]
    slab = weights.shape[1]
    weight = weights[...].reshape(3 * slab, weights.shape[2])
    for k in range(inputs):

        @pl.when(pl.program_id(0) == k)
        def _(k=k):
            mixed = dot_nt(xs[k][...], weight)
            for t in range(3):
                columns = pl.ds(pl.multiple_of(parts[side, t] * slab, slab), slab)
                out_ref[:, columns] = (
                    mixed[:, t * slab : (t + 1) * slab] + shift[:, columns]
                ).astype(out_ref.dtype)


def project(parts, side, xs, weights, shift):
    size, model = xs[0].shape
    slab = weights.shape[1]
    return pl.pallas_call(
        functools.partial(project_kernel, len(xs), side),
        grid_spec=pltpu.PrefetchScalarGridSpec(
            num_scalar_prefetch=1,
            grid=(len(xs),),
            in_specs=[pl.BlockSpec((size, model), lambda i, *_: (0, 0))] * len(xs)
            + [
                pl.BlockSpec(weights.shape, lambda i, *_: (0, 0, 0)),
                pl.BlockSpec(shift.shape, lambda i, *_: (0, 0)),
            ],
            out_specs=pl.BlockSpec((size, 3 * slab), lambda i, *_: (i, 0)),
        ),
        out_shape=jax.ShapeDtypeStruct((len(xs) * size, 3 * slab), jnp.bfloat16),
        compiler_params=pltpu.CompilerParams(vmem_limit_bytes=VMEM_BYTES),
        cost_estimate=pl.CostEstimate(
            flops=6 * len(xs) * size * slab * model,
            bytes_accessed=6 * slab * model + 2 * len(xs) * size * (model + 3 * slab),
            transcendentals=0,
        ),
    )(parts, *xs, weights, shift)


def unproject_kernel(order, parts, active, mine, theirs, own, other, *outs):
    slab = own.shape[1]
    here = active[order[pl.program_id(0)]] != 0

    @pl.when(here)
    def _():
        total = None
        for side, (left, right) in enumerate(((mine, own), (theirs, other))):
            for t in range(3):
                columns = pl.ds(pl.multiple_of(parts[side, t] * slab, slab), slab)
                term = dot_nn(left[:, columns], right[t])
                total = term if total is None else total + term
        arrange(outs, total)

    @pl.when(jnp.logical_not(here))
    def _():
        arrange(outs, jnp.zeros((mine.shape[0], own.shape[2]), jnp.float32))


def unproject(order, parts, counts, mine, theirs, own, other):
    blocks = counts.shape[0]
    rows = mine.shape[0]
    slab, model = own.shape[1:]
    left = pl.BlockSpec((rows // blocks, 3 * slab), lambda i, order, *_: (order[i], 0))
    fixed = pl.BlockSpec(own.shape, lambda i, *_: (0, 0, 0))
    specs, shapes = arranged(rows, model)
    return pl.pallas_call(
        unproject_kernel,
        grid_spec=pltpu.PrefetchScalarGridSpec(
            num_scalar_prefetch=3,
            grid=(blocks,),
            in_specs=[left, left, fixed, fixed],
            out_specs=specs,
        ),
        out_shape=shapes,
        compiler_params=pltpu.CompilerParams(vmem_limit_bytes=VMEM_BYTES),
        cost_estimate=cost(1, 1),
    )(order, parts, counts, mine, theirs, own, other)


def weight_grad_kernel(inputs, added, columns, *refs):
    left, rights = refs[0], refs[1 : 1 + inputs]
    tokens, sems = refs[-2:]
    outs = refs[1 + inputs + added : -2]
    fetch(rights, tokens, sems)
    total = dot_tn(left[...], tokens[0])
    if added:
        total = total + refs[1 + inputs][...].astype(jnp.float32)
    size = outs[0].shape[0]
    if size == total.shape[0]:
        for k, out_ref in enumerate(outs):

            @pl.when((len(outs) == 1) | (pl.program_id(0) == k))
            def _(out_ref=out_ref):
                out_ref[...] = total.astype(out_ref.dtype)

    else:
        for k, out_ref in enumerate(outs):
            out_ref[...] = total[k * size : (k + 1) * size].astype(out_ref.dtype)


def weight_grad(left, columns, tile, rights, extra=None, outputs=1, apart=False):
    rows = left.shape[0]
    model = rights[0].shape[1]
    steps = columns.shape[0]
    output = pl.BlockSpec((tile // outputs, model), lambda i, *_: (i, 0))
    extras = [] if extra is None else [extra]
    shape = jax.ShapeDtypeStruct((steps * tile // outputs, model), jnp.bfloat16)
    added = [output] * len(extras)
    if apart:
        outputs = steps
        output = pl.BlockSpec((tile, model), lambda i, *_: (0, 0))
        shape = jax.ShapeDtypeStruct((tile, model), jnp.bfloat16)
    results = pl.pallas_call(
        functools.partial(weight_grad_kernel, len(rights), len(extras)),
        grid_spec=pltpu.PrefetchScalarGridSpec(
            num_scalar_prefetch=1,
            grid=(steps,),
            in_specs=[pl.BlockSpec((rows, tile), lambda i, columns: (0, columns[i]))]
            + [pl.BlockSpec(memory_space=pl.ANY)] * len(rights)
            + added,
            out_specs=[output] * outputs,
            scratch_shapes=[
                pltpu.VMEM((1, rows, model), jnp.bfloat16),
                pltpu.SemaphoreType.DMA((len(rights),)),
            ],
        ),
        out_shape=[shape] * outputs,
        compiler_params=pltpu.CompilerParams(vmem_limit_bytes=VMEM_BYTES),
        cost_estimate=cost(1, 1),
    )(columns, left, *rights, *extras)
    return results[0] if outputs == 1 else results


def chain_sum(values, axis):
    size = lax.axis_size(axis)
    if size != 4:
        return lax.psum(values.astype(jnp.bfloat16), axis).astype(jnp.float32)
    place = lax.axis_index(axis)
    outer = lax.ppermute(values.astype(jnp.bfloat16), axis, [(0, 1), (3, 2)])
    half = (values + outer.astype(jnp.float32)).astype(jnp.bfloat16)
    other = lax.ppermute(half, axis, [(1, 2), (2, 1)])
    whole = (half.astype(jnp.float32) + other.astype(jnp.float32)).astype(jnp.bfloat16)
    ends = lax.ppermute(whole, axis, [(1, 0), (2, 3)])
    inner = (place == 1) | (place == 2)
    return jnp.where(inner, whole, ends).astype(jnp.float32)


def normalize(values):
    center = values - jnp.mean(values, axis=-1, keepdims=True)
    inverse = lax.rsqrt(jnp.mean(center * center, axis=-1, keepdims=True) + epsilon)
    return center * inverse, inverse


def normalize_back(grad, gain, normal, inverse):
    scaled = grad * gain
    grad_values = inverse * (
        scaled
        - jnp.mean(scaled, axis=-1, keepdims=True)
        - normal * jnp.mean(scaled * normal, axis=-1, keepdims=True)
    )
    return grad_values, jnp.sum(grad * normal, axis=0), jnp.sum(grad, axis=0)


def local_general(
    hidden,
    cotangent,
    exit_layer,
    ln1_gain,
    ln1_bias,
    qkv_weight,
    query_bias,
    value_bias,
    out_weight,
    out_bias,
    ln2_gain,
    ln2_bias,
    up_weight,
    up_bias,
    down_weight,
    down_bias,
):
    width = lax.axis_size("wide")
    rank = lax.axis_index("wide")
    rows, model = hidden.shape
    group = rows * width
    slab = model // width
    head_size = model // HEADS
    units_own = up_weight.shape[0]
    keep = exit_layer >= LAYER
    counts = jnp.sum(keep.astype(jnp.int32), axis=1)
    active = lax.dynamic_slice_in_dim(keep.reshape(group), rank * rows, rows, 0)
    active = active.astype(jnp.float32)[:, None]
    grad_out = cotangent.astype(jnp.float32)

    routes = [[(w, (3 * w + t) % width) for w in range(width)] for t in range(3)]
    part_at = np.zeros((width, 3), np.int32)
    for t in range(3):
        for w, d in routes[t]:
            part_at[d, t] = (3 * w + t) // width
    place_of = jnp.asarray(np.argsort(part_at, axis=1).astype(np.int32))[rank]
    part_of = jnp.asarray(part_at)[rank]

    hidden_wide = hidden.astype(jnp.float32)
    normal1, inverse1 = normalize(hidden_wide)
    normed1 = lax.all_gather(
        (normal1 * ln1_gain + ln1_bias).astype(jnp.bfloat16), "wide", axis=0, tiled=True
    )
    slabs = qkv_weight.reshape(3, slab, model)
    received = jnp.stack([lax.ppermute(slabs[t], "wide", routes[t]) for t in range(3)])
    qkv_own = jnp.concatenate(
        [lax.dynamic_index_in_dim(received, place_of[p], 0, keepdims=False) for p in range(3)]
    )
    own = lambda vector: lax.dynamic_slice_in_dim(vector, rank * slab, slab, 0)
    qkv_shift = jnp.concatenate(
        [own(query_bias), jnp.zeros((slab,), jnp.float32), own(value_bias)]
    )

    grad_ffn = (active * grad_out).astype(jnp.bfloat16)
    down_bias_grad = jnp.sum(grad_ffn.astype(jnp.float32), axis=0)
    piece = rows // CHUNKS
    part = lambda values, c: values[c * piece : (c + 1) * piece]
    gather = lambda values: lax.all_gather(values, "wide", axis=0, tiled=True)
    scatter = lambda values: lax.psum_scatter(
        values.astype(jnp.bfloat16), "wide", scatter_dimension=0, tiled=True
    )
    grad_ffns = [gather(part(grad_ffn, c)) for c in range(CHUNKS)]
    out_whole = gather(out_weight)

    mixed = (dot_nt(normed1, qkv_own) + qkv_shift).astype(jnp.bfloat16)
    mixed = jnp.split(mixed, group // TILE)
    slots = jnp.arange(group // TILE, dtype=jnp.int32).reshape(counts.shape[0], -1)
    attended, logs = attend(mixed, slots, counts, head_size)
    attended_rows = lax.all_to_all(attended, "wide", split_axis=0, concat_axis=1, tiled=True)
    middle = hidden_wide + active * (dot_nn(attended_rows, out_whole) + out_bias)
    normal2, inverse2 = normalize(middle)
    normed2 = (normal2 * ln2_gain + ln2_bias).astype(jnp.bfloat16)
    up_shift = lax.dynamic_slice_in_dim(up_bias, rank * units_own, units_own, 0)

    normed2s = [gather(part(normed2, c)) for c in range(CHUNKS)]
    units, grad_pres, grad_normed2, ffn_out = [], [], [], []
    for c in range(CHUNKS):
        grad_units = dot_nt(grad_ffns[c], down_weight)
        pre = dot_nt(normed2s[c], up_weight) + up_shift
        below = 0.5 + 0.5 * lax.erf(pre * 0.7071067811865476)
        bell = jnp.exp(-0.5 * pre * pre) * 0.3989422804014327
        units.append((pre * below).astype(jnp.bfloat16))
        grad_pres.append((grad_units * (below + pre * bell)).astype(jnp.bfloat16))
        grad_normed2.append(scatter(dot_nn(grad_pres[c], up_weight)))
    for c in range(CHUNKS):
        ffn_out.append(scatter(dot_nn(units[c], down_weight)))
    grad_normed2 = jnp.concatenate(grad_normed2).astype(jnp.float32)
    ffn_out = jnp.concatenate(ffn_out).astype(jnp.float32)
    output = (middle + active * (ffn_out + down_bias)).astype(jnp.bfloat16)

    up_bias_own = sum(jnp.sum(g.astype(jnp.float32), axis=0) for g in grad_pres)
    down_grad = sum(dot_tn(units[c], grad_ffns[c]) for c in range(CHUNKS))
    up_grad = sum(dot_tn(grad_pres[c], normed2s[c]) for c in range(CHUNKS))
    halves = lambda values: jnp.concatenate(
        [chain_sum(half, "batch") for half in jnp.split(values, 2)]
    )
    down_grad = halves(down_grad)
    up_grad = halves(up_grad)

    grad_middle, ln2_gain_grad, ln2_bias_grad = normalize_back(
        grad_normed2, ln2_gain, normal2, inverse2
    )
    grad_middle = grad_out + grad_middle
    grad_branch = (active * grad_middle).astype(jnp.bfloat16)
    out_bias_grad = jnp.sum(grad_branch.astype(jnp.float32), axis=0)
    grad_attended = dot_nt(grad_branch, out_whole).astype(jnp.bfloat16)
    grad_heads = lax.all_to_all(grad_attended, "wide", split_axis=1, concat_axis=0, tiled=True)
    out_grad = chain_sum(scatter(dot_tn(attended_rows, grad_branch)).astype(jnp.float32), "batch")

    placed = lambda vector, size: lax.dynamic_update_slice_in_dim(
        jnp.zeros((size,), jnp.float32), vector, rank * vector.shape[0], 0
    )
    early = lax.psum(
        (
            out_bias_grad,
            ln2_gain_grad,
            ln2_bias_grad,
            placed(up_bias_own, up_bias.shape[0]),
            down_bias_grad,
        ),
        ("batch", "wide"),
    )

    grad_mixed = jnp.concatenate(
        attend_back(mixed, slots, grad_heads, attended, logs, counts, head_size)
    )
    grad_normed1 = scatter(dot_nn(grad_mixed, qkv_own)).astype(jnp.float32)
    sums = jnp.sum(grad_mixed.astype(jnp.float32), axis=0)
    qkv_parts = []
    for t in range(3):
        columns = lax.dynamic_slice_in_dim(grad_mixed, part_of[t] * slab, slab, 1)
        total = chain_sum(dot_tn(columns, normed1), "batch").astype(jnp.bfloat16)
        back = [(d, w) for w, d in routes[t]]
        qkv_parts.append(lax.ppermute(total, "wide", back).astype(jnp.float32))
    qkv_grad = jnp.concatenate(qkv_parts)

    grad_hidden, ln1_gain_grad, ln1_bias_grad = normalize_back(
        grad_normed1, ln1_gain, normal1, inverse1
    )
    input_grad = grad_middle + grad_hidden
    late = lax.psum(
        (
            ln1_gain_grad,
            ln1_bias_grad,
            placed(sums[:slab], model),
            placed(sums[2 * slab :], model),
        ),
        ("batch", "wide"),
    )
    return (
        output,
        input_grad,
        late[0],
        late[1],
        qkv_grad,
        late[2],
        late[3],
        out_grad,
        early[0],
        early[1],
        early[2],
        up_grad,
        early[3],
        down_grad,
        early[4],
    )


def swap(values, bits):
    width = lax.axis_size("wide")
    return lax.ppermute(values, "wide", [(w, w ^ bits) for w in range(width)])


def after(values, *done):
    return lax.optimization_barrier((values, done))[0]


def relay(along_x, along_y):
    half = along_x.shape[0] // 2
    return [swap(along_y[:half], 2), swap(along_x[half:], 4)]


class Scatter:
    def __init__(self, to_x, to_y, rest):
        self.half = half = to_x.shape[0] // 2
        self.sent = (to_x, to_y)
        self.rest = rest
        self.from_x, self.from_y = swap(to_x, 2), swap(to_y, 4)

    def second(self, *done):
        half = self.half
        from_x, from_y = after((self.from_x, self.from_y), *done)
        self.near = (from_x[half:], from_y[half:])
        self.own = self.rest[2 * half :]
        return self.forward(self.rest[:half], self.rest[half : 2 * half], from_x[:half], from_y[:half])

    def forward(self, along_y, along_x, top, bottom):
        wide = lambda values: values.astype(jnp.float32)
        y_top = (wide(along_y) + wide(top)).astype(jnp.bfloat16)
        x_bottom = (wide(along_x) + wide(bottom)).astype(jnp.bfloat16)
        self.last = (swap(y_top, 4), swap(x_bottom, 2))
        return y_top, x_bottom

    def finish(self, *done):
        wide = lambda values: values.astype(jnp.float32)
        y_top, x_bottom = after(self.last, *done)
        x_top, y_bottom = self.near
        return jnp.concatenate(
            [
                wide(self.own[: self.half]) + wide(x_top) + wide(y_top),
                wide(self.own[self.half :]) + wide(x_bottom) + wide(y_bottom),
            ]
        )


def split_for_scatter(own, along_x, along_y, diagonal):
    half = own.shape[0] // 2
    return (
        jnp.concatenate([diagonal[:half], along_x[:half]]),
        jnp.concatenate([diagonal[half:], along_y[half:]]),
        jnp.concatenate([along_y[:half], along_x[half:], own]),
    )


class EarlyScatter(Scatter):
    def __init__(self, own, along_x, along_y):
        self.half = half = own.shape[0] // 2
        self.own, self.along_x, self.along_y = own, along_x, along_y
        self.near = (swap(along_x[:half], 2), swap(along_y[half:], 4))

    def first(self, diagonal):
        self.from_far = (swap(diagonal[: self.half], 2), swap(diagonal[self.half :], 4))
        self.near = after(self.near, diagonal)
        return self.near

    def second(self, *done):
        half = self.half
        far = after(self.from_far, *done)
        return self.forward(self.along_y[:half], self.along_x[half:], *far)


def tree_sum(values):
    total = values + swap(values, 1)
    total = (total + swap(total, 2)) + (swap(total, 4) + swap(total, 6))
    size = lax.axis_size("batch")
    terms = [total] + [
        lax.ppermute(total, "batch", [(z, z ^ bits) for z in range(size)])
        for bits in range(1, size)
    ]
    while len(terms) > 1:
        terms = [terms[k] + terms[k + 1] for k in range(0, len(terms), 2)]
    return terms[0]


def local_chips(
    hidden,
    cotangent,
    exit_layer,
    ln1_gain,
    ln1_bias,
    qkv_weight,
    query_bias,
    value_bias,
    out_weight,
    out_bias,
    ln2_gain,
    ln2_bias,
    up_weight,
    up_bias,
    down_weight,
    down_bias,
):
    width = lax.axis_size("wide")
    rank = lax.axis_index("wide")
    rows, model = hidden.shape
    group = rows * width
    slab = model // width
    head_size = model // HEADS
    units_own = up_weight.shape[0]
    keep = exit_layer >= LAYER
    counts = jnp.sum(keep.astype(jnp.int32), axis=1)
    active = lax.dynamic_slice_in_dim(keep.reshape(group), rank * rows, rows, 0)
    active = active.astype(jnp.float32)[:, None]
    grad_out = cotangent.astype(jnp.float32)

    tiles = jnp.arange(group // rows, dtype=jnp.int32)
    slots = ((tiles ^ rank) & 1) * 4 + ((tiles >> 1) ^ (rank >> 1))
    slots = slots.reshape(counts.shape[0], -1)

    routes = [[(w, (3 * w + t) % width) for w in range(width)] for t in range(3)]
    part_at = np.zeros((width, 3), np.int32)
    for t in range(3):
        for w, d in routes[t]:
            part_at[d, t] = (3 * w + t) // width
    part_at = jnp.asarray(part_at)
    other = rank ^ 1
    parts = jnp.stack([part_at[rank], part_at[other]])

    hidden_wide = hidden.astype(jnp.float32)
    normal1, inverse1 = normalize(hidden_wide)
    slabs = qkv_weight.reshape(3, slab, model)
    slabs = [lax.ppermute(slabs[t], "wide", routes[t]) for t in range(3)]
    normed1 = (normal1 * ln1_gain + ln1_bias).astype(jnp.bfloat16)
    normed1 = [normed1, swap(normed1, 2), swap(normed1, 4)]
    diagonal1 = relay(normed1[1], normed1[2])
    qkv_own = jnp.stack(after(slabs, normed1[1:]))
    qkv_other = swap(qkv_own, 1)

    def shift_of(device):
        own = lambda vector: lax.dynamic_slice_in_dim(vector, device * slab, slab, 0)
        shift = [own(query_bias), jnp.zeros((slab,), jnp.float32), own(value_bias)]
        return jnp.concatenate(shift)[None]

    bias_of = lambda device: lax.dynamic_slice_in_dim(up_bias, device * units_own, units_own, 0)
    up_shifts = [bias_of(rank)[None], bias_of(other)[None]]

    mixed_near = project(parts, 0, normed1, qkv_own, shift_of(rank))
    qkv_other = after(qkv_other, mixed_near, diagonal1)
    lent_near = project(parts, 1, normed1, qkv_other, shift_of(other))
    diagonal1 = after(diagonal1, lent_near)
    lent_far = project(parts, 1, diagonal1, qkv_other, shift_of(other))
    mixed_far = project(parts, 0, after(diagonal1, lent_far), qkv_own, shift_of(rank))
    mixed = [mixed_near, mixed_far, swap(lent_near, 1), swap(lent_far, 1)]

    out_whole = lax.all_gather(after(out_weight, diagonal1), "wide", axis=0, tiled=True)
    grad_ffn = (after(active, diagonal1) * grad_out).astype(jnp.bfloat16)
    down_bias_grad = jnp.sum(grad_ffn.astype(jnp.float32), axis=0)

    attended, logs = attend(mixed, slots, counts, head_size)
    attended_rows = lax.all_to_all(attended, "wide", split_axis=0, concat_axis=1, tiled=True)
    grad_ffn = after(grad_ffn, attended_rows)
    grad_ffn = [grad_ffn, swap(grad_ffn, 2), swap(grad_ffn, 4)]
    up_other, down_other = swap(after((up_weight, down_weight), attended), 1)
    middle = attend_out(attended_rows, out_whole, out_bias, hidden, active)
    normal2, inverse2 = normalize(middle)
    normed2 = (normal2 * ln2_gain + ln2_bias).astype(jnp.bfloat16)
    normed2 = [normed2, swap(normed2, 2), swap(normed2, 4)]

    per_tile = jnp.sum(keep.reshape(group // rows, rows).astype(jnp.int32), axis=1)
    block_chip = (rank >> 1) ^ jnp.arange(4, dtype=jnp.int32)
    block_counts = per_tile[2 * block_chip + (rank & 1)]
    ups, downs = [up_weight, up_other], [down_weight, down_other]

    def ffn(place, block, xs, gs, kept):
        *kept, partial = ffn_blocks(
            place, block, block_counts, xs, gs, ups, downs, up_shifts, tuple(kept)
        )
        return kept, partial

    kept, partial_own = ffn(2, 0, [after(normed2[0], grad_ffn[1:])], grad_ffn[:1], ())
    normed2[1:] = after(normed2[1:], partial_own)
    diagonal2 = relay(normed2[1], normed2[2])
    diagonal_ffn = relay(*after(grad_ffn[1:], attended_rows))
    kept, partial_near = ffn(0, 1, normed2[1:], grad_ffn[1:], kept)
    scatter2 = EarlyScatter(partial_own, partial_near[:rows], partial_near[rows:])
    diagonal2 = after(diagonal2, partial_near)
    (units, grad_pres), partial_far = ffn(3, 3, diagonal2, diagonal_ffn, kept)
    wait = scatter2.first(partial_far)
    tokens2 = [*normed2[1:], normed2[0], *diagonal2]
    tokens_ffn = [*grad_ffn[1:], grad_ffn[0], *diagonal_ffn]

    wide = lambda values: values.astype(jnp.float32)
    lowered = lambda values: values.astype(jnp.bfloat16)
    tile = 512
    tiles = jnp.arange(2 * units_own // tile, dtype=jnp.int32)

    down_own, down_lent = weight_grad(after(units, wait), tiles, tile, tokens_ffn, outputs=2)
    wait = scatter2.second(down_lent)
    down_lent = swap(down_lent, 1)
    up_own, up_lent = weight_grad(after(grad_pres, wait), tiles, tile, tokens2, outputs=2)

    up_lent = swap(up_lent, 1)
    down_sum = lowered(wide(down_own) + wide(after(down_lent, up_own)))
    up_sum = lowered(wide(up_own) + wide(up_lent))
    down_grad, up_grad = lax.psum((down_sum, up_sum), "batch")
    grad_middle, ln2_gain_grad, ln2_bias_grad = normalize_back(
        scatter2.finish(up_own), ln2_gain, normal2, inverse2
    )
    grad_middle = grad_out + grad_middle
    grad_branch = (active * grad_middle).astype(jnp.bfloat16)
    out_bias_grad = jnp.sum(grad_branch.astype(jnp.float32), axis=0)
    grad_branch = after(grad_branch, down_sum, up_sum)
    grad_attended = attend_out_back(grad_branch, out_whole)
    grad_heads = lax.all_to_all(grad_attended, "wide", split_axis=1, concat_axis=0, tiled=True)
    owners = 2 * block_chip + (rank & 1)
    grad_branch = after(grad_branch, grad_attended)
    out_lent = weight_grad(attended_rows, owners ^ 1, slab, [grad_branch])
    out_lent = swap(out_lent, 1)
    out_own = weight_grad(after(attended_rows, out_lent), owners, slab, [grad_branch], out_lent)

    back_own, back_other = attend_back(
        mixed, slots, after(grad_heads, out_own), attended, logs, counts, head_size
    )

    theirs = swap(back_other, 1)
    out_own = after(out_own, back_own)
    scatter_out = Scatter(*split_for_scatter(*jnp.split(out_own, 4)))
    order = jnp.array([3, 0, 1, 2], jnp.int32)
    ffn_counts = block_counts[jnp.array([1, 2, 0, 3])]
    ffn_parts = products(order, ffn_counts, after(units, scatter_out.sent), *downs)
    tokens1 = [*normed1, *diagonal1]
    theirs = after(theirs, ffn_parts[0])
    qkv_lent = weight_grad(theirs, parts[1], slab, tokens1)
    wait = scatter_out.second(qkv_lent)
    grad_parts = unproject(
        jnp.array([3, 1, 2, 0], jnp.int32),
        parts,
        block_counts,
        after(back_own, wait),
        theirs,
        qkv_own,
        qkv_other,
    )
    qkv_lent = swap(qkv_lent, 1)
    scatter1 = Scatter(*grad_parts)
    qkv_total = weight_grad(
        after(back_own, grad_parts[0]),
        parts[0],
        slab,
        tokens1,
        after(qkv_lent, grad_parts[0]),
        apart=True,
    )

    returned = [
        lax.ppermute(total, "wide", [(d, w) for w, d in route])
        for total, route in zip(qkv_total, routes)
    ]
    down_grad, up_grad = after((down_grad, up_grad), returned)
    out_total = lowered(scatter_out.finish(up_grad))
    *qkv_grad, out_grad = lax.psum(after((*returned, out_total), up_grad), "batch")
    wait = scatter1.second(out_total, up_grad)
    scatter_ffn = Scatter(*after(ffn_parts, wait))
    grad_normed1 = scatter1.finish(wait, scatter_ffn.sent)
    grad_hidden, ln1_gain_grad, ln1_bias_grad = normalize_back(
        grad_normed1, ln1_gain, normal1, inverse1
    )
    input_grad = grad_middle + grad_hidden
    grad_pres, back_own, back_other = after((grad_pres, back_own, back_other), wait)
    up_bias_own = jnp.sum(wide(grad_pres), axis=0).reshape(-1, 2, 256)
    up_bias_own = [up_bias_own[:, side].reshape(units_own) for side in range(2)]
    sums = jnp.sum(wide(back_own), axis=0) + jnp.sum(wide(back_other), axis=0)
    wait = scatter_ffn.second(input_grad)
    down_grad, up_grad = wide(after(down_grad, wait)), wide(after(up_grad, wait))
    ffn_out = scatter_ffn.finish(down_grad, up_grad)
    output = (middle + active * (ffn_out + down_bias)).astype(jnp.bfloat16)
    placed = lambda vector, size, device: lax.dynamic_update_slice_in_dim(
        jnp.zeros((size,), jnp.float32), vector, device * vector.shape[0], 0
    )
    smalls = tree_sum(
        jnp.concatenate(
            [
                placed(up_bias_own[0], up_bias.shape[0], rank)
                + placed(up_bias_own[1], up_bias.shape[0], other),
                down_bias_grad,
                out_bias_grad,
                ln2_gain_grad,
                ln2_bias_grad,
                placed(sums[:slab], model, rank),
                placed(sums[2 * slab :], model, rank),
                ln1_gain_grad,
                ln1_bias_grad,
            ]
        )
    )
    up_bias_grad = smalls[: up_bias.shape[0]]
    smalls = smalls[up_bias.shape[0] :].reshape(8, model)
    qkv_grad = wide(jnp.concatenate(qkv_grad))
    out_grad = wide(out_grad)
    return (
        output,
        input_grad,
        smalls[6],
        smalls[7],
        qkv_grad,
        smalls[4],
        smalls[5],
        out_grad,
        smalls[1],
        smalls[2],
        smalls[3],
        up_grad,
        up_bias_grad,
        down_grad,
        smalls[0],
    )


def solution(mesh):
    chips = mesh.shape["wide"] == 8 and mesh.shape["batch"] == 4
    local = local_chips if chips else local_general
    rows = P(("batch", "wide"), None)
    weight = P("wide", None)
    return jax.shard_map(
        local,
        mesh=mesh,
        in_specs=(
            rows,
            rows,
            P("batch", None),
            P(),
            P(),
            weight,
            P(),
            P(),
            weight,
            P(),
            P(),
            P(),
            weight,
            P(),
            weight,
            P(),
        ),
        out_specs=(
            rows,
            rows,
            P(),
            P(),
            weight,
            P(),
            P(),
            weight,
            P(),
            P(),
            P(),
            weight,
            P(),
            weight,
            P(),
        ),
        check_vma=False,
    )
```

profile of v0, /device:TPU:0, one launch (start us, length us, event | category | flops | bytes accessed | tf_op | source)
XLA Modules:
  0.0 1010.8 jit_solution(15104024190828771487)
XLA Ops:
  20.3 4.0 collective-permute-start.4
  24.4 49.5 %collective-permute-done.3 = bf16[256,2048]{1,0:T(8,128)(2,1)S(1)} collective-permute-done((bf16[256,2048]{1,0:T(8,128)(2,1)S(1)}, bf16[256,2048]{1,0:T(8,128)(2,1)S(1)}, u32[]{:S(2)}, u32[]{:S(2)}) %collective-permute-start.3) | collective-permute-done | bytes 1048608 | tf_op jit(solution)/shard_map/ppermute | solution.py:1012
  73.9 9.8 collective-permute-done.4
  96.4 10.2 %shard_map.307.refs_0_ = bf16[1536,768]{1,0:T(8,128)(2,1)} custom-call(s32[2,3]{1,0:T(2,128)S(1)} %pad_add_fusion.parts, bf16[512,2048]{1,0:T(8,128)(2,1)S(1)} %copy-done.8, bf16[512,2048]{1,0:T(8,128)(2,1)S(1)} %copy-done.11, bf16[512,2048]{1,0:T(8,128)(2,1)} %copy-done.29, bf16[3,256,2048]{2,1,0:T(8,128)(2,1)} %pad_maximum_fusion.2.refs_3_.refs_2_.own, ...), custom_call_target="tpu_custom_call" | custom-call | flops 4831838208 | bytes 11796480 | tf_op jit(solution)/shard_map/pallas_call | solution.py:564
  106.6 7.0 collective-permute-done.5.refs_0_.refs_4_
  115.5 10.2 %shard_map.308 = bf16[1536,768]{1,0:T(8,128)(2,1)} custom-call(s32[2,3]{1,0:T(2,128)S(1)} %pad_add_fusion.parts, bf16[512,2048]{1,0:T(8,128)(2,1)S(1)} %copy-done.8, bf16[512,2048]{1,0:T(8,128)(2,1)S(1)} %copy-done.11, bf16[512,2048]{1,0:T(8,128)(2,1)} %copy-done.29, bf16[3,256,2048]{2,1,0:T(8,128)(2,1)} %collective-permute-done.7.refs_3_.refs_2_.other, ...), custom_call_target="tpu_custom_call" | custom-call | flops 4831838208 | bytes 11796480 | tf_op jit(solution)/shard_map/pallas_call | solution.py:564
  125.8 5.3 shard_map.309
  131.8 6.0 shard_map.310.refs_1_
  137.8 39.9 %shard_map.311 = (bf16[4096,256]{1,0:T(8,128)(2,1)S(1)}, f32[2,4,2048]{2,1,0:T(4,128)S(1)}) custom-call(s32[2]{0:T(128)S(1)} %convert_reduce_fusion.6.counts, s32[2,4]{1,0:T(2,128)S(1)} %xor_add_fusion.slots, bf16[1536,768]{1,0:T(8,128)(2,1)S(1)} %copy-done.16, bf16[512,768]{1,0:T(8,128)(2,1)S(1)} %shard_map.310.refs_1_, ...), custom_call_target="tpu_custom_call" | custom-call | flops 4294967296 | bytes 8388608 | tf_op jit(solution)/shard_map/pallas_call | solution.py:157
  179.1 4.6 all-to-all-start
  187.8 22.5 %all-to-all-done = bf16[8,512,256]{2,1,0:T(8,128)(2,1)} async-done(((bf16[8,512,256]{2,1,0:T(8,128)(2,1)}), bf16[8,512,256]{2,1,0:T(8,128)(2,1)}, u32[]{:S(2)}, u32[]{:S(2)}) %all-to-all-start) | async-done | bytes 2097184 | tf_op jit(solution)/shard_map/all_to_all | solution.py:1040
  216.4 8.5 shard_map.312
  234.3 28.0 %collective-permute-done.12.refs_2_.refs_1_ = bf16[512,2048]{1,0:T(8,128)(2,1)} collective-permute-done((bf16[512,2048]{1,0:T(8,128)(2,1)}, bf16[512,2048]{1,0:T(8,128)(2,1)}, u32[]{:S(2)}, u32[]{:S(2)}) %collective-permute-start.12) | collective-permute-done | bytes 2097184 | tf_op jit(solution)/shard_map/ppermute | solution.py:881
  269.0 25.7 %shard_map.313 = (bf16[2048,2048]{1,0:T(8,128)(2,1)}, bf16[2048,2048]{1,0:T(8,128)(2,1)}, bf16[512,2048]{1,0:T(8,128)(2,1)S(1)}) custom-call(s32[4]{0:T(128)S(1)} %gather_fusion, bf16[512,2048]{1,0:T(8,128)(2,1)} %add_convert_fusion.2.refs_0_.refs_3_, bf16[512,2048]{1,0:T(8,128)(2,1)} %get-tuple-element.117.refs_1_.refs_3_, bf16[1024,2048]{1,0:T(8,128)(2,1)} %refs_4_.5, ...), custom_call_target="tpu_custom_call" | custom-call | flops 12884901888 | bytes 25165824 | tf_op jit(solution)/shard_map/pallas_call | solution.py:394
  294.8 12.5 %collective-permute-done.10.refs_0_.refs_1_ = bf16[512,2048]{1,0:T(8,128)(2,1)} collective-permute-done((bf16[512,2048]{1,0:T(8,128)(2,1)}, bf16[512,2048]{1,0:T(8,128)(2,1)}, u32[]{:S(2)}, u32[]{:S(2)}) %collective-permute-start.10) | collective-permute-done | bytes 2097184 | tf_op jit(solution)/shard_map/ppermute | solution.py:881
  317.0 29.9 %shard_map.314 = (bf16[2048,2048]{1,0:T(8,128)(2,1)}, bf16[2048,2048]{1,0:T(8,128)(2,1)}, bf16[1024,2048]{1,0:T(8,128)(2,1)}) custom-call(s32[4]{0:T(128)S(1)} %gather_fusion, bf16[512,2048]{1,0:T(8,128)(2,1)} %collective-permute-done.10.refs_0_.refs_1_, ...), custom_call_target="tpu_custom_call", output_to_operand_aliasing={{0}: (11, {}), {1}: (12, {})} | custom-call | flops 25769803776 | bytes 33554432 | tf_op jit(solution)/shard_map/pallas_call | solution.py:394
  348.6 18.8 %collective-permute-start.20 = (bf16[256,2048]{1,0:T(8,128)(2,1)S(1)}, bf16[256,2048]{1,0:T(8,128)(2,1)S(1)}, u32[]{:S(2)}, u32[]{:S(2)}) collective-permute-start(bf16[256,2048]{1,0:T(8,128)(2,1)S(1)} %get-tuple-element.245), channel_id=1, source_target_pairs={{0,2},{1,3},{2,0},{3,1},{4,6},{5,7},{6,4},{7,5},{8,10},{9,11},{10,... | collective-permute-start | bytes 3145736 | tf_op jit(solution)/shard_map/ppermute | solution.py:881
  367.5 23.2 %shard_map.315 = (bf16[2048,2048]{1,0:T(8,128)(2,1)}, bf16[2048,2048]{1,0:T(8,128)(2,1)}, bf16[512,2048]{1,0:T(8,128)(2,1)}) custom-call(s32[4]{0:T(128)S(1)} %gather_fusion, bf16[256,2048]{1,0:T(8,128)(2,1)S(1)} %collective-permute-done.16.refs_0_.refs_4_, ...), custom_call_target="tpu_custom_call", output_to_operand_aliasing={{0}: (11, {}), {1}: (12, {})} | custom-call | flops 12884901888 | bytes 25165824 | tf_op jit(solution)/shard_map/pallas_call | solution.py:394
  397.3 25.0 %shard_map.316 = (bf16[1024,2048]{1,0:T(8,128)(2,1)}, bf16[1024,2048]{1,0:T(8,128)(2,1)}) custom-call(s32[4]{0:T(128)S(1)} %iota.43.columns, bf16[2048,2048]{1,0:T(8,128)(2,1)} %get-tuple-element.156.refs_0_.left, bf16[512,2048]{1,0:T(8,128)(2,1)} %collective-permute-done.12.refs_2_.refs_1_, bf16[512,2048]{1,0:T(8,128)(2,1)} %collective-permute-done.13.refs_3_.refs_2_, ...), custom_call_target="tpu_custom_call" | custom-call | flops 1 | bytes 1 | tf_op jit(solution)/shard_map/pallas_call | solution.py:659
  425.7 25.1 %shard_map.317 = (bf16[1024,2048]{1,0:T(8,128)(2,1)}, bf16[1024,2048]{1,0:T(8,128)(2,1)}) custom-call(s32[4]{0:T(128)S(1)} %iota.44.columns, bf16[2048,2048]{1,0:T(8,128)(2,1)} %get-tuple-element.190.refs_0_, bf16[512,2048]{1,0:T(8,128)(2,1)} %collective-permute-done.10.refs_0_.refs_1_, bf16[512,2048]{1,0:T(8,128)(2,1)} %collective-permute-done.11.refs_1_.refs_2_, ...), custom_call_target="tpu_custom_call" | custom-call | flops 1 | bytes 1 | tf_op jit(solution)/shard_map/pallas_call | solution.py:659
  453.3 23.3 %collective-permute-done.24 = bf16[256,2048]{1,0:T(8,128)(2,1)S(1)} collective-permute-done((bf16[256,2048]{1,0:T(8,128)(2,1)S(1)}, bf16[256,2048]{1,0:T(8,128)(2,1)S(1)}, u32[]{:S(2)}, u32[]{:S(2)}) %collective-permute-start.24) | collective-permute-done | bytes 1048608 | tf_op jit(solution)/shard_map/ppermute | solution.py:881
  482.3 4.1 convert_reduce_fusion.4
  486.4 6.2 add_convert_fusion.1
  492.6 6.1 add_convert_fusion
  500.3 7.3 shard_map.318
  507.7 5.1 shard_map.319
  514.3 4.3 all-to-all-start.1
  523.5 7.5 shard_map.320
  531.1 14.2 %all-to-all-done.1 = bf16[512,8,256]{2,0,1:T(8,128)(2,1)} async-done(((bf16[512,8,256]{2,0,1:T(8,128)(2,1)}), bf16[512,8,256]{2,0,1:T(8,128)(2,1)}, u32[]{:S(2)}, u32[]{:S(2)}) %all-to-all-start.1) | async-done | bytes 2097184 | tf_op jit(solution)/shard_map/all_to_all | solution.py:1094
  549.2 53.7 %shard_map.321 = (bf16[2048,768]{1,0:T(8,128)(2,1)}, bf16[2048,768]{1,0:T(8,128)(2,1)}) custom-call(s32[2]{0:T(128)S(1)} %convert_reduce_fusion.6.counts, s32[2,4]{1,0:T(2,128)S(1)} %xor_add_fusion.slots, bf16[1536,768]{1,0:T(8,128)(2,1)} %shard_map.307.refs_0_, bf16[512,768]{1,0:T(8,128)(2,1)S(1)} %copy-done.15, ...), custom_call_target="tpu_custom_call" | custom-call | flops 1 | bytes 1 | tf_op jit(solution)/shard_map/pallas_call | solution.py:301
  605.5 22.7 %shard_map.322 = (bf16[512,2048]{1,0:T(8,128)(2,1)S(1)}, bf16[512,2048]{1,0:T(8,128)(2,1)S(1)}, bf16[1024,2048]{1,0:T(8,128)(2,1)}) custom-call(s32[4]{0:T(128)S(1)} %copy-done.20, s32[4]{0:T(128)S(1)} %gather_fusion.1, bf16[2048,2048]{1,0:T(8,128)(2,1)} %get-tuple-element.156.refs_0_.left, bf16[1024,2048]{1,0:T(8,128)(2,1)} %own.1, ...), custom_call_target="tpu_custom_call" | custom-call | flops 1 | bytes 1 | tf_op jit(solution)/shard_map/pallas_call | solution.py:476
  629.6 12.8 %shard_map.323 = bf16[768,2048]{1,0:T(8,128)(2,1)} custom-call(s32[3]{0:T(128)S(1)} %get-tuple-element.270.columns, bf16[2048,768]{1,0:T(8,128)(2,1)} %collective-permute-done.31.refs_0_.theirs, bf16[512,2048]{1,0:T(8,128)(2,1)S(1)} %copy-done.9, bf16[512,2048]{1,0:T(8,128)(2,1)} %copy-done.10, bf16[512,2048]{1,0:T(8,128)(2,1)} %copy-done.29, ...), custom_call_target="tpu_custom_call" | custom-call | flops 1 | bytes 1 | tf_op jit(solution)/shard_map/pallas_call | solution.py:659
  644.2 23.8 %collective-permute-done.30 = bf16[256,2048]{1,0:T(8,128)(2,1)S(1)} collective-permute-done((bf16[256,2048]{1,0:T(8,128)(2,1)S(1)}, bf16[256,2048]{1,0:T(8,128)(2,1)S(1)}, u32[]{:S(2)}, u32[]{:S(2)}) %collective-permute-start.30) | collective-permute-done | bytes 1048608 | tf_op jit(solution)/shard_map/ppermute | solution.py:881
  671.4 20.6 %shard_map.324 = (bf16[512,2048]{1,0:T(8,128)(2,1)}, bf16[512,2048]{1,0:T(8,128)(2,1)}, bf16[1024,2048]{1,0:T(8,128)(2,1)}) custom-call(s32[4]{0:T(128)S(1)} %copy-done.21, s32[2,3]{1,0:T(2,128)S(1)} %pad_add_fusion.parts, s32[4]{0:T(128)S(1)} %gather_fusion, bf16[2048,768]{1,0:T(8,128)(2,1)} %get-tuple-element.191.mine.refs_0_, ...), custom_call_target="tpu_custom_call" | custom-call | flops 1 | bytes 1 | tf_op jit(solution)/shard_map/pallas_call | solution.py:612
  693.8 13.8 %shard_map.325 = (bf16[256,2048]{1,0:T(8,128)(2,1)S(1)}, bf16[256,2048]{1,0:T(8,128)(2,1)S(1)}, bf16[256,2048]{1,0:T(8,128)(2,1)}) custom-call(s32[3]{0:T(128)S(1)} %get-tuple-element.269.columns, bf16[2048,768]{1,0:T(8,128)(2,1)} %get-tuple-element.191.mine.refs_0_, bf16[512,2048]{1,0:T(8,128)(2,1)} %copy-done.7, bf16[512,2048]{1,0:T(8,128)(2,1)} %copy-done.10, ...), custom_call_target="tpu_custom_call" | custom-call | flops 1 | bytes 1 | tf_op jit(solution)/shard_map/pallas_call | solution.py:659
  715.5 15.1 %collective-permute-done.38 = bf16[256,2048]{1,0:T(8,128)(2,1)S(1)} collective-permute-done((bf16[256,2048]{1,0:T(8,128)(2,1)S(1)}, bf16[256,2048]{1,0:T(8,128)(2,1)S(1)}, u32[]{:S(2)}, u32[]{:S(2)}) %collective-permute-start.38) | collective-permute-done | bytes 1048608 | tf_op jit(solution)/shard_map/ppermute | solution.py:1136
  731.6 6.0 collective-permute-start.35
  737.7 77.3 %all-reduce.7.cloned.1.call-done = (bf16[1024,2048]{1,0:T(8,128)(2,1)}, bf16[1024,2048]{1,0:T(8,128)(2,1)}) async-done(((bf16[1024,2048]{1,0:T(8,128)(2,1)}, bf16[1024,2048]{1,0:T(8,128)(2,1)}), (bf16[1024,2048]{1,0:T(8,128)(2,1)}, bf16[1024,2048]{1,0:T(8,128)(2,1)})) %all-reduce.7.cloned.1.call-update) | async-done | bytes 8388624 | tf_op jit(solution)/shard_map/psum | solution.py:1085
  818.5 4.5 add_convert_fusion.5
  827.1 4.7 convert_reduce_fusion
  833.9 15.4 %collective-permute-done.42 = bf16[256,2048]{1,0:T(8,128)(2,1)S(1)} collective-permute-done((bf16[256,2048]{1,0:T(8,128)(2,1)}, bf16[256,2048]{1,0:T(8,128)(2,1)S(1)}, u32[]{:S(2)}, u32[]{:S(2)}) %collective-permute-start.42) | collective-permute-done | bytes 1048608 | tf_op jit(solution)/shard_map/ppermute | solution.py:881
  864.1 31.8 %collective-permute-done.40 = bf16[512,2048]{1,0:T(8,128)(2,1)} collective-permute-done((bf16[512,2048]{1,0:T(8,128)(2,1)}, bf16[512,2048]{1,0:T(8,128)(2,1)}, u32[]{:S(2)}, u32[]{:S(2)}) %collective-permute-start.40) | collective-permute-done | bytes 2097184 | tf_op jit(solution)/shard_map/ppermute | solution.py:881
  904.8 5.2 collective-permute-done.50
  910.0 6.0 collective-permute-done.51
  917.4 4.4 convert_element_type.284
  921.9 4.6 convert_element_type.283
  931.2 64.7 %all-reduce.5.cloned.1.call-done = (bf16[256,2048]{1,0:T(8,128)(2,1)}, bf16[256,2048]{1,0:T(8,128)(2,1)}, bf16[256,2048]{1,0:T(8,128)(2,1)}, bf16[256,2048]{1,0:T(8,128)(2,1)}) async-done(((bf16[256,2048]{1,0:T(8,128)(2,1)}, bf16[256,2048]{1,0:T(8,128)(2,1)}, bf16[256,2048]{1,0:T(8,128)(2,1)}, bf16[256,2048]{1,0:T(8,128)(2,1)}), (bf16[256,2048]{1,0:T(8,128)(2,1)}, bf16[256,2048]{1,0:T(8,128)(2,1)}, ...) | async-done | bytes 4194320 | tf_op jit(solution)/shard_map/psum | solution.py:1141
  998.6 5.4 maximum_convert_fusion
  (313 shorter events, 159.2 us)
Async XLA Ops:
  7.2 207.6 %all-gather.2.cloned.1.call-start = ((), (), s32[]{:S(2)}) async-start(), calls=%async_computation.2 | async-start | bytes 9437184 | tf_op jit(solution)/shard_map/all_gather | solution.py:1035
  12.6 71.1 %collective-permute-start = (bf16[512,2048]{1,0:T(8,128)(2,1)S(1)}, bf16[512,2048]{1,0:T(8,128)(2,1)S(1)}, u32[]{:S(2)}, u32[]{:S(2)}) collective-permute-start(bf16[512,2048]{1,0:T(8,128)(2,1)S(1)} %fusion.7.refs_0_.refs_1_), channel_id=1, source_target_pairs={{0,2},{1,3},{2,0},{3,1},{4,6},{5,7},{6,4},{7,5},{8,10},{9,11},{10,... | collective-permute-start | bytes 6291464 | tf_op jit(solution)/shard_map/ppermute | solution.py:881
  15.6 68.1 %collective-permute-start.1 = (bf16[512,2048]{1,0:T(8,128)(2,1)S(1)}, bf16[512,2048]{1,0:T(8,128)(2,1)S(1)}, u32[]{:S(2)}, u32[]{:S(2)}) collective-permute-start(bf16[512,2048]{1,0:T(8,128)(2,1)S(1)} %fusion.7.refs_0_.refs_1_), channel_id=1, source_target_pairs={{0,4},{1,5},{2,6},{3,7},{4,0},{5,1},{6,2},{7,3},{8,12},{9,13},{10,... | collective-permute-start | bytes 6291464 | tf_op jit(solution)/shard_map/ppermute | solution.py:881
  19.6 54.3 %collective-permute-start.3 = (bf16[256,2048]{1,0:T(8,128)(2,1)S(1)}, bf16[256,2048]{1,0:T(8,128)(2,1)S(1)}, u32[]{:S(2)}, u32[]{:S(2)}) collective-permute-start(bf16[256,2048]{1,0:T(8,128)(2,1)S(1)} %get-tuple-element.248), channel_id=1, source_target_pairs={{0,1},{1,4},{2,7},{3,2},{4,5},{5,0},{6,3},{7,6},{8,9},{9,12},{10,1... | collective-permute-start | bytes 3145736 | tf_op jit(solution)/shard_map/ppermute | solution.py:1012
  20.3 63.3 %collective-permute-start.4 = (bf16[256,2048]{1,0:T(8,128)(2,1)S(1)}, bf16[256,2048]{1,0:T(8,128)(2,1)S(1)}, u32[]{:S(2)}, u32[]{:S(2)}) collective-permute-start(bf16[256,2048]{1,0:T(8,128)(2,1)S(1)} %get-tuple-element.246), channel_id=1, source_target_pairs={{0,2},{1,5},{2,0},{3,3},{4,6},{5,1},{6,4},{7,7},{8,10},{9,13},{10,... | collective-permute-start | bytes 3145736 | tf_op jit(solution)/shard_map/ppermute | solution.py:1012
  85.9 29.5 %collective-permute-start.7 = (bf16[3,256,2048]{2,1,0:T(8,128)(2,1)}, bf16[3,256,2048]{2,1,0:T(8,128)(2,1)}, u32[]{:S(2)}, u32[]{:S(2)}) collective-permute-start(bf16[3,256,2048]{2,1,0:T(8,128)(2,1)} %pad_maximum_fusion.2.refs_3_.refs_2_.own), channel_id=1, source_target_pairs={{0,1},{1,0},{2,3},{3,2},{4,5},{5,4},{6,7},{7,6},{8,9},{9,8},{10,11... | collective-permute-start | bytes 9437192 | tf_op jit(solution)/shard_map/ppermute | solution.py:881
  88.3 25.3 %collective-permute-start.5 = (bf16[256,2048]{1,0:T(8,128)(2,1)}, bf16[256,2048]{1,0:T(8,128)(2,1)S(1)}, u32[]{:S(2)}, u32[]{:S(2)}) collective-permute-start(bf16[256,2048]{1,0:T(8,128)(2,1)} %slice.276), channel_id=1, source_target_pairs={{0,2},{1,3},{2,0},{3,1},{4,6},{5,7},{6,4},{7,5},{8,10},{9,11},{10,... | collective-permute-start | bytes 3145736 | tf_op jit(solution)/shard_map/ppermute | solution.py:881
  90.0 25.5 %collective-permute-start.6 = (bf16[256,2048]{1,0:T(8,128)(2,1)}, bf16[256,2048]{1,0:T(8,128)(2,1)}, u32[]{:S(2)}, u32[]{:S(2)}) collective-permute-start(bf16[256,2048]{1,0:T(8,128)(2,1)} %slice.277), channel_id=1, source_target_pairs={{0,4},{1,5},{2,6},{3,7},{4,0},{5,1},{6,2},{7,3},{8,12},{9,13},{10,... | collective-permute-start | bytes 3145736 | tf_op jit(solution)/shard_map/ppermute | solution.py:881
  179.1 31.2 %all-to-all-start = ((bf16[8,512,256]{2,1,0:T(8,128)(2,1)}), bf16[8,512,256]{2,1,0:T(8,128)(2,1)}, u32[]{:S(2)}, u32[]{:S(2)}) async-start(bf16[8,512,256]{2,1,0:T(8,128)(2,1)} %bitcast.30), calls=%async_computation | async-start | bytes 4194304 | tf_op jit(solution)/shard_map/all_to_all | solution.py:1040
  183.6 84.0 %collective-permute-start.14 = (bf16[1024,2048]{1,0:T(8,128)(2,1)}, bf16[1024,2048]{1,0:T(8,128)(2,1)}, u32[]{:S(2)}, u32[]{:S(2)}) collective-permute-start(bf16[1024,2048]{1,0:T(8,128)(2,1)} %refs_4_.5), channel_id=1, source_target_pairs={{0,1},{1,0},{2,3},{3,2},{4,5},{5,4},{6,7},{7,6},{8,9},{9,8},{10,11... | collective-permute-start | bytes 12582920 | tf_op jit(solution)/shard_map/ppermute | solution.py:881
  184.1 84.9 %collective-permute-start.15 = (bf16[1024,2048]{1,0:T(8,128)(2,1)}, bf16[1024,2048]{1,0:T(8,128)(2,1)}, u32[]{:S(2)}, u32[]{:S(2)}) collective-permute-start(bf16[1024,2048]{1,0:T(8,128)(2,1)} %own.1), channel_id=1, source_target_pairs={{0,1},{1,0},{2,3},{3,2},{4,5},{5,4},{6,7},{7,6},{8,9},{9,8},{10,11... | collective-permute-start | bytes 12582920 | tf_op jit(solution)/shard_map/ppermute | solution.py:881
  213.5 48.9 %collective-permute-start.12 = (bf16[512,2048]{1,0:T(8,128)(2,1)}, bf16[512,2048]{1,0:T(8,128)(2,1)}, u32[]{:S(2)}, u32[]{:S(2)}) collective-permute-start(bf16[512,2048]{1,0:T(8,128)(2,1)} %get-tuple-element.117.refs_1_.refs_3_), channel_id=1, source_target_pairs={{0,2},{1,3},{2,0},{3,1},{4,6},{5,7},{6,4},{7,5},{8,10},{9,11},{10,... | collective-permute-start | bytes 6291464 | tf_op jit(solution)/shard_map/ppermute | solution.py:881
  214.1 50.3 %collective-permute-start.13 = (bf16[512,2048]{1,0:T(8,128)(2,1)}, bf16[512,2048]{1,0:T(8,128)(2,1)}, u32[]{:S(2)}, u32[]{:S(2)}) collective-permute-start(bf16[512,2048]{1,0:T(8,128)(2,1)} %get-tuple-element.117.refs_1_.refs_3_), channel_id=1, source_target_pairs={{0,4},{1,5},{2,6},{3,7},{4,0},{5,1},{6,2},{7,3},{8,12},{9,13},{10,... | collective-permute-start | bytes 6291464 | tf_op jit(solution)/shard_map/ppermute | solution.py:881
  232.9 74.4 %collective-permute-start.10 = (bf16[512,2048]{1,0:T(8,128)(2,1)}, bf16[512,2048]{1,0:T(8,128)(2,1)}, u32[]{:S(2)}, u32[]{:S(2)}) collective-permute-start(bf16[512,2048]{1,0:T(8,128)(2,1)} %add_convert_fusion.2.refs_0_.refs_3_), channel_id=1, source_target_pairs={{0,2},{1,3},{2,0},{3,1},{4,6},{5,7},{6,4},{7,5},{8,10},{9,11},{10,... | collective-permute-start | bytes 6291464 | tf_op jit(solution)/shard_map/ppermute | solution.py:881
  262.3 48.9 %collective-permute-start.11 = (bf16[512,2048]{1,0:T(8,128)(2,1)}, bf16[512,2048]{1,0:T(8,128)(2,1)}, u32[]{:S(2)}, u32[]{:S(2)}) collective-permute-start(bf16[512,2048]{1,0:T(8,128)(2,1)} %add_convert_fusion.2.refs_0_.refs_3_), channel_id=1, source_target_pairs={{0,4},{1,5},{2,6},{3,7},{4,0},{5,1},{6,2},{7,3},{8,12},{9,13},{10,... | collective-permute-start | bytes 6291464 | tf_op jit(solution)/shard_map/ppermute | solution.py:881
  265.7 101.7 %collective-permute-start.18 = (bf16[256,2048]{1,0:T(8,128)(2,1)S(1)}, bf16[256,2048]{1,0:T(8,128)(2,1)S(1)}, u32[]{:S(2)}, u32[]{:S(2)}) collective-permute-start(bf16[256,2048]{1,0:T(8,128)(2,1)S(1)} %slice.221), channel_id=1, source_target_pairs={{0,2},{1,3},{2,0},{3,1},{4,6},{5,7},{6,4},{7,5},{8,10},{9,11},{10,... | collective-permute-start | bytes 3145736 | tf_op jit(solution)/shard_map/ppermute | solution.py:881
  267.6 99.8 %collective-permute-start.19 = (bf16[256,2048]{1,0:T(8,128)(2,1)S(1)}, bf16[256,2048]{1,0:T(8,128)(2,1)S(1)}, u32[]{:S(2)}, u32[]{:S(2)}) collective-permute-start(bf16[256,2048]{1,0:T(8,128)(2,1)S(1)} %slice.222), channel_id=1, source_target_pairs={{0,4},{1,5},{2,6},{3,7},{4,0},{5,1},{6,2},{7,3},{8,12},{9,13},{10,... | collective-permute-start | bytes 3145736 | tf_op jit(solution)/shard_map/ppermute | solution.py:881
  313.5 53.9 %collective-permute-start.16 = (bf16[256,2048]{1,0:T(8,128)(2,1)}, bf16[256,2048]{1,0:T(8,128)(2,1)S(1)}, u32[]{:S(2)}, u32[]{:S(2)}) collective-permute-start(bf16[256,2048]{1,0:T(8,128)(2,1)} %slice.219), channel_id=1, source_target_pairs={{0,2},{1,3},{2,0},{3,1},{4,6},{5,7},{6,4},{7,5},{8,10},{9,11},{10,... | collective-permute-start | bytes 3145736 | tf_op jit(solution)/shard_map/ppermute | solution.py:881
  316.3 51.1 %collective-permute-start.17 = (bf16[256,2048]{1,0:T(8,128)(2,1)}, bf16[256,2048]{1,0:T(8,128)(2,1)S(1)}, u32[]{:S(2)}, u32[]{:S(2)}) collective-permute-start(bf16[256,2048]{1,0:T(8,128)(2,1)} %slice.220), channel_id=1, source_target_pairs={{0,4},{1,5},{2,6},{3,7},{4,0},{5,1},{6,2},{7,3},{8,12},{9,13},{10,... | collective-permute-start | bytes 3145736 | tf_op jit(solution)/shard_map/ppermute | solution.py:881
  348.6 47.3 %collective-permute-start.20 = (bf16[256,2048]{1,0:T(8,128)(2,1)S(1)}, bf16[256,2048]{1,0:T(8,128)(2,1)S(1)}, u32[]{:S(2)}, u32[]{:S(2)}) collective-permute-start(bf16[256,2048]{1,0:T(8,128)(2,1)S(1)} %get-tuple-element.245), channel_id=1, source_target_pairs={{0,2},{1,3},{2,0},{3,1},{4,6},{5,7},{6,4},{7,5},{8,10},{9,11},{10,... | collective-permute-start | bytes 3145736 | tf_op jit(solution)/shard_map/ppermute | solution.py:881
  367.4 28.5 %collective-permute-start.21 = (bf16[256,2048]{1,0:T(8,128)(2,1)S(1)}, bf16[256,2048]{1,0:T(8,128)(2,1)S(1)}, u32[]{:S(2)}, u32[]{:S(2)}) collective-permute-start(bf16[256,2048]{1,0:T(8,128)(2,1)S(1)} %get-tuple-element.244), channel_id=1, source_target_pairs={{0,4},{1,5},{2,6},{3,7},{4,0},{5,1},{6,2},{7,3},{8,12},{9,13},{10,... | collective-permute-start | bytes 3145736 | tf_op jit(solution)/shard_map/ppermute | solution.py:881
  393.8 28.5 %collective-permute-start.22 = (bf16[256,2048]{1,0:T(8,128)(2,1)}, bf16[256,2048]{1,0:T(8,128)(2,1)}, u32[]{:S(2)}, u32[]{:S(2)}) collective-permute-start(bf16[256,2048]{1,0:T(8,128)(2,1)} %get-tuple-element.252), channel_id=1, source_target_pairs={{0,2},{1,3},{2,0},{3,1},{4,6},{5,7},{6,4},{7,5},{8,10},{9,11},{10,... | collective-permute-start | bytes 3145736 | tf_op jit(solution)/shard_map/ppermute | solution.py:881
  395.7 26.7 %collective-permute-start.23 = (bf16[256,2048]{1,0:T(8,128)(2,1)}, bf16[256,2048]{1,0:T(8,128)(2,1)}, u32[]{:S(2)}, u32[]{:S(2)}) collective-permute-start(bf16[256,2048]{1,0:T(8,128)(2,1)} %get-tuple-element.251), channel_id=1, source_target_pairs={{0,4},{1,5},{2,6},{3,7},{4,0},{5,1},{6,2},{7,3},{8,12},{9,13},{10,... | collective-permute-start | bytes 3145736 | tf_op jit(solution)/shard_map/ppermute | solution.py:881
  422.3 64.1 %collective-permute-start.26 = (bf16[1024,2048]{1,0:T(8,128)(2,1)}, bf16[1024,2048]{1,0:T(8,128)(2,1)}, u32[]{:S(2)}, u32[]{:S(2)}) collective-permute-start(bf16[1024,2048]{1,0:T(8,128)(2,1)} %get-tuple-element.138), channel_id=1, source_target_pairs={{0,1},{1,0},{2,3},{3,2},{4,5},{5,4},{6,7},{7,6},{8,9},{9,8},{10,11... | collective-permute-start | bytes 12582920 | tf_op jit(solution)/shard_map/ppermute | solution.py:881
  450.8 41.9 %collective-permute-start.27 = (bf16[1024,2048]{1,0:T(8,128)(2,1)}, bf16[1024,2048]{1,0:T(8,128)(2,1)}, u32[]{:S(2)}, u32[]{:S(2)}) collective-permute-start(bf16[1024,2048]{1,0:T(8,128)(2,1)} %get-tuple-element.148), channel_id=1, source_target_pairs={{0,1},{1,0},{2,3},{3,2},{4,5},{5,4},{6,7},{7,6},{8,9},{9,8},{10,11... | collective-permute-start | bytes 12582920 | tf_op jit(solution)/shard_map/ppermute | solution.py:881
  451.3 25.2 %collective-permute-start.24 = (bf16[256,2048]{1,0:T(8,128)(2,1)S(1)}, bf16[256,2048]{1,0:T(8,128)(2,1)S(1)}, u32[]{:S(2)}, u32[]{:S(2)}) collective-permute-start(bf16[256,2048]{1,0:T(8,128)(2,1)S(1)} %copy-done.46), channel_id=1, source_target_pairs={{0,4},{1,5},{2,6},{3,7},{4,0},{5,1},{6,2},{7,3},{8,12},{9,13},{10,... | collective-permute-start | bytes 3145736 | tf_op jit(solution)/shard_map/ppermute | solution.py:881
  453.1 24.9 %collective-permute-start.25 = (bf16[256,2048]{1,0:T(8,128)(2,1)S(1)}, bf16[256,2048]{1,0:T(8,128)(2,1)S(1)}, u32[]{:S(2)}, u32[]{:S(2)}) collective-permute-start(bf16[256,2048]{1,0:T(8,128)(2,1)S(1)} %get-tuple-element.242), channel_id=1, source_target_pairs={{0,2},{1,3},{2,0},{3,1},{4,6},{5,7},{6,4},{7,5},{8,10},{9,11},{10,... | collective-permute-start | bytes 3145736 | tf_op jit(solution)/shard_map/ppermute | solution.py:881
  514.3 31.0 %all-to-all-start.1 = ((bf16[512,8,256]{2,0,1:T(8,128)(2,1)}), bf16[512,8,256]{2,0,1:T(8,128)(2,1)}, u32[]{:S(2)}, u32[]{:S(2)}) async-start(bf16[512,8,256]{2,0,1:T(8,128)(2,1)} %bitcast.39), calls=%async_computation.1 | async-start | bytes 4194304 | tf_op jit(solution)/shard_map/all_to_all | solution.py:1094
  518.7 296.3 %all-reduce.7.cloned.1.call-start = ((), (), s32[]{:S(2)}) async-start(), calls=%async_computation.4 | async-start | bytes 16777216 | tf_op jit(solution)/shard_map/psum | solution.py:1085
  519.4 476.4 %all-reduce.5.cloned.1.call-start = ((), (), s32[]{:S(2)}) async-start(), calls=%async_computation.3 | async-start | bytes 8388608 | tf_op jit(solution)/shard_map/psum | solution.py:1141
  602.9 26.7 %collective-permute-start.31 = (bf16[2048,768]{1,0:T(8,128)(2,1)}, bf16[2048,768]{1,0:T(8,128)(2,1)}, u32[]{:S(2)}, u32[]{:S(2)}) collective-permute-start(bf16[2048,768]{1,0:T(8,128)(2,1)} %get-tuple-element.192), channel_id=1, source_target_pairs={{0,1},{1,0},{2,3},{3,2},{4,5},{5,4},{6,7},{7,6},{8,9},{9,8},{10,11... | collective-permute-start | bytes 9437192 | tf_op jit(solution)/shard_map/ppermute | solution.py:881
  642.4 49.7 %collective-permute-start.36 = (bf16[768,2048]{1,0:T(8,128)(2,1)}, bf16[768,2048]{1,0:T(8,128)(2,1)S(1)}, u32[]{:S(2)}, u32[]{:S(2)}) collective-permute-start(bf16[768,2048]{1,0:T(8,128)(2,1)} %shard_map.323), channel_id=1, source_target_pairs={{0,1},{1,0},{2,3},{3,2},{4,5},{5,4},{6,7},{7,6},{8,9},{9,8},{10,11... | collective-permute-start | bytes 9437192 | tf_op jit(solution)/shard_map/ppermute | solution.py:881
  642.9 25.1 %collective-permute-start.30 = (bf16[256,2048]{1,0:T(8,128)(2,1)S(1)}, bf16[256,2048]{1,0:T(8,128)(2,1)S(1)}, u32[]{:S(2)}, u32[]{:S(2)}) collective-permute-start(bf16[256,2048]{1,0:T(8,128)(2,1)S(1)} %pad_maximum_fusion.4), channel_id=1, source_target_pairs={{0,4},{1,5},{2,6},{3,7},{4,0},{5,1},{6,2},{7,3},{8,12},{9,13},{10,... | collective-permute-start | bytes 3145736 | tf_op jit(solution)/shard_map/ppermute | solution.py:881
  642.9 25.2 %collective-permute-start.29 = (bf16[256,2048]{1,0:T(8,128)(2,1)S(1)}, bf16[256,2048]{1,0:T(8,128)(2,1)S(1)}, u32[]{:S(2)}, u32[]{:S(2)}) collective-permute-start(bf16[256,2048]{1,0:T(8,128)(2,1)S(1)} %pad_maximum_fusion.3), channel_id=1, source_target_pairs={{0,2},{1,3},{2,0},{3,1},{4,6},{5,7},{6,4},{7,5},{8,10},{9,11},{10,... | collective-permute-start | bytes 3145736 | tf_op jit(solution)/shard_map/ppermute | solution.py:881
  709.5 109.0 %collective-permute-start.32 = (bf16[512,2048]{1,0:T(8,128)(2,1)}, bf16[512,2048]{1,0:T(8,128)(2,1)}, u32[]{:S(2)}, u32[]{:S(2)}) collective-permute-start(bf16[512,2048]{1,0:T(8,128)(2,1)} %get-tuple-element.166), channel_id=1, source_target_pairs={{0,2},{1,3},{2,0},{3,1},{4,6},{5,7},{6,4},{7,5},{8,10},{9,11},{10,... | collective-permute-start | bytes 6291464 | tf_op jit(solution)/shard_map/ppermute | solution.py:881
  710.8 107.7 %collective-permute-start.33 = (bf16[512,2048]{1,0:T(8,128)(2,1)}, bf16[512,2048]{1,0:T(8,128)(2,1)}, u32[]{:S(2)}, u32[]{:S(2)}) collective-permute-start(bf16[512,2048]{1,0:T(8,128)(2,1)} %get-tuple-element.167), channel_id=1, source_target_pairs={{0,4},{1,5},{2,6},{3,7},{4,0},{5,1},{6,2},{7,3},{8,12},{9,13},{10,... | collective-permute-start | bytes 6291464 | tf_op jit(solution)/shard_map/ppermute | solution.py:881
  710.8 104.1 %collective-permute-start.39 = (bf16[256,2048]{1,0:T(8,128)(2,1)}, bf16[256,2048]{1,0:T(8,128)(2,1)}, u32[]{:S(2)}, u32[]{:S(2)}) collective-permute-start(bf16[256,2048]{1,0:T(8,128)(2,1)} %get-tuple-element.172), channel_id=1, source_target_pairs={{2,0},{5,1},{0,2},{3,3},{6,4},{1,5},{4,6},{7,7},{10,8},{13,9},{8,1... | collective-permute-start | bytes 3145736 | tf_op jit(solution)/shard_map/ppermute | solution.py:1136
  714.3 100.6 %collective-permute-start.34 = (bf16[128,2048]{1,0:T(8,128)(2,1)}, bf16[128,2048]{1,0:T(8,128)(2,1)}, u32[]{:S(2)}, u32[]{:S(2)}) collective-permute-start(bf16[128,2048]{1,0:T(8,128)(2,1)} %get-tuple-element.237), channel_id=1, source_target_pairs={{0,4},{1,5},{2,6},{3,7},{4,0},{5,1},{6,2},{7,3},{8,12},{9,13},{10,... | collective-permute-start | bytes 1572872 | tf_op jit(solution)/shard_map/ppermute | solution.py:881
  731.6 83.3 %collective-permute-start.35 = (bf16[128,2048]{1,0:T(8,128)(2,1)}, bf16[128,2048]{1,0:T(8,128)(2,1)}, u32[]{:S(2)}, u32[]{:S(2)}) collective-permute-start(bf16[128,2048]{1,0:T(8,128)(2,1)} %get-tuple-element.236), channel_id=1, source_target_pairs={{0,2},{1,3},{2,0},{3,1},{4,6},{5,7},{6,4},{7,5},{8,10},{9,11},{10,... | collective-permute-start | bytes 1572872 | tf_op jit(solution)/shard_map/ppermute | solution.py:881
  823.0 26.3 %collective-permute-start.42 = (bf16[256,2048]{1,0:T(8,128)(2,1)}, bf16[256,2048]{1,0:T(8,128)(2,1)S(1)}, u32[]{:S(2)}, u32[]{:S(2)}) collective-permute-start(bf16[256,2048]{1,0:T(8,128)(2,1)} %get-tuple-element.233), channel_id=1, source_target_pairs={{0,4},{1,5},{2,6},{3,7},{4,0},{5,1},{6,2},{7,3},{8,12},{9,13},{10,... | collective-permute-start | bytes 3145736 | tf_op jit(solution)/shard_map/ppermute | solution.py:881
  824.6 26.4 %collective-permute-start.43 = (bf16[256,2048]{1,0:T(8,128)(2,1)}, bf16[256,2048]{1,0:T(8,128)(2,1)}, u32[]{:S(2)}, u32[]{:S(2)}) collective-permute-start(bf16[256,2048]{1,0:T(8,128)(2,1)} %get-tuple-element.232), channel_id=1, source_target_pairs={{0,2},{1,3},{2,0},{3,1},{4,6},{5,7},{6,4},{7,5},{8,10},{9,11},{10,... | collective-permute-start | bytes 3145736 | tf_op jit(solution)/shard_map/ppermute | solution.py:881
  832.2 63.8 %collective-permute-start.40 = (bf16[512,2048]{1,0:T(8,128)(2,1)}, bf16[512,2048]{1,0:T(8,128)(2,1)}, u32[]{:S(2)}, u32[]{:S(2)}) collective-permute-start(bf16[512,2048]{1,0:T(8,128)(2,1)} %copy-done.23), channel_id=1, source_target_pairs={{0,2},{1,3},{2,0},{3,1},{4,6},{5,7},{6,4},{7,5},{8,10},{9,11},{10,... | collective-permute-start | bytes 6291464 | tf_op jit(solution)/shard_map/ppermute | solution.py:881
  832.8 63.1 %collective-permute-start.41 = (bf16[512,2048]{1,0:T(8,128)(2,1)}, bf16[512,2048]{1,0:T(8,128)(2,1)}, u32[]{:S(2)}, u32[]{:S(2)}) collective-permute-start(bf16[512,2048]{1,0:T(8,128)(2,1)} %copy-done.22), channel_id=1, source_target_pairs={{0,4},{1,5},{2,6},{3,7},{4,0},{5,1},{6,2},{7,3},{8,12},{9,13},{10,... | collective-permute-start | bytes 6291464 | tf_op jit(solution)/shard_map/ppermute | solution.py:881
  860.6 39.8 %collective-permute-start.47 = (f32[24576]{0:T(1024)S(1)}, f32[24576]{0:T(1024)S(1)}, u32[]{:S(2)}, u32[]{:S(2)}) collective-permute-start(f32[24576]{0:T(1024)S(1)} %add.282), channel_id=1, source_target_pairs={{0,2},{1,3},{2,0},{3,1},{4,6},{5,7},{6,4},{7,5},{8,10},{9,11},{10,... | collective-permute-start | bytes 294920 | tf_op jit(solution)/shard_map/ppermute | solution.py:881
  862.1 38.2 %collective-permute-start.48 = (f32[24576]{0:T(1024)S(1)}, f32[24576]{0:T(1024)S(1)}, u32[]{:S(2)}, u32[]{:S(2)}) collective-permute-start(f32[24576]{0:T(1024)S(1)} %add.282), channel_id=1, source_target_pairs={{0,4},{1,5},{2,6},{3,7},{4,0},{5,1},{6,2},{7,3},{8,12},{9,13},{10,... | collective-permute-start | bytes 294920 | tf_op jit(solution)/shard_map/ppermute | solution.py:881
  862.7 37.7 %collective-permute-start.49 = (f32[24576]{0:T(1024)S(1)}, f32[24576]{0:T(1024)S(1)}, u32[]{:S(2)}, u32[]{:S(2)}) collective-permute-start(f32[24576]{0:T(1024)S(1)} %add.282), channel_id=1, source_target_pairs={{0,6},{1,7},{2,4},{3,5},{4,2},{5,3},{6,0},{7,1},{8,14},{9,15},{10,... | collective-permute-start | bytes 294920 | tf_op jit(solution)/shard_map/ppermute | solution.py:881
  898.2 28.2 %collective-permute-start.44 = (bf16[256,2048]{1,0:T(8,128)(2,1)S(1)}, bf16[256,2048]{1,0:T(8,128)(2,1)S(1)}, u32[]{:S(2)}, u32[]{:S(2)}) collective-permute-start(bf16[256,2048]{1,0:T(8,128)(2,1)S(1)} %get-tuple-element.229), channel_id=1, source_target_pairs={{0,4},{1,5},{2,6},{3,7},{4,0},{5,1},{6,2},{7,3},{8,12},{9,13},{10,... | collective-permute-start | bytes 3145736 | tf_op jit(solution)/shard_map/ppermute | solution.py:881
  898.8 27.6 %collective-permute-start.45 = (bf16[256,2048]{1,0:T(8,128)(2,1)S(1)}, bf16[256,2048]{1,0:T(8,128)(2,1)S(1)}, u32[]{:S(2)}, u32[]{:S(2)}) collective-permute-start(bf16[256,2048]{1,0:T(8,128)(2,1)S(1)} %get-tuple-element.228), channel_id=1, source_target_pairs={{0,2},{1,3},{2,0},{3,1},{4,6},{5,7},{6,4},{7,5},{8,10},{9,11},{10,... | collective-permute-start | bytes 3145736 | tf_op jit(solution)/shard_map/ppermute | solution.py:881
  (71 other events, 968.9 us)
Sparse Core Ops, SparseCore 0:
  125.8 55.2 all-gather.1
  522.1 292.7 all-reduce.6
  833.4 162.3 all-reduce.4
where the time goes:
time: 1020 us; the launch traced here: 1010 us
  waiting for transfers between devices  417 us (41%)
  Pallas kernels  353 us (35%)
  other arithmetic  92.7 us (9%)
  starting transfers between devices  83.7 us (8%)
  local copies, waits for them, and re-layouts  50 us (5%)
  between operations  15.1 us (1%)
    ppermute x44, waiting for transfers between devices, swap(): return lax.ppermute(values, 'wide', [(w, w ^ bits) for w in range(width)])  152 us
    pallas_call x6, Pallas kernels, weight_grad(): pl.pallas_call(functools.partial(weight_grad_kernel, len(rights), len(ext...  89.3 us
    pallas_call x3, Pallas kernels, ffn_blocks(): pl.pallas_call(functools.partial(ffn_kernel, block, len(xs), len(gs)), gr...  78.8 us
    psum x1, waiting for transfers between devices, local_chips(): down_grad, up_grad = lax.psum((down_sum, up_sum), 'batch')  77.3 us
    psum x1, waiting for transfers between devices, local_chips(): lax.psum(after((*returned, out_total), up_grad), 'batch')  64.7 us
    ppermute x44, starting transfers between devices, swap(): return lax.ppermute(values, 'wide', [(w, w ^ bits) for w in range(width)])  59.4 us
    ppermute x3, waiting for transfers between devices, local_chips(): slabs = [lax.ppermute(slabs[t], 'wide', routes[t]) for t in range(3)]  59.3 us
    pallas_call x1, Pallas kernels, attend_back(): pl.pallas_call(functools.partial(attend_back_kernel, head_size, len(mixed...  53.7 us
  transfers between devices with their start and end apart: 58, of which 23 were waited for; matrix products, arithmetic and copies ran while one was open for 9% of the time, Pallas kernels for 33%

commit v1 on v0

--- a/solution.py
+++ b/solution.py
@@ -176,7 +176,7 @@
             jax.ShapeDtypeStruct((sequences, heads, length), jnp.float32),
         ],
         compiler_params=pltpu.CompilerParams(vmem_limit_bytes=VMEM_BYTES),
-        cost_estimate=cost(rows * length * lanes * 2, rows * lanes * 8, rows * length * heads // 2),
+        cost_estimate=cost(1, 1),
     )(counts, slots, *mixed)
 
 
@@ -412,7 +412,7 @@
         out_shape=[full, full, jax.ShapeDtypeStruct((rows, model), jnp.bfloat16)],
         input_output_aliases={len(xs) + len(gs) + 7 + k: k for k in range(len(kept))},
         compiler_params=pltpu.CompilerParams(vmem_limit_bytes=VMEM_BYTES),
-        cost_estimate=cost(12 * rows * units * model, 8 * units * model + 8 * rows * model, 4 * rows * units),
+        cost_estimate=cost(1, 1),
     )(counts, *xs, *gs, *ups, *downs, *shifts, *kept)
 
 
@@ -515,7 +515,7 @@
         out_specs=column,
         out_shape=jax.ShapeDtypeStruct((rows, columns), jnp.float32),
         compiler_params=pltpu.CompilerParams(vmem_limit_bytes=VMEM_BYTES),
-        cost_estimate=cost(2 * rows * depth * columns, 2 * depth * columns + 8 * rows * columns),
+        cost_estimate=cost(1, 1),
     )(left, weight, bias[None], hidden, active)
 
 
@@ -575,11 +575,7 @@
         ),
         out_shape=jax.ShapeDtypeStruct((len(xs) * size, 3 * slab), jnp.bfloat16),
         compiler_params=pltpu.CompilerParams(vmem_limit_bytes=VMEM_BYTES),
-        cost_estimate=pl.CostEstimate(
-            flops=6 * len(xs) * size * slab * model,
-            bytes_accessed=6 * slab * model + 2 * len(xs) * size * (model + 3 * slab),
-            transcendentals=0,
-        ),
+        cost_estimate=cost(1, 1),
     )(parts, *xs, weights, shift)
 
 
@@ -644,7 +640,7 @@
             out_ref[...] = total[k * size : (k + 1) * size].astype(out_ref.dtype)
 
 
-def weight_grad(left, columns, tile, rights, extra=None, outputs=1, apart=False):
+def weight_grad(left, columns, tile, rights, extra=None, outputs=1, apart=False, counted=False):
     rows = left.shape[0]
     model = rights[0].shape[1]
     steps = columns.shape[0]
@@ -672,7 +668,7 @@
         ),
         out_shape=[shape] * outputs,
         compiler_params=pltpu.CompilerParams(vmem_limit_bytes=VMEM_BYTES),
-        cost_estimate=cost(1, 1),
+        cost_estimate=cost(2 * steps * tile * rows * model, 4 * rows * model) if counted else cost(1, 1),
     )(columns, left, *rights, *extras)
     return results[0] if outputs == 1 else results
 
@@ -1025,7 +1021,7 @@
     up_shifts = [bias_of(rank)[None], bias_of(other)[None]]
 
     mixed_near = project(parts, 0, normed1, qkv_own, shift_of(rank))
-    qkv_other = after(qkv_other, mixed_near, diagonal1)
+    qkv_other = after(qkv_other, mixed_near)
     lent_near = project(parts, 1, normed1, qkv_other, shift_of(other))
     diagonal1 = after(diagonal1, lent_near)
     lent_far = project(parts, 1, diagonal1, qkv_other, shift_of(other))
@@ -1035,11 +1031,11 @@
     out_whole = lax.all_gather(after(out_weight, diagonal1), "wide", axis=0, tiled=True)
     grad_ffn = (after(active, diagonal1) * grad_out).astype(jnp.bfloat16)
     down_bias_grad = jnp.sum(grad_ffn.astype(jnp.float32), axis=0)
+    grad_ffn = [grad_ffn, swap(grad_ffn, 2), swap(grad_ffn, 4)]
 
     attended, logs = attend(mixed, slots, counts, head_size)
     attended_rows = lax.all_to_all(attended, "wide", split_axis=0, concat_axis=1, tiled=True)
-    grad_ffn = after(grad_ffn, attended_rows)
-    grad_ffn = [grad_ffn, swap(grad_ffn, 2), swap(grad_ffn, 4)]
+    attended_rows = after(attended_rows, grad_ffn[1:])
     up_other, down_other = swap(after((up_weight, down_weight), attended), 1)
     middle = attend_out(attended_rows, out_whole, out_bias, hidden, active)
     normal2, inverse2 = normalize(middle)
@@ -1057,7 +1053,7 @@
         )
         return kept, partial
 
-    kept, partial_own = ffn(2, 0, [after(normed2[0], grad_ffn[1:])], grad_ffn[:1], ())
+    kept, partial_own = ffn(2, 0, normed2[:1], grad_ffn[:1], ())
     normed2[1:] = after(normed2[1:], partial_own)
     diagonal2 = relay(normed2[1], normed2[2])
     diagonal_ffn = relay(*after(grad_ffn[1:], attended_rows))
@@ -1077,7 +1073,9 @@
     down_own, down_lent = weight_grad(after(units, wait), tiles, tile, tokens_ffn, outputs=2)
     wait = scatter2.second(down_lent)
     down_lent = swap(down_lent, 1)
-    up_own, up_lent = weight_grad(after(grad_pres, wait), tiles, tile, tokens2, outputs=2)
+    up_own, up_lent = weight_grad(
+        after(grad_pres, wait), tiles, tile, tokens2, outputs=2, counted=True
+    )
 
     up_lent = swap(up_lent, 1)
     down_sum = lowered(wide(down_own) + wide(after(down_lent, up_own)))

time: 1020 us -> 1010 us (level)
  Pallas kernels: 353 us -> 341 us
    ppermute x44, waiting for transfers between devices: 152 us -> 118 us  [swap(): return lax.ppermute(values, 'wide', [(w, w ^ bits) for w in range(width)])]
    all_to_all x1, waiting for transfers between devices: 22.5 us -> 53.7 us  [local_chips(): lax.all_to_all(attended, 'wide', split_axis=0, concat_axis=1, tiled=True)]
    unnamed x129 -> x123, local copies, waits for them, and re-layouts: 23.2 us -> 22 us
  transfers between devices with their start and end apart: 58 -> 58, of which waited for: 23 -> 19; matrix products, arithmetic and copies ran while one was open for 9% -> 9% of each run, Pallas kernels for 33% -> 33%
where the time goes in v1:
time: 1010 us; the launch traced here: 1000 us
  waiting for transfers between devices  419 us (41%)
  Pallas kernels  341 us (34%)
  other arithmetic  92.1 us (9%)
  starting transfers between devices  86.1 us (9%)
  local copies, waits for them, and re-layouts  48.8 us (5%)
  between operations  15.1 us (1%)
    ppermute x44, waiting for transfers between devices, swap(): return lax.ppermute(values, 'wide', [(w, w ^ bits) for w in range(width)])  118 us
    pallas_call x6, Pallas kernels, weight_grad(): pl.pallas_call(functools.partial(weight_grad_kernel, len(rights), len(ext...  88.9 us
    psum x1, waiting for transfers between devices, local_chips(): down_grad, up_grad = lax.psum((down_sum, up_sum), 'batch')  84.2 us
    pallas_call x3, Pallas kernels, ffn_blocks(): pl.pallas_call(functools.partial(ffn_kernel, block, len(xs), len(gs)), gr...  78.6 us
    psum x1, waiting for transfers between devices, local_chips(): lax.psum(after((*returned, out_total), up_grad), 'batch')  64.7 us
    ppermute x44, starting transfers between devices, swap(): return lax.ppermute(values, 'wide', [(w, w ^ bits) for w in range(width)])  64.5 us
    ppermute x3, waiting for transfers between devices, local_chips(): slabs = [lax.ppermute(slabs[t], 'wide', routes[t]) for t in range(3)]  59.8 us
    all_to_all x1, waiting for transfers between devices, local_chips(): lax.all_to_all(attended, 'wide', split_axis=0, concat_axis=1, tiled=True)  53.7 us
  transfers between devices with their start and end apart: 58, of which 19 were waited for; matrix products, arithmetic and copies ran while one was open for 9% of the time, Pallas kernels for 33%

profile of v1, /device:TPU:0, one launch (start us, length us, event | category | flops | bytes accessed | tf_op | source)
XLA Modules:
  0.0 1001.7 jit_solution(14775217461933092790)
XLA Ops:
  20.3 3.5 collective-permute-start.4
  23.8 50.1 %collective-permute-done.3 = bf16[256,2048]{1,0:T(8,128)(2,1)S(1)} collective-permute-done((bf16[256,2048]{1,0:T(8,128)(2,1)S(1)}, bf16[256,2048]{1,0:T(8,128)(2,1)S(1)}, u32[]{:S(2)}, u32[]{:S(2)}) %collective-permute-start.3) | collective-permute-done | bytes 1048608 | tf_op jit(solution)/shard_map/ppermute | solution.py:1008
  73.9 9.8 collective-permute-done.4
  96.4 10.4 %shard_map.307.refs_0_ = bf16[1536,768]{1,0:T(8,128)(2,1)} custom-call(s32[2,3]{1,0:T(2,128)S(1)} %pad_add_fusion.parts, bf16[512,2048]{1,0:T(8,128)(2,1)S(1)} %copy-done.2, bf16[512,2048]{1,0:T(8,128)(2,1)S(1)} %copy-done.5, bf16[512,2048]{1,0:T(8,128)(2,1)} %copy-done.25, bf16[3,256,2048]{2,1,0:T(8,128)(2,1)} %pad_maximum_fusion.2.refs_3_.refs_2_.own, ...), custom_call_target="tpu_custom_call" | custom-call | flops 1 | bytes 1 | tf_op jit(solution)/shard_map/pallas_call | solution.py:564
  106.8 10.2 %shard_map.308 = bf16[1536,768]{1,0:T(8,128)(2,1)} custom-call(s32[2,3]{1,0:T(2,128)S(1)} %pad_add_fusion.parts, bf16[512,2048]{1,0:T(8,128)(2,1)S(1)} %copy-done.2, bf16[512,2048]{1,0:T(8,128)(2,1)S(1)} %copy-done.5, bf16[512,2048]{1,0:T(8,128)(2,1)} %copy-done.25, bf16[3,256,2048]{2,1,0:T(8,128)(2,1)} %collective-permute-done.7.refs_3_.refs_2_.other, ...), custom_call_target="tpu_custom_call" | custom-call | flops 1 | bytes 1 | tf_op jit(solution)/shard_map/pallas_call | solution.py:564
  117.1 6.0 shard_map.309
  123.7 3.7 convert_reduce_fusion.5
  129.3 5.5 shard_map.310.refs_1_
  134.8 34.5 %shard_map.311 = (bf16[4096,256]{1,0:T(8,128)(2,1)S(1)}, f32[2,4,2048]{2,1,0:T(4,128)S(1)}) custom-call(s32[2]{0:T(128)S(1)} %convert_reduce_fusion.6.counts, s32[2,4]{1,0:T(2,128)S(1)} %xor_add_fusion.slots, bf16[1536,768]{1,0:T(8,128)(2,1)S(1)} %copy-done.12, bf16[512,768]{1,0:T(8,128)(2,1)S(1)} %shard_map.310.refs_1_, ...), custom_call_target="tpu_custom_call" | custom-call | flops 1 | bytes 1 | tf_op jit(solution)/shard_map/pallas_call | solution.py:157
  170.7 4.9 all-to-all-start
  176.4 53.7 %all-to-all-done = bf16[8,512,256]{2,1,0:T(8,128)(2,1)} async-done(((bf16[8,512,256]{2,1,0:T(8,128)(2,1)}), bf16[8,512,256]{2,1,0:T(8,128)(2,1)}, u32[]{:S(2)}, u32[]{:S(2)}) %all-to-all-start) | async-done | bytes 2097184 | tf_op jit(solution)/shard_map/all_to_all | solution.py:1037
  234.8 8.5 shard_map.312
  255.8 25.7 %shard_map.313 = (bf16[2048,2048]{1,0:T(8,128)(2,1)}, bf16[2048,2048]{1,0:T(8,128)(2,1)}, bf16[512,2048]{1,0:T(8,128)(2,1)S(1)}) custom-call(s32[4]{0:T(128)S(1)} %gather_fusion, bf16[512,2048]{1,0:T(8,128)(2,1)} %add_convert_fusion.2.refs_0_.refs_3_, bf16[512,2048]{1,0:T(8,128)(2,1)} %get-tuple-element.219.refs_1_.refs_3_, bf16[1024,2048]{1,0:T(8,128)(2,1)} %refs_4_.5, ...), custom_call_target="tpu_custom_call" | custom-call | flops 1 | bytes 1 | tf_op jit(solution)/shard_map/pallas_call | solution.py:394
  281.5 16.7 %collective-permute-done.12.refs_0_.refs_1_ = bf16[512,2048]{1,0:T(8,128)(2,1)} collective-permute-done((bf16[512,2048]{1,0:T(8,128)(2,1)}, bf16[512,2048]{1,0:T(8,128)(2,1)}, u32[]{:S(2)}, u32[]{:S(2)}) %collective-permute-start.12) | collective-permute-done | bytes 2097184 | tf_op jit(solution)/shard_map/ppermute | solution.py:877
  309.7 29.7 %shard_map.314 = (bf16[2048,2048]{1,0:T(8,128)(2,1)}, bf16[2048,2048]{1,0:T(8,128)(2,1)}, bf16[1024,2048]{1,0:T(8,128)(2,1)}) custom-call(s32[4]{0:T(128)S(1)} %gather_fusion, bf16[512,2048]{1,0:T(8,128)(2,1)} %collective-permute-done.12.refs_0_.refs_1_, ...), custom_call_target="tpu_custom_call", output_to_operand_aliasing={{0}: (11, {}), {1}: (12, {})} | custom-call | flops 1 | bytes 1 | tf_op jit(solution)/shard_map/pallas_call | solution.py:394
  341.1 17.7 %collective-permute-start.20 = (bf16[256,2048]{1,0:T(8,128)(2,1)S(1)}, bf16[256,2048]{1,0:T(8,128)(2,1)S(1)}, u32[]{:S(2)}, u32[]{:S(2)}) collective-permute-start(bf16[256,2048]{1,0:T(8,128)(2,1)S(1)} %get-tuple-element.243), channel_id=1, source_target_pairs={{0,2},{1,3},{2,0},{3,1},{4,6},{5,7},{6,4},{7,5},{8,10},{9,11},{10,... | collective-permute-start | bytes 3145736 | tf_op jit(solution)/shard_map/ppermute | solution.py:877
  359.1 23.2 %shard_map.315 = (bf16[2048,2048]{1,0:T(8,128)(2,1)}, bf16[2048,2048]{1,0:T(8,128)(2,1)}, bf16[512,2048]{1,0:T(8,128)(2,1)}) custom-call(s32[4]{0:T(128)S(1)} %gather_fusion, bf16[256,2048]{1,0:T(8,128)(2,1)S(1)} %collective-permute-done.16.refs_0_.refs_4_, ...), custom_call_target="tpu_custom_call", output_to_operand_aliasing={{0}: (11, {}), {1}: (12, {})} | custom-call | flops 1 | bytes 1 | tf_op jit(solution)/shard_map/pallas_call | solution.py:394
  388.9 25.0 %shard_map.316 = (bf16[1024,2048]{1,0:T(8,128)(2,1)}, bf16[1024,2048]{1,0:T(8,128)(2,1)}) custom-call(s32[4]{0:T(128)S(1)} %iota.43.columns, bf16[2048,2048]{1,0:T(8,128)(2,1)} %get-tuple-element.154.refs_0_.left, bf16[512,2048]{1,0:T(8,128)(2,1)} %collective-permute-done.10.refs_2_.refs_1_, bf16[512,2048]{1,0:T(8,128)(2,1)} %collective-permute-done.11.refs_3_.refs_2_, ...), custom_call_target="tpu_custom_call" | custom-call | flops 1 | bytes 1 | tf_op jit(solution)/shard_map/pallas_call | solution.py:655
  416.4 25.1 %shard_map.317 = (bf16[1024,2048]{1,0:T(8,128)(2,1)}, bf16[1024,2048]{1,0:T(8,128)(2,1)}) custom-call(s32[4]{0:T(128)S(1)} %iota.44.columns, bf16[2048,2048]{1,0:T(8,128)(2,1)} %get-tuple-element.188.refs_0_, bf16[512,2048]{1,0:T(8,128)(2,1)} %collective-permute-done.12.refs_0_.refs_1_, bf16[512,2048]{1,0:T(8,128)(2,1)} %collective-permute-done.13.refs_1_.refs_2_, ...), custom_call_target="tpu_custom_call" | custom-call | flops 17179869184 | bytes 16777216 | tf_op jit(solution)/shard_map/pallas_call | solution.py:655
  444.1 23.3 %collective-permute-done.24 = bf16[256,2048]{1,0:T(8,128)(2,1)S(1)} collective-permute-done((bf16[256,2048]{1,0:T(8,128)(2,1)S(1)}, bf16[256,2048]{1,0:T(8,128)(2,1)S(1)}, u32[]{:S(2)}, u32[]{:S(2)}) %collective-permute-start.24) | collective-permute-done | bytes 1048608 | tf_op jit(solution)/shard_map/ppermute | solution.py:877
  473.1 4.1 convert_reduce_fusion.4
  477.3 6.2 add_convert_fusion.1
  483.5 6.1 add_convert_fusion
  491.2 7.3 shard_map.318
  498.5 5.1 shard_map.319
  505.2 4.4 all-to-all-start.1
  514.4 7.1 shard_map.320
  521.5 14.7 %all-to-all-done.1 = bf16[512,8,256]{2,0,1:T(8,128)(2,1)} async-done(((bf16[512,8,256]{2,0,1:T(8,128)(2,1)}), bf16[512,8,256]{2,0,1:T(8,128)(2,1)}, u32[]{:S(2)}, u32[]{:S(2)}) %all-to-all-start.1) | async-done | bytes 2097184 | tf_op jit(solution)/shard_map/all_to_all | solution.py:1092
  538.9 47.3 %shard_map.321 = (bf16[2048,768]{1,0:T(8,128)(2,1)}, bf16[2048,768]{1,0:T(8,128)(2,1)}) custom-call(s32[2]{0:T(128)S(1)} %convert_reduce_fusion.6.counts, s32[2,4]{1,0:T(2,128)S(1)} %xor_add_fusion.slots, bf16[1536,768]{1,0:T(8,128)(2,1)} %shard_map.307.refs_0_, bf16[512,768]{1,0:T(8,128)(2,1)S(1)} %copy-done.16, ...), custom_call_target="tpu_custom_call" | custom-call | flops 1 | bytes 1 | tf_op jit(solution)/shard_map/pallas_call | solution.py:301
  588.8 23.1 %shard_map.322 = (bf16[512,2048]{1,0:T(8,128)(2,1)S(1)}, bf16[512,2048]{1,0:T(8,128)(2,1)S(1)}, bf16[1024,2048]{1,0:T(8,128)(2,1)}) custom-call(s32[4]{0:T(128)S(1)} %copy-done.18, s32[4]{0:T(128)S(1)} %gather_fusion.1, bf16[2048,2048]{1,0:T(8,128)(2,1)} %get-tuple-element.154.refs_0_.left, bf16[1024,2048]{1,0:T(8,128)(2,1)} %own.1, ...), custom_call_target="tpu_custom_call" | custom-call | flops 1 | bytes 1 | tf_op jit(solution)/shard_map/pallas_call | solution.py:476
  613.3 12.8 %shard_map.323 = bf16[768,2048]{1,0:T(8,128)(2,1)} custom-call(s32[3]{0:T(128)S(1)} %get-tuple-element.268.columns, bf16[2048,768]{1,0:T(8,128)(2,1)} %collective-permute-done.31.refs_0_.theirs, bf16[512,2048]{1,0:T(8,128)(2,1)S(1)} %copy-done.3, bf16[512,2048]{1,0:T(8,128)(2,1)} %copy-done.4, bf16[512,2048]{1,0:T(8,128)(2,1)} %copy-done.25, ...), custom_call_target="tpu_custom_call" | custom-call | flops 1 | bytes 1 | tf_op jit(solution)/shard_map/pallas_call | solution.py:655
  626.9 24.9 %collective-permute-done.30 = bf16[256,2048]{1,0:T(8,128)(2,1)S(1)} collective-permute-done((bf16[256,2048]{1,0:T(8,128)(2,1)S(1)}, bf16[256,2048]{1,0:T(8,128)(2,1)S(1)}, u32[]{:S(2)}, u32[]{:S(2)}) %collective-permute-start.30) | collective-permute-done | bytes 1048608 | tf_op jit(solution)/shard_map/ppermute | solution.py:877
  655.1 20.4 %shard_map.324 = (bf16[512,2048]{1,0:T(8,128)(2,1)}, bf16[512,2048]{1,0:T(8,128)(2,1)}, bf16[1024,2048]{1,0:T(8,128)(2,1)}) custom-call(s32[4]{0:T(128)S(1)} %copy-done.19, s32[2,3]{1,0:T(2,128)S(1)} %pad_add_fusion.parts, s32[4]{0:T(128)S(1)} %gather_fusion, bf16[2048,768]{1,0:T(8,128)(2,1)} %get-tuple-element.189.mine.refs_0_, ...), custom_call_target="tpu_custom_call" | custom-call | flops 1 | bytes 1 | tf_op jit(solution)/shard_map/pallas_call | solution.py:608
  677.2 13.8 %shard_map.325 = (bf16[256,2048]{1,0:T(8,128)(2,1)S(1)}, bf16[256,2048]{1,0:T(8,128)(2,1)S(1)}, bf16[256,2048]{1,0:T(8,128)(2,1)}) custom-call(s32[3]{0:T(128)S(1)} %get-tuple-element.267.columns, bf16[2048,768]{1,0:T(8,128)(2,1)} %get-tuple-element.189.mine.refs_0_, bf16[512,2048]{1,0:T(8,128)(2,1)} %copy-done.1, bf16[512,2048]{1,0:T(8,128)(2,1)} %copy-done.4, ...), custom_call_target="tpu_custom_call" | custom-call | flops 1 | bytes 1 | tf_op jit(solution)/shard_map/pallas_call | solution.py:655
  698.9 12.2 %collective-permute-done.38 = bf16[256,2048]{1,0:T(8,128)(2,1)S(1)} collective-permute-done((bf16[256,2048]{1,0:T(8,128)(2,1)S(1)}, bf16[256,2048]{1,0:T(8,128)(2,1)S(1)}, u32[]{:S(2)}, u32[]{:S(2)}) %collective-permute-start.38) | collective-permute-done | bytes 1048608 | tf_op jit(solution)/shard_map/ppermute | solution.py:1134
  712.2 9.5 collective-permute-start.35
  721.7 84.2 %all-reduce.7.cloned.1.call-done = (bf16[1024,2048]{1,0:T(8,128)(2,1)}, bf16[1024,2048]{1,0:T(8,128)(2,1)}) async-done(((bf16[1024,2048]{1,0:T(8,128)(2,1)}, bf16[1024,2048]{1,0:T(8,128)(2,1)}), (bf16[1024,2048]{1,0:T(8,128)(2,1)}, bf16[1024,2048]{1,0:T(8,128)(2,1)})) %all-reduce.7.cloned.1.call-update) | async-done | bytes 8388624 | tf_op jit(solution)/shard_map/psum | solution.py:1083
  809.5 4.5 add_convert_fusion.5
  818.1 4.7 convert_reduce_fusion
  824.8 15.5 %collective-permute-done.42 = bf16[256,2048]{1,0:T(8,128)(2,1)S(1)} collective-permute-done((bf16[256,2048]{1,0:T(8,128)(2,1)}, bf16[256,2048]{1,0:T(8,128)(2,1)S(1)}, u32[]{:S(2)}, u32[]{:S(2)}) %collective-permute-start.42) | collective-permute-done | bytes 1048608 | tf_op jit(solution)/shard_map/ppermute | solution.py:877
  842.0 3.8 fusion.24
  855.1 31.8 %collective-permute-done.40 = bf16[512,2048]{1,0:T(8,128)(2,1)} collective-permute-done((bf16[512,2048]{1,0:T(8,128)(2,1)}, bf16[512,2048]{1,0:T(8,128)(2,1)}, u32[]{:S(2)}, u32[]{:S(2)}) %collective-permute-start.40) | collective-permute-done | bytes 2097184 | tf_op jit(solution)/shard_map/ppermute | solution.py:877
  895.8 5.2 collective-permute-done.50
  901.0 6.0 collective-permute-done.51
  908.4 4.4 convert_element_type.284
  912.9 4.6 convert_element_type.283
  922.2 64.7 %all-reduce.5.cloned.1.call-done = (bf16[256,2048]{1,0:T(8,128)(2,1)}, bf16[256,2048]{1,0:T(8,128)(2,1)}, bf16[256,2048]{1,0:T(8,128)(2,1)}, bf16[256,2048]{1,0:T(8,128)(2,1)}) async-done(((bf16[256,2048]{1,0:T(8,128)(2,1)}, bf16[256,2048]{1,0:T(8,128)(2,1)}, bf16[256,2048]{1,0:T(8,128)(2,1)}, bf16[256,2048]{1,0:T(8,128)(2,1)}), (bf16[256,2048]{1,0:T(8,128)(2,1)}, bf16[256,2048]{1,0:T(8,128)(2,1)}, ...) | async-done | bytes 4194320 | tf_op jit(solution)/shard_map/psum | solution.py:1139
  989.6 5.4 maximum_convert_fusion
  (307 shorter events, 145.8 us)
Async XLA Ops:
  7.2 226.0 %all-gather.2.cloned.1.call-start = ((), (), s32[]{:S(2)}) async-start(), calls=%async_computation.2 | async-start | bytes 9437184 | tf_op jit(solution)/shard_map/all_gather | solution.py:1031
  12.6 71.1 %collective-permute-start = (bf16[512,2048]{1,0:T(8,128)(2,1)S(1)}, bf16[512,2048]{1,0:T(8,128)(2,1)S(1)}, u32[]{:S(2)}, u32[]{:S(2)}) collective-permute-start(bf16[512,2048]{1,0:T(8,128)(2,1)S(1)} %fusion.7.refs_0_.refs_1_), channel_id=1, source_target_pairs={{0,2},{1,3},{2,0},{3,1},{4,6},{5,7},{6,4},{7,5},{8,10},{9,11},{10,... | collective-permute-start | bytes 6291464 | tf_op jit(solution)/shard_map/ppermute | solution.py:877
  15.6 68.1 %collective-permute-start.1 = (bf16[512,2048]{1,0:T(8,128)(2,1)S(1)}, bf16[512,2048]{1,0:T(8,128)(2,1)S(1)}, u32[]{:S(2)}, u32[]{:S(2)}) collective-permute-start(bf16[512,2048]{1,0:T(8,128)(2,1)S(1)} %fusion.7.refs_0_.refs_1_), channel_id=1, source_target_pairs={{0,4},{1,5},{2,6},{3,7},{4,0},{5,1},{6,2},{7,3},{8,12},{9,13},{10,... | collective-permute-start | bytes 6291464 | tf_op jit(solution)/shard_map/ppermute | solution.py:877
  19.6 54.3 %collective-permute-start.3 = (bf16[256,2048]{1,0:T(8,128)(2,1)S(1)}, bf16[256,2048]{1,0:T(8,128)(2,1)S(1)}, u32[]{:S(2)}, u32[]{:S(2)}) collective-permute-start(bf16[256,2048]{1,0:T(8,128)(2,1)S(1)} %get-tuple-element.246), channel_id=1, source_target_pairs={{0,1},{1,4},{2,7},{3,2},{4,5},{5,0},{6,3},{7,6},{8,9},{9,12},{10,1... | collective-permute-start | bytes 3145736 | tf_op jit(solution)/shard_map/ppermute | solution.py:1008
  20.3 63.3 %collective-permute-start.4 = (bf16[256,2048]{1,0:T(8,128)(2,1)S(1)}, bf16[256,2048]{1,0:T(8,128)(2,1)S(1)}, u32[]{:S(2)}, u32[]{:S(2)}) collective-permute-start(bf16[256,2048]{1,0:T(8,128)(2,1)S(1)} %get-tuple-element.244), channel_id=1, source_target_pairs={{0,2},{1,5},{2,0},{3,3},{4,6},{5,1},{6,4},{7,7},{8,10},{9,13},{10,... | collective-permute-start | bytes 3145736 | tf_op jit(solution)/shard_map/ppermute | solution.py:1008
  85.9 20.8 %collective-permute-start.7 = (bf16[3,256,2048]{2,1,0:T(8,128)(2,1)}, bf16[3,256,2048]{2,1,0:T(8,128)(2,1)}, u32[]{:S(2)}, u32[]{:S(2)}) collective-permute-start(bf16[3,256,2048]{2,1,0:T(8,128)(2,1)} %pad_maximum_fusion.2.refs_3_.refs_2_.own), channel_id=1, source_target_pairs={{0,1},{1,0},{2,3},{3,2},{4,5},{5,4},{6,7},{7,6},{8,9},{9,8},{10,11... | collective-permute-start | bytes 9437192 | tf_op jit(solution)/shard_map/ppermute | solution.py:877
  88.3 28.7 %collective-permute-start.5 = (bf16[256,2048]{1,0:T(8,128)(2,1)}, bf16[256,2048]{1,0:T(8,128)(2,1)S(1)}, u32[]{:S(2)}, u32[]{:S(2)}) collective-permute-start(bf16[256,2048]{1,0:T(8,128)(2,1)} %slice.276), channel_id=1, source_target_pairs={{0,2},{1,3},{2,0},{3,1},{4,6},{5,7},{6,4},{7,5},{8,10},{9,11},{10,... | collective-permute-start | bytes 3145736 | tf_op jit(solution)/shard_map/ppermute | solution.py:877
  90.0 27.0 %collective-permute-start.6 = (bf16[256,2048]{1,0:T(8,128)(2,1)}, bf16[256,2048]{1,0:T(8,128)(2,1)}, u32[]{:S(2)}, u32[]{:S(2)}) collective-permute-start(bf16[256,2048]{1,0:T(8,128)(2,1)} %slice.277), channel_id=1, source_target_pairs={{0,4},{1,5},{2,6},{3,7},{4,0},{5,1},{6,2},{7,3},{8,12},{9,13},{10,... | collective-permute-start | bytes 3145736 | tf_op jit(solution)/shard_map/ppermute | solution.py:877
  127.4 105.8 %collective-permute-start.10 = (bf16[512,2048]{1,0:T(8,128)(2,1)}, bf16[512,2048]{1,0:T(8,128)(2,1)}, u32[]{:S(2)}, u32[]{:S(2)}) collective-permute-start(bf16[512,2048]{1,0:T(8,128)(2,1)} %get-tuple-element.219.refs_1_.refs_3_), channel_id=1, source_target_pairs={{0,2},{1,3},{2,0},{3,1},{4,6},{5,7},{6,4},{7,5},{8,10},{9,11},{10,... | collective-permute-start | bytes 6291464 | tf_op jit(solution)/shard_map/ppermute | solution.py:877
  128.8 104.4 %collective-permute-start.11 = (bf16[512,2048]{1,0:T(8,128)(2,1)}, bf16[512,2048]{1,0:T(8,128)(2,1)}, u32[]{:S(2)}, u32[]{:S(2)}) collective-permute-start(bf16[512,2048]{1,0:T(8,128)(2,1)} %get-tuple-element.219.refs_1_.refs_3_), channel_id=1, source_target_pairs={{0,4},{1,5},{2,6},{3,7},{4,0},{5,1},{6,2},{7,3},{8,12},{9,13},{10,... | collective-permute-start | bytes 6291464 | tf_op jit(solution)/shard_map/ppermute | solution.py:877
  170.7 59.3 %all-to-all-start = ((bf16[8,512,256]{2,1,0:T(8,128)(2,1)}), bf16[8,512,256]{2,1,0:T(8,128)(2,1)}, u32[]{:S(2)}, u32[]{:S(2)}) async-start(bf16[8,512,256]{2,1,0:T(8,128)(2,1)} %bitcast.30), calls=%async_computation | async-start | bytes 4194304 | tf_op jit(solution)/shard_map/all_to_all | solution.py:1037
  175.6 80.2 %collective-permute-start.14 = (bf16[1024,2048]{1,0:T(8,128)(2,1)}, bf16[1024,2048]{1,0:T(8,128)(2,1)}, u32[]{:S(2)}, u32[]{:S(2)}) collective-permute-start(bf16[1024,2048]{1,0:T(8,128)(2,1)} %refs_4_.5), channel_id=1, source_target_pairs={{0,1},{1,0},{2,3},{3,2},{4,5},{5,4},{6,7},{7,6},{8,9},{9,8},{10,11... | collective-permute-start | bytes 12582920 | tf_op jit(solution)/shard_map/ppermute | solution.py:877
  176.1 79.7 %collective-permute-start.15 = (bf16[1024,2048]{1,0:T(8,128)(2,1)}, bf16[1024,2048]{1,0:T(8,128)(2,1)}, u32[]{:S(2)}, u32[]{:S(2)}) collective-permute-start(bf16[1024,2048]{1,0:T(8,128)(2,1)} %own.1), channel_id=1, source_target_pairs={{0,1},{1,0},{2,3},{3,2},{4,5},{5,4},{6,7},{7,6},{8,9},{9,8},{10,11... | collective-permute-start | bytes 12582920 | tf_op jit(solution)/shard_map/ppermute | solution.py:877
  251.4 46.9 %collective-permute-start.12 = (bf16[512,2048]{1,0:T(8,128)(2,1)}, bf16[512,2048]{1,0:T(8,128)(2,1)}, u32[]{:S(2)}, u32[]{:S(2)}) collective-permute-start(bf16[512,2048]{1,0:T(8,128)(2,1)} %add_convert_fusion.2.refs_0_.refs_3_), channel_id=1, source_target_pairs={{0,2},{1,3},{2,0},{3,1},{4,6},{5,7},{6,4},{7,5},{8,10},{9,11},{10,... | collective-permute-start | bytes 6291464 | tf_op jit(solution)/shard_map/ppermute | solution.py:877
  252.4 47.3 %collective-permute-start.13 = (bf16[512,2048]{1,0:T(8,128)(2,1)}, bf16[512,2048]{1,0:T(8,128)(2,1)}, u32[]{:S(2)}, u32[]{:S(2)}) collective-permute-start(bf16[512,2048]{1,0:T(8,128)(2,1)} %add_convert_fusion.2.refs_0_.refs_3_), channel_id=1, source_target_pairs={{0,4},{1,5},{2,6},{3,7},{4,0},{5,1},{6,2},{7,3},{8,12},{9,13},{10,... | collective-permute-start | bytes 6291464 | tf_op jit(solution)/shard_map/ppermute | solution.py:877
  302.0 56.8 %collective-permute-start.16 = (bf16[256,2048]{1,0:T(8,128)(2,1)}, bf16[256,2048]{1,0:T(8,128)(2,1)S(1)}, u32[]{:S(2)}, u32[]{:S(2)}) collective-permute-start(bf16[256,2048]{1,0:T(8,128)(2,1)} %slice.219), channel_id=1, source_target_pairs={{0,2},{1,3},{2,0},{3,1},{4,6},{5,7},{6,4},{7,5},{8,10},{9,11},{10,... | collective-permute-start | bytes 3145736 | tf_op jit(solution)/shard_map/ppermute | solution.py:877
  303.6 55.6 %collective-permute-start.17 = (bf16[256,2048]{1,0:T(8,128)(2,1)S(1)}, bf16[256,2048]{1,0:T(8,128)(2,1)S(1)}, u32[]{:S(2)}, u32[]{:S(2)}) collective-permute-start(bf16[256,2048]{1,0:T(8,128)(2,1)S(1)} %slice.220), channel_id=1, source_target_pairs={{0,4},{1,5},{2,6},{3,7},{4,0},{5,1},{6,2},{7,3},{8,12},{9,13},{10,... | collective-permute-start | bytes 3145736 | tf_op jit(solution)/shard_map/ppermute | solution.py:877
  304.2 55.0 %collective-permute-start.18 = (bf16[256,2048]{1,0:T(8,128)(2,1)S(1)}, bf16[256,2048]{1,0:T(8,128)(2,1)S(1)}, u32[]{:S(2)}, u32[]{:S(2)}) collective-permute-start(bf16[256,2048]{1,0:T(8,128)(2,1)S(1)} %slice.221), channel_id=1, source_target_pairs={{0,2},{1,3},{2,0},{3,1},{4,6},{5,7},{6,4},{7,5},{8,10},{9,11},{10,... | collective-permute-start | bytes 3145736 | tf_op jit(solution)/shard_map/ppermute | solution.py:877
  308.2 50.9 %collective-permute-start.19 = (bf16[256,2048]{1,0:T(8,128)(2,1)}, bf16[256,2048]{1,0:T(8,128)(2,1)S(1)}, u32[]{:S(2)}, u32[]{:S(2)}) collective-permute-start(bf16[256,2048]{1,0:T(8,128)(2,1)} %slice.222), channel_id=1, source_target_pairs={{0,4},{1,5},{2,6},{3,7},{4,0},{5,1},{6,2},{7,3},{8,12},{9,13},{10,... | collective-permute-start | bytes 3145736 | tf_op jit(solution)/shard_map/ppermute | solution.py:877
  341.1 46.4 %collective-permute-start.20 = (bf16[256,2048]{1,0:T(8,128)(2,1)S(1)}, bf16[256,2048]{1,0:T(8,128)(2,1)S(1)}, u32[]{:S(2)}, u32[]{:S(2)}) collective-permute-start(bf16[256,2048]{1,0:T(8,128)(2,1)S(1)} %get-tuple-element.243), channel_id=1, source_target_pairs={{0,2},{1,3},{2,0},{3,1},{4,6},{5,7},{6,4},{7,5},{8,10},{9,11},{10,... | collective-permute-start | bytes 3145736 | tf_op jit(solution)/shard_map/ppermute | solution.py:877
  358.8 28.8 %collective-permute-start.21 = (bf16[256,2048]{1,0:T(8,128)(2,1)S(1)}, bf16[256,2048]{1,0:T(8,128)(2,1)S(1)}, u32[]{:S(2)}, u32[]{:S(2)}) collective-permute-start(bf16[256,2048]{1,0:T(8,128)(2,1)S(1)} %get-tuple-element.242), channel_id=1, source_target_pairs={{0,4},{1,5},{2,6},{3,7},{4,0},{5,1},{6,2},{7,3},{8,12},{9,13},{10,... | collective-permute-start | bytes 3145736 | tf_op jit(solution)/shard_map/ppermute | solution.py:877
  385.6 28.4 %collective-permute-start.22 = (bf16[256,2048]{1,0:T(8,128)(2,1)}, bf16[256,2048]{1,0:T(8,128)(2,1)}, u32[]{:S(2)}, u32[]{:S(2)}) collective-permute-start(bf16[256,2048]{1,0:T(8,128)(2,1)} %get-tuple-element.250), channel_id=1, source_target_pairs={{0,2},{1,3},{2,0},{3,1},{4,6},{5,7},{6,4},{7,5},{8,10},{9,11},{10,... | collective-permute-start | bytes 3145736 | tf_op jit(solution)/shard_map/ppermute | solution.py:877
  387.5 26.5 %collective-permute-start.23 = (bf16[256,2048]{1,0:T(8,128)(2,1)}, bf16[256,2048]{1,0:T(8,128)(2,1)}, u32[]{:S(2)}, u32[]{:S(2)}) collective-permute-start(bf16[256,2048]{1,0:T(8,128)(2,1)} %get-tuple-element.249), channel_id=1, source_target_pairs={{0,4},{1,5},{2,6},{3,7},{4,0},{5,1},{6,2},{7,3},{8,12},{9,13},{10,... | collective-permute-start | bytes 3145736 | tf_op jit(solution)/shard_map/ppermute | solution.py:877
  413.9 63.4 %collective-permute-start.26 = (bf16[1024,2048]{1,0:T(8,128)(2,1)}, bf16[1024,2048]{1,0:T(8,128)(2,1)}, u32[]{:S(2)}, u32[]{:S(2)}) collective-permute-start(bf16[1024,2048]{1,0:T(8,128)(2,1)} %get-tuple-element.136), channel_id=1, source_target_pairs={{0,1},{1,0},{2,3},{3,2},{4,5},{5,4},{6,7},{7,6},{8,9},{9,8},{10,11... | collective-permute-start | bytes 12582920 | tf_op jit(solution)/shard_map/ppermute | solution.py:877
  441.4 42.0 %collective-permute-start.27 = (bf16[1024,2048]{1,0:T(8,128)(2,1)}, bf16[1024,2048]{1,0:T(8,128)(2,1)}, u32[]{:S(2)}, u32[]{:S(2)}) collective-permute-start(bf16[1024,2048]{1,0:T(8,128)(2,1)} %get-tuple-element.146), channel_id=1, source_target_pairs={{0,1},{1,0},{2,3},{3,2},{4,5},{5,4},{6,7},{7,6},{8,9},{9,8},{10,11... | collective-permute-start | bytes 12582920 | tf_op jit(solution)/shard_map/ppermute | solution.py:877
  442.0 25.4 %collective-permute-start.24 = (bf16[256,2048]{1,0:T(8,128)(2,1)S(1)}, bf16[256,2048]{1,0:T(8,128)(2,1)S(1)}, u32[]{:S(2)}, u32[]{:S(2)}) collective-permute-start(bf16[256,2048]{1,0:T(8,128)(2,1)S(1)} %get-tuple-element.241), channel_id=1, source_target_pairs={{0,4},{1,5},{2,6},{3,7},{4,0},{5,1},{6,2},{7,3},{8,12},{9,13},{10,... | collective-permute-start | bytes 3145736 | tf_op jit(solution)/shard_map/ppermute | solution.py:877
  444.0 24.9 %collective-permute-start.25 = (bf16[256,2048]{1,0:T(8,128)(2,1)S(1)}, bf16[256,2048]{1,0:T(8,128)(2,1)S(1)}, u32[]{:S(2)}, u32[]{:S(2)}) collective-permute-start(bf16[256,2048]{1,0:T(8,128)(2,1)S(1)} %get-tuple-element.240), channel_id=1, source_target_pairs={{0,2},{1,3},{2,0},{3,1},{4,6},{5,7},{6,4},{7,5},{8,10},{9,11},{10,... | collective-permute-start | bytes 3145736 | tf_op jit(solution)/shard_map/ppermute | solution.py:877
  505.2 31.0 %all-to-all-start.1 = ((bf16[512,8,256]{2,0,1:T(8,128)(2,1)}), bf16[512,8,256]{2,0,1:T(8,128)(2,1)}, u32[]{:S(2)}, u32[]{:S(2)}) async-start(bf16[512,8,256]{2,0,1:T(8,128)(2,1)} %bitcast.39), calls=%async_computation.1 | async-start | bytes 4194304 | tf_op jit(solution)/shard_map/all_to_all | solution.py:1092
  509.6 296.4 %all-reduce.7.cloned.1.call-start = ((), (), s32[]{:S(2)}) async-start(), calls=%async_computation.4 | async-start | bytes 16777216 | tf_op jit(solution)/shard_map/psum | solution.py:1083
  510.3 476.5 %all-reduce.5.cloned.1.call-start = ((), (), s32[]{:S(2)}) async-start(), calls=%async_computation.3 | async-start | bytes 8388608 | tf_op jit(solution)/shard_map/psum | solution.py:1139
  586.2 27.0 %collective-permute-start.31 = (bf16[2048,768]{1,0:T(8,128)(2,1)}, bf16[2048,768]{1,0:T(8,128)(2,1)}, u32[]{:S(2)}, u32[]{:S(2)}) collective-permute-start(bf16[2048,768]{1,0:T(8,128)(2,1)} %get-tuple-element.190), channel_id=1, source_target_pairs={{0,1},{1,0},{2,3},{3,2},{4,5},{5,4},{6,7},{7,6},{8,9},{9,8},{10,11... | collective-permute-start | bytes 9437192 | tf_op jit(solution)/shard_map/ppermute | solution.py:877
  626.1 49.4 %collective-permute-start.36 = (bf16[768,2048]{1,0:T(8,128)(2,1)}, bf16[768,2048]{1,0:T(8,128)(2,1)S(1)}, u32[]{:S(2)}, u32[]{:S(2)}) collective-permute-start(bf16[768,2048]{1,0:T(8,128)(2,1)} %shard_map.323), channel_id=1, source_target_pairs={{0,1},{1,0},{2,3},{3,2},{4,5},{5,4},{6,7},{7,6},{8,9},{9,8},{10,11... | collective-permute-start | bytes 9437192 | tf_op jit(solution)/shard_map/ppermute | solution.py:877
  626.2 25.6 %collective-permute-start.30 = (bf16[256,2048]{1,0:T(8,128)(2,1)S(1)}, bf16[256,2048]{1,0:T(8,128)(2,1)S(1)}, u32[]{:S(2)}, u32[]{:S(2)}) collective-permute-start(bf16[256,2048]{1,0:T(8,128)(2,1)S(1)} %pad_maximum_fusion.4), channel_id=1, source_target_pairs={{0,4},{1,5},{2,6},{3,7},{4,0},{5,1},{6,2},{7,3},{8,12},{9,13},{10,... | collective-permute-start | bytes 3145736 | tf_op jit(solution)/shard_map/ppermute | solution.py:877
  626.3 25.5 %collective-permute-start.29 = (bf16[256,2048]{1,0:T(8,128)(2,1)S(1)}, bf16[256,2048]{1,0:T(8,128)(2,1)S(1)}, u32[]{:S(2)}, u32[]{:S(2)}) collective-permute-start(bf16[256,2048]{1,0:T(8,128)(2,1)S(1)} %pad_maximum_fusion.3), channel_id=1, source_target_pairs={{0,2},{1,3},{2,0},{3,1},{4,6},{5,7},{6,4},{7,5},{8,10},{9,11},{10,... | collective-permute-start | bytes 3145736 | tf_op jit(solution)/shard_map/ppermute | solution.py:877
  691.8 117.7 %collective-permute-start.32 = (bf16[512,2048]{1,0:T(8,128)(2,1)}, bf16[512,2048]{1,0:T(8,128)(2,1)}, u32[]{:S(2)}, u32[]{:S(2)}) collective-permute-start(bf16[512,2048]{1,0:T(8,128)(2,1)} %get-tuple-element.164), channel_id=1, source_target_pairs={{0,2},{1,3},{2,0},{3,1},{4,6},{5,7},{6,4},{7,5},{8,10},{9,11},{10,... | collective-permute-start | bytes 6291464 | tf_op jit(solution)/shard_map/ppermute | solution.py:877
  694.8 114.6 %collective-permute-start.33 = (bf16[512,2048]{1,0:T(8,128)(2,1)}, bf16[512,2048]{1,0:T(8,128)(2,1)}, u32[]{:S(2)}, u32[]{:S(2)}) collective-permute-start(bf16[512,2048]{1,0:T(8,128)(2,1)} %get-tuple-element.165), channel_id=1, source_target_pairs={{0,4},{1,5},{2,6},{3,7},{4,0},{5,1},{6,2},{7,3},{8,12},{9,13},{10,... | collective-permute-start | bytes 6291464 | tf_op jit(solution)/shard_map/ppermute | solution.py:877
  694.8 111.1 %collective-permute-start.39 = (bf16[256,2048]{1,0:T(8,128)(2,1)}, bf16[256,2048]{1,0:T(8,128)(2,1)}, u32[]{:S(2)}, u32[]{:S(2)}) collective-permute-start(bf16[256,2048]{1,0:T(8,128)(2,1)} %get-tuple-element.170), channel_id=1, source_target_pairs={{2,0},{5,1},{0,2},{3,3},{6,4},{1,5},{4,6},{7,7},{10,8},{13,9},{8,1... | collective-permute-start | bytes 3145736 | tf_op jit(solution)/shard_map/ppermute | solution.py:1134
  696.9 109.1 %collective-permute-start.34 = (bf16[128,2048]{1,0:T(8,128)(2,1)}, bf16[128,2048]{1,0:T(8,128)(2,1)}, u32[]{:S(2)}, u32[]{:S(2)}) collective-permute-start(bf16[128,2048]{1,0:T(8,128)(2,1)} %get-tuple-element.235), channel_id=1, source_target_pairs={{0,4},{1,5},{2,6},{3,7},{4,0},{5,1},{6,2},{7,3},{8,12},{9,13},{10,... | collective-permute-start | bytes 1572872 | tf_op jit(solution)/shard_map/ppermute | solution.py:877
  712.2 93.7 %collective-permute-start.35 = (bf16[128,2048]{1,0:T(8,128)(2,1)}, bf16[128,2048]{1,0:T(8,128)(2,1)}, u32[]{:S(2)}, u32[]{:S(2)}) collective-permute-start(bf16[128,2048]{1,0:T(8,128)(2,1)} %get-tuple-element.234), channel_id=1, source_target_pairs={{0,2},{1,3},{2,0},{3,1},{4,6},{5,7},{6,4},{7,5},{8,10},{9,11},{10,... | collective-permute-start | bytes 1572872 | tf_op jit(solution)/shard_map/ppermute | solution.py:877
  814.0 26.3 %collective-permute-start.42 = (bf16[256,2048]{1,0:T(8,128)(2,1)}, bf16[256,2048]{1,0:T(8,128)(2,1)S(1)}, u32[]{:S(2)}, u32[]{:S(2)}) collective-permute-start(bf16[256,2048]{1,0:T(8,128)(2,1)} %get-tuple-element.231), channel_id=1, source_target_pairs={{0,4},{1,5},{2,6},{3,7},{4,0},{5,1},{6,2},{7,3},{8,12},{9,13},{10,... | collective-permute-start | bytes 3145736 | tf_op jit(solution)/shard_map/ppermute | solution.py:877
  815.5 26.4 %collective-permute-start.43 = (bf16[256,2048]{1,0:T(8,128)(2,1)}, bf16[256,2048]{1,0:T(8,128)(2,1)}, u32[]{:S(2)}, u32[]{:S(2)}) collective-permute-start(bf16[256,2048]{1,0:T(8,128)(2,1)} %get-tuple-element.230), channel_id=1, source_target_pairs={{0,2},{1,3},{2,0},{3,1},{4,6},{5,7},{6,4},{7,5},{8,10},{9,11},{10,... | collective-permute-start | bytes 3145736 | tf_op jit(solution)/shard_map/ppermute | solution.py:877
  823.1 63.8 %collective-permute-start.40 = (bf16[512,2048]{1,0:T(8,128)(2,1)}, bf16[512,2048]{1,0:T(8,128)(2,1)}, u32[]{:S(2)}, u32[]{:S(2)}) collective-permute-start(bf16[512,2048]{1,0:T(8,128)(2,1)} %copy-done.21), channel_id=1, source_target_pairs={{0,2},{1,3},{2,0},{3,1},{4,6},{5,7},{6,4},{7,5},{8,10},{9,11},{10,... | collective-permute-start | bytes 6291464 | tf_op jit(solution)/shard_map/ppermute | solution.py:877
  823.8 63.1 %collective-permute-start.41 = (bf16[512,2048]{1,0:T(8,128)(2,1)}, bf16[512,2048]{1,0:T(8,128)(2,1)}, u32[]{:S(2)}, u32[]{:S(2)}) collective-permute-start(bf16[512,2048]{1,0:T(8,128)(2,1)} %copy-done.20), channel_id=1, source_target_pairs={{0,4},{1,5},{2,6},{3,7},{4,0},{5,1},{6,2},{7,3},{8,12},{9,13},{10,... | collective-permute-start | bytes 6291464 | tf_op jit(solution)/shard_map/ppermute | solution.py:877
  851.6 39.8 %collective-permute-start.47 = (f32[24576]{0:T(1024)S(1)}, f32[24576]{0:T(1024)S(1)}, u32[]{:S(2)}, u32[]{:S(2)}) collective-permute-start(f32[24576]{0:T(1024)S(1)} %add.282), channel_id=1, source_target_pairs={{0,2},{1,3},{2,0},{3,1},{4,6},{5,7},{6,4},{7,5},{8,10},{9,11},{10,... | collective-permute-start | bytes 294920 | tf_op jit(solution)/shard_map/ppermute | solution.py:877
  853.1 38.2 %collective-permute-start.48 = (f32[24576]{0:T(1024)S(1)}, f32[24576]{0:T(1024)S(1)}, u32[]{:S(2)}, u32[]{:S(2)}) collective-permute-start(f32[24576]{0:T(1024)S(1)} %add.282), channel_id=1, source_target_pairs={{0,4},{1,5},{2,6},{3,7},{4,0},{5,1},{6,2},{7,3},{8,12},{9,13},{10,... | collective-permute-start | bytes 294920 | tf_op jit(solution)/shard_map/ppermute | solution.py:877
  853.6 37.7 %collective-permute-start.49 = (f32[24576]{0:T(1024)S(1)}, f32[24576]{0:T(1024)S(1)}, u32[]{:S(2)}, u32[]{:S(2)}) collective-permute-start(f32[24576]{0:T(1024)S(1)} %add.282), channel_id=1, source_target_pairs={{0,6},{1,7},{2,4},{3,5},{4,2},{5,3},{6,0},{7,1},{8,14},{9,15},{10,... | collective-permute-start | bytes 294920 | tf_op jit(solution)/shard_map/ppermute | solution.py:877
  889.2 28.2 %collective-permute-start.44 = (bf16[256,2048]{1,0:T(8,128)(2,1)S(1)}, bf16[256,2048]{1,0:T(8,128)(2,1)S(1)}, u32[]{:S(2)}, u32[]{:S(2)}) collective-permute-start(bf16[256,2048]{1,0:T(8,128)(2,1)S(1)} %get-tuple-element.227), channel_id=1, source_target_pairs={{0,4},{1,5},{2,6},{3,7},{4,0},{5,1},{6,2},{7,3},{8,12},{9,13},{10,... | collective-permute-start | bytes 3145736 | tf_op jit(solution)/shard_map/ppermute | solution.py:877
  889.8 27.6 %collective-permute-start.45 = (bf16[256,2048]{1,0:T(8,128)(2,1)S(1)}, bf16[256,2048]{1,0:T(8,128)(2,1)S(1)}, u32[]{:S(2)}, u32[]{:S(2)}) collective-permute-start(bf16[256,2048]{1,0:T(8,128)(2,1)S(1)} %get-tuple-element.226), channel_id=1, source_target_pairs={{0,2},{1,3},{2,0},{3,1},{4,6},{5,7},{6,4},{7,5},{8,10},{9,11},{10,... | collective-permute-start | bytes 3145736 | tf_op jit(solution)/shard_map/ppermute | solution.py:877
  (68 other events, 937.3 us)
Sparse Core Ops, SparseCore 0:
  117.1 86.3 all-gather.1
  513.0 292.8 all-reduce.6
  824.4 162.3 all-reduce.4

commit v2 on v1

--- a/solution.py
+++ b/solution.py
@@ -1079,22 +1079,22 @@
 
     up_lent = swap(up_lent, 1)
     down_sum = lowered(wide(down_own) + wide(after(down_lent, up_own)))
-    up_sum = lowered(wide(up_own) + wide(up_lent))
-    down_grad, up_grad = lax.psum((down_sum, up_sum), "batch")
     grad_middle, ln2_gain_grad, ln2_bias_grad = normalize_back(
         scatter2.finish(up_own), ln2_gain, normal2, inverse2
     )
     grad_middle = grad_out + grad_middle
     grad_branch = (active * grad_middle).astype(jnp.bfloat16)
     out_bias_grad = jnp.sum(grad_branch.astype(jnp.float32), axis=0)
-    grad_branch = after(grad_branch, down_sum, up_sum)
+    grad_branch = after(grad_branch, down_sum)
     grad_attended = attend_out_back(grad_branch, out_whole)
     grad_heads = lax.all_to_all(grad_attended, "wide", split_axis=1, concat_axis=0, tiled=True)
     owners = 2 * block_chip + (rank & 1)
     grad_branch = after(grad_branch, grad_attended)
     out_lent = weight_grad(attended_rows, owners ^ 1, slab, [grad_branch])
+    up_sum = lowered(wide(up_own) + wide(after(up_lent, out_lent)))
+    down_grad, up_grad = lax.psum((down_sum, up_sum), "batch")
     out_lent = swap(out_lent, 1)
-    out_own = weight_grad(after(attended_rows, out_lent), owners, slab, [grad_branch], out_lent)
+    out_own = weight_grad(after(attended_rows, up_sum), owners, slab, [grad_branch], out_lent)
 
     back_own, back_other = attend_back(
         mixed, slots, after(grad_heads, out_own), attended, logs, counts, head_size

time: 1010 us -> 984 us (0.974)
  waiting for transfers between devices: 419 us -> 383 us
  Pallas kernels: 341 us -> 355 us
    ppermute x44, waiting for transfers between devices: 118 us -> 92.2 us  [swap(): return lax.ppermute(values, 'wide', [(w, w ^ bits) for w in range(width)])]
  transfers between devices with their start and end apart: 58 -> 58, of which waited for: 19 -> 18; matrix products, arithmetic and copies ran while one was open for 9% -> 10% of each run, Pallas kernels for 33% -> 36%
where the time goes in v2:
time: 984 us; the launch traced here: 978 us
  waiting for transfers between devices  383 us (39%)
  Pallas kernels  355 us (36%)
  other arithmetic  96.9 us (10%)
  starting transfers between devices  80.3 us (8%)
  local copies, waits for them, and re-layouts  47.8 us (5%)
  between operations  15.1 us (2%)
    ppermute x44, waiting for transfers between devices, swap(): return lax.ppermute(values, 'wide', [(w, w ^ bits) for w in range(width)])  92.2 us
    pallas_call x6, Pallas kernels, weight_grad(): pl.pallas_call(functools.partial(weight_grad_kernel, len(rights), len(ext...  89.1 us
    psum x1, waiting for transfers between devices, local_chips(): down_grad, up_grad = lax.psum((down_sum, up_sum), 'batch')  83.5 us
    pallas_call x3, Pallas kernels, ffn_blocks(): pl.pallas_call(functools.partial(ffn_kernel, block, len(xs), len(gs)), gr...  82.6 us
    psum x1, waiting for transfers between devices, local_chips(): lax.psum(after((*returned, out_total), up_grad), 'batch')  64.6 us
    ppermute x3, waiting for transfers between devices, local_chips(): slabs = [lax.ppermute(slabs[t], 'wide', routes[t]) for t in range(3)]  59.8 us
    ppermute x44, starting transfers between devices, swap(): return lax.ppermute(values, 'wide', [(w, w ^ bits) for w in range(width)])  56 us
    pallas_call x1, Pallas kernels, attend_back(): pl.pallas_call(functools.partial(attend_back_kernel, head_size, len(mixed...  53.9 us
  transfers between devices with their start and end apart: 58, of which 18 were waited for; matrix products, arithmetic and copies ran while one was open for 10% of the time, Pallas kernels for 36%

profile of v2, /device:TPU:0, one launch (start us, length us, event | category | flops | bytes accessed | tf_op | source)
XLA Modules:
  0.0 978.1 jit_solution(16792637628011121174)
XLA Ops:
  20.3 3.5 collective-permute-start.4
  23.8 50.1 %collective-permute-done.3 = bf16[256,2048]{1,0:T(8,128)(2,1)S(1)} collective-permute-done((bf16[256,2048]{1,0:T(8,128)(2,1)S(1)}, bf16[256,2048]{1,0:T(8,128)(2,1)S(1)}, u32[]{:S(2)}, u32[]{:S(2)}) %collective-permute-start.3) | collective-permute-done | bytes 1048608 | tf_op jit(solution)/shard_map/ppermute | solution.py:1008
  73.9 9.8 collective-permute-done.4
  96.3 10.4 %shard_map.307.refs_0_ = bf16[1536,768]{1,0:T(8,128)(2,1)} custom-call(s32[2,3]{1,0:T(2,128)S(1)} %pad_add_fusion.parts, bf16[512,2048]{1,0:T(8,128)(2,1)S(1)} %copy-done.2, bf16[512,2048]{1,0:T(8,128)(2,1)S(1)} %copy-done.5, bf16[512,2048]{1,0:T(8,128)(2,1)} %copy-done.24, bf16[3,256,2048]{2,1,0:T(8,128)(2,1)} %pad_maximum_fusion.2.refs_3_.refs_2_.own, ...), custom_call_target="tpu_custom_call" | custom-call | flops 1 | bytes 1 | tf_op jit(solution)/shard_map/pallas_call | solution.py:564
  106.7 10.2 %shard_map.308 = bf16[1536,768]{1,0:T(8,128)(2,1)} custom-call(s32[2,3]{1,0:T(2,128)S(1)} %pad_add_fusion.parts, bf16[512,2048]{1,0:T(8,128)(2,1)S(1)} %copy-done.2, bf16[512,2048]{1,0:T(8,128)(2,1)S(1)} %copy-done.5, bf16[512,2048]{1,0:T(8,128)(2,1)} %copy-done.24, bf16[3,256,2048]{2,1,0:T(8,128)(2,1)} %collective-permute-done.7.refs_3_.refs_2_.other, ...), custom_call_target="tpu_custom_call" | custom-call | flops 1 | bytes 1 | tf_op jit(solution)/shard_map/pallas_call | solution.py:564
  117.0 6.0 shard_map.309
  123.6 3.7 convert_reduce_fusion.5
  129.3 5.5 shard_map.310.refs_1_
  134.8 40.1 %shard_map.311 = (bf16[4096,256]{1,0:T(8,128)(2,1)S(1)}, f32[2,4,2048]{2,1,0:T(4,128)S(1)}) custom-call(s32[2]{0:T(128)S(1)} %convert_reduce_fusion.6.counts, s32[2,4]{1,0:T(2,128)S(1)} %xor_add_fusion.slots, bf16[1536,768]{1,0:T(8,128)(2,1)S(1)} %copy-done.11, bf16[512,768]{1,0:T(8,128)(2,1)S(1)} %shard_map.310.refs_1_, ...), custom_call_target="tpu_custom_call" | custom-call | flops 1 | bytes 1 | tf_op jit(solution)/shard_map/pallas_call | solution.py:157
  176.2 4.9 all-to-all-start
  181.8 48.1 %all-to-all-done = bf16[8,512,256]{2,1,0:T(8,128)(2,1)} async-done(((bf16[8,512,256]{2,1,0:T(8,128)(2,1)}), bf16[8,512,256]{2,1,0:T(8,128)(2,1)}, u32[]{:S(2)}, u32[]{:S(2)}) %all-to-all-start) | async-done | bytes 2097184 | tf_op jit(solution)/shard_map/all_to_all | solution.py:1037
  234.8 8.5 shard_map.312
  255.8 25.7 %shard_map.313 = (bf16[2048,2048]{1,0:T(8,128)(2,1)}, bf16[2048,2048]{1,0:T(8,128)(2,1)}, bf16[512,2048]{1,0:T(8,128)(2,1)S(1)}) custom-call(s32[4]{0:T(128)S(1)} %gather_fusion, bf16[512,2048]{1,0:T(8,128)(2,1)} %add_convert_fusion.2.refs_0_.refs_3_, bf16[512,2048]{1,0:T(8,128)(2,1)} %get-tuple-element.221.refs_1_.refs_3_, bf16[1024,2048]{1,0:T(8,128)(2,1)} %refs_4_.5, ...), custom_call_target="tpu_custom_call" | custom-call | flops 1 | bytes 1 | tf_op jit(solution)/shard_map/pallas_call | solution.py:394
  281.5 16.7 %collective-permute-done.12.refs_0_.refs_1_ = bf16[512,2048]{1,0:T(8,128)(2,1)} collective-permute-done((bf16[512,2048]{1,0:T(8,128)(2,1)}, bf16[512,2048]{1,0:T(8,128)(2,1)}, u32[]{:S(2)}, u32[]{:S(2)}) %collective-permute-start.12) | collective-permute-done | bytes 2097184 | tf_op jit(solution)/shard_map/ppermute | solution.py:877
  309.7 47.0 %shard_map.314 = (bf16[2048,2048]{1,0:T(8,128)(2,1)}, bf16[2048,2048]{1,0:T(8,128)(2,1)}, bf16[1024,2048]{1,0:T(8,128)(2,1)}) custom-call(s32[4]{0:T(128)S(1)} %gather_fusion, bf16[512,2048]{1,0:T(8,128)(2,1)} %collective-permute-done.12.refs_0_.refs_1_, ...), custom_call_target="tpu_custom_call", output_to_operand_aliasing={{0}: (11, {}), {1}: (12, {})} | custom-call | flops 1 | bytes 1 | tf_op jit(solution)/shard_map/pallas_call | solution.py:394
  359.3 9.9 %shard_map.315 = (bf16[2048,2048]{1,0:T(8,128)(2,1)}, bf16[2048,2048]{1,0:T(8,128)(2,1)}, bf16[512,2048]{1,0:T(8,128)(2,1)}) custom-call(s32[4]{0:T(128)S(1)} %gather_fusion, bf16[256,2048]{1,0:T(8,128)(2,1)S(1)} %collective-permute-done.16.refs_0_.refs_4_, ...), custom_call_target="tpu_custom_call", output_to_operand_aliasing={{0}: (11, {}), {1}: (12, {})} | custom-call | flops 1 | bytes 1 | tf_op jit(solution)/shard_map/pallas_call | solution.py:394
  372.4 14.5 %collective-permute-start.20 = (bf16[256,2048]{1,0:T(8,128)(2,1)}, bf16[256,2048]{1,0:T(8,128)(2,1)}, u32[]{:S(2)}, u32[]{:S(2)}) collective-permute-start(bf16[256,2048]{1,0:T(8,128)(2,1)} %get-tuple-element.252), channel_id=1, source_target_pairs={{0,2},{1,3},{2,0},{3,1},{4,6},{5,7},{6,4},{7,5},{8,10},{9,11},{10,... | collective-permute-start | bytes 3145736 | tf_op jit(solution)/shard_map/ppermute | solution.py:877
  390.2 25.0 %shard_map.316 = (bf16[1024,2048]{1,0:T(8,128)(2,1)}, bf16[1024,2048]{1,0:T(8,128)(2,1)}) custom-call(s32[4]{0:T(128)S(1)} %iota.44.columns, bf16[2048,2048]{1,0:T(8,128)(2,1)} %get-tuple-element.156.refs_0_.left, bf16[512,2048]{1,0:T(8,128)(2,1)} %collective-permute-done.10.refs_2_.refs_1_, bf16[512,2048]{1,0:T(8,128)(2,1)} %collective-permute-done.11.refs_3_.refs_2_, ...), custom_call_target="tpu_custom_call" | custom-call | flops 1 | bytes 1 | tf_op jit(solution)/shard_map/pallas_call | solution.py:655
  415.3 3.7 add_convert_fusion.7
  419.1 25.1 %shard_map.317 = (bf16[1024,2048]{1,0:T(8,128)(2,1)}, bf16[1024,2048]{1,0:T(8,128)(2,1)}) custom-call(s32[4]{0:T(128)S(1)} %iota.43.columns, bf16[2048,2048]{1,0:T(8,128)(2,1)} %get-tuple-element.190.refs_0_, bf16[512,2048]{1,0:T(8,128)(2,1)} %collective-permute-done.12.refs_0_.refs_1_, bf16[512,2048]{1,0:T(8,128)(2,1)} %collective-permute-done.13.refs_1_.refs_2_, ...), custom_call_target="tpu_custom_call" | custom-call | flops 17179869184 | bytes 16777216 | tf_op jit(solution)/shard_map/pallas_call | solution.py:655
  451.9 3.9 convert_reduce_fusion.4
  455.8 6.8 add_convert_fusion.1
  462.6 7.3 shard_map.318
  470.0 5.0 shard_map.319
  476.5 4.7 all-to-all-start.1
  481.2 7.8 add_convert_fusion
  492.3 7.3 shard_map.320
  499.6 8.3 all-to-all-done.1
  510.7 53.9 %shard_map.321 = (bf16[2048,768]{1,0:T(8,128)(2,1)}, bf16[2048,768]{1,0:T(8,128)(2,1)}) custom-call(s32[2]{0:T(128)S(1)} %convert_reduce_fusion.6.counts, s32[2,4]{1,0:T(2,128)S(1)} %xor_add_fusion.slots, bf16[1536,768]{1,0:T(8,128)(2,1)} %shard_map.307.refs_0_, bf16[512,768]{1,0:T(8,128)(2,1)S(1)} %copy-done.15, ...), custom_call_target="tpu_custom_call" | custom-call | flops 1 | bytes 1 | tf_op jit(solution)/shard_map/pallas_call | solution.py:301
  567.2 22.0 %shard_map.322 = (bf16[512,2048]{1,0:T(8,128)(2,1)S(1)}, bf16[512,2048]{1,0:T(8,128)(2,1)S(1)}, bf16[1024,2048]{1,0:T(8,128)(2,1)}) custom-call(s32[4]{0:T(128)S(1)} %copy-done.17, s32[4]{0:T(128)S(1)} %gather_fusion.1, bf16[2048,2048]{1,0:T(8,128)(2,1)} %get-tuple-element.156.refs_0_.left, bf16[1024,2048]{1,0:T(8,128)(2,1)} %own.1, ...), custom_call_target="tpu_custom_call" | custom-call | flops 1 | bytes 1 | tf_op jit(solution)/shard_map/pallas_call | solution.py:476
  590.5 12.8 %shard_map.323 = bf16[768,2048]{1,0:T(8,128)(2,1)} custom-call(s32[3]{0:T(128)S(1)} %get-tuple-element.270.columns, bf16[2048,768]{1,0:T(8,128)(2,1)} %collective-permute-done.31.refs_0_.theirs, bf16[512,2048]{1,0:T(8,128)(2,1)S(1)} %copy-done.3, bf16[512,2048]{1,0:T(8,128)(2,1)} %copy-done.4, bf16[512,2048]{1,0:T(8,128)(2,1)} %copy-done.24, ...), custom_call_target="tpu_custom_call" | custom-call | flops 1 | bytes 1 | tf_op jit(solution)/shard_map/pallas_call | solution.py:655
  605.4 23.6 %collective-permute-done.30 = bf16[256,2048]{1,0:T(8,128)(2,1)S(1)} collective-permute-done((bf16[256,2048]{1,0:T(8,128)(2,1)S(1)}, bf16[256,2048]{1,0:T(8,128)(2,1)S(1)}, u32[]{:S(2)}, u32[]{:S(2)}) %collective-permute-start.30) | collective-permute-done | bytes 1048608 | tf_op jit(solution)/shard_map/ppermute | solution.py:877
  633.3 19.4 %shard_map.324 = (bf16[512,2048]{1,0:T(8,128)(2,1)}, bf16[512,2048]{1,0:T(8,128)(2,1)}, bf16[1024,2048]{1,0:T(8,128)(2,1)}) custom-call(s32[4]{0:T(128)S(1)} %copy-done.18, s32[2,3]{1,0:T(2,128)S(1)} %pad_add_fusion.parts, s32[4]{0:T(128)S(1)} %gather_fusion, bf16[2048,768]{1,0:T(8,128)(2,1)} %get-tuple-element.191.mine.refs_0_, ...), custom_call_target="tpu_custom_call" | custom-call | flops 1 | bytes 1 | tf_op jit(solution)/shard_map/pallas_call | solution.py:608
  654.4 13.8 %shard_map.325 = (bf16[256,2048]{1,0:T(8,128)(2,1)S(1)}, bf16[256,2048]{1,0:T(8,128)(2,1)S(1)}, bf16[256,2048]{1,0:T(8,128)(2,1)}) custom-call(s32[3]{0:T(128)S(1)} %get-tuple-element.269.columns, bf16[2048,768]{1,0:T(8,128)(2,1)} %get-tuple-element.191.mine.refs_0_, bf16[512,2048]{1,0:T(8,128)(2,1)} %copy-done.1, bf16[512,2048]{1,0:T(8,128)(2,1)} %copy-done.4, ...), custom_call_target="tpu_custom_call" | custom-call | flops 1 | bytes 1 | tf_op jit(solution)/shard_map/pallas_call | solution.py:655
  676.9 15.0 %collective-permute-done.38 = bf16[256,2048]{1,0:T(8,128)(2,1)S(1)} collective-permute-done((bf16[256,2048]{1,0:T(8,128)(2,1)S(1)}, bf16[256,2048]{1,0:T(8,128)(2,1)S(1)}, u32[]{:S(2)}, u32[]{:S(2)}) %collective-permute-start.38) | collective-permute-done | bytes 1048608 | tf_op jit(solution)/shard_map/ppermute | solution.py:1134
  692.8 6.0 collective-permute-start.35
  698.8 83.5 %all-reduce.7.cloned.1.call-done = (bf16[1024,2048]{1,0:T(8,128)(2,1)}, bf16[1024,2048]{1,0:T(8,128)(2,1)}) async-done(((bf16[1024,2048]{1,0:T(8,128)(2,1)}, bf16[1024,2048]{1,0:T(8,128)(2,1)}), (bf16[1024,2048]{1,0:T(8,128)(2,1)}, bf16[1024,2048]{1,0:T(8,128)(2,1)})) %all-reduce.7.cloned.1.call-update) | async-done | bytes 8388624 | tf_op jit(solution)/shard_map/psum | solution.py:1095
  785.8 4.5 add_convert_fusion.5
  794.4 4.7 convert_reduce_fusion
  801.1 15.5 %collective-permute-done.42 = bf16[256,2048]{1,0:T(8,128)(2,1)S(1)} collective-permute-done((bf16[256,2048]{1,0:T(8,128)(2,1)}, bf16[256,2048]{1,0:T(8,128)(2,1)S(1)}, u32[]{:S(2)}, u32[]{:S(2)}) %collective-permute-start.42) | collective-permute-done | bytes 1048608 | tf_op jit(solution)/shard_map/ppermute | solution.py:877
  818.3 3.8 fusion.24
  831.5 31.8 %collective-permute-done.40 = bf16[512,2048]{1,0:T(8,128)(2,1)} collective-permute-done((bf16[512,2048]{1,0:T(8,128)(2,1)}, bf16[512,2048]{1,0:T(8,128)(2,1)}, u32[]{:S(2)}, u32[]{:S(2)}) %collective-permute-start.40) | collective-permute-done | bytes 2097184 | tf_op jit(solution)/shard_map/ppermute | solution.py:877
  872.2 5.2 collective-permute-done.50
  877.4 6.0 collective-permute-done.51
  884.8 4.4 convert_element_type.284
  889.2 4.6 convert_element_type.283
  898.5 64.6 %all-reduce.5.cloned.1.call-done = (bf16[256,2048]{1,0:T(8,128)(2,1)}, bf16[256,2048]{1,0:T(8,128)(2,1)}, bf16[256,2048]{1,0:T(8,128)(2,1)}, bf16[256,2048]{1,0:T(8,128)(2,1)}) async-done(((bf16[256,2048]{1,0:T(8,128)(2,1)}, bf16[256,2048]{1,0:T(8,128)(2,1)}, bf16[256,2048]{1,0:T(8,128)(2,1)}, bf16[256,2048]{1,0:T(8,128)(2,1)}), (bf16[256,2048]{1,0:T(8,128)(2,1)}, bf16[256,2048]{1,0:T(8,128)(2,1)}, ...) | async-done | bytes 4194320 | tf_op jit(solution)/shard_map/psum | solution.py:1139
  966.0 5.4 maximum_convert_fusion
  (307 shorter events, 142.9 us)
Async XLA Ops:
  7.2 226.0 %all-gather.2.cloned.1.call-start = ((), (), s32[]{:S(2)}) async-start(), calls=%async_computation.2 | async-start | bytes 9437184 | tf_op jit(solution)/shard_map/all_gather | solution.py:1031
  12.6 71.1 %collective-permute-start = (bf16[512,2048]{1,0:T(8,128)(2,1)S(1)}, bf16[512,2048]{1,0:T(8,128)(2,1)S(1)}, u32[]{:S(2)}, u32[]{:S(2)}) collective-permute-start(bf16[512,2048]{1,0:T(8,128)(2,1)S(1)} %fusion.7.refs_0_.refs_1_), channel_id=1, source_target_pairs={{0,2},{1,3},{2,0},{3,1},{4,6},{5,7},{6,4},{7,5},{8,10},{9,11},{10,... | collective-permute-start | bytes 6291464 | tf_op jit(solution)/shard_map/ppermute | solution.py:877
  15.6 68.1 %collective-permute-start.1 = (bf16[512,2048]{1,0:T(8,128)(2,1)S(1)}, bf16[512,2048]{1,0:T(8,128)(2,1)S(1)}, u32[]{:S(2)}, u32[]{:S(2)}) collective-permute-start(bf16[512,2048]{1,0:T(8,128)(2,1)S(1)} %fusion.7.refs_0_.refs_1_), channel_id=1, source_target_pairs={{0,4},{1,5},{2,6},{3,7},{4,0},{5,1},{6,2},{7,3},{8,12},{9,13},{10,... | collective-permute-start | bytes 6291464 | tf_op jit(solution)/shard_map/ppermute | solution.py:877
  19.6 54.3 %collective-permute-start.3 = (bf16[256,2048]{1,0:T(8,128)(2,1)S(1)}, bf16[256,2048]{1,0:T(8,128)(2,1)S(1)}, u32[]{:S(2)}, u32[]{:S(2)}) collective-permute-start(bf16[256,2048]{1,0:T(8,128)(2,1)S(1)} %get-tuple-element.248), channel_id=1, source_target_pairs={{0,1},{1,4},{2,7},{3,2},{4,5},{5,0},{6,3},{7,6},{8,9},{9,12},{10,1... | collective-permute-start | bytes 3145736 | tf_op jit(solution)/shard_map/ppermute | solution.py:1008
  20.3 63.3 %collective-permute-start.4 = (bf16[256,2048]{1,0:T(8,128)(2,1)S(1)}, bf16[256,2048]{1,0:T(8,128)(2,1)S(1)}, u32[]{:S(2)}, u32[]{:S(2)}) collective-permute-start(bf16[256,2048]{1,0:T(8,128)(2,1)S(1)} %get-tuple-element.246), channel_id=1, source_target_pairs={{0,2},{1,5},{2,0},{3,3},{4,6},{5,1},{6,4},{7,7},{8,10},{9,13},{10,... | collective-permute-start | bytes 3145736 | tf_op jit(solution)/shard_map/ppermute | solution.py:1008
  88.2 28.7 %collective-permute-start.5 = (bf16[256,2048]{1,0:T(8,128)(2,1)}, bf16[256,2048]{1,0:T(8,128)(2,1)S(1)}, u32[]{:S(2)}, u32[]{:S(2)}) collective-permute-start(bf16[256,2048]{1,0:T(8,128)(2,1)} %slice.276), channel_id=1, source_target_pairs={{0,2},{1,3},{2,0},{3,1},{4,6},{5,7},{6,4},{7,5},{8,10},{9,11},{10,... | collective-permute-start | bytes 3145736 | tf_op jit(solution)/shard_map/ppermute | solution.py:877
  89.9 27.0 %collective-permute-start.6 = (bf16[256,2048]{1,0:T(8,128)(2,1)}, bf16[256,2048]{1,0:T(8,128)(2,1)}, u32[]{:S(2)}, u32[]{:S(2)}) collective-permute-start(bf16[256,2048]{1,0:T(8,128)(2,1)} %slice.277), channel_id=1, source_target_pairs={{0,4},{1,5},{2,6},{3,7},{4,0},{5,1},{6,2},{7,3},{8,12},{9,13},{10,... | collective-permute-start | bytes 3145736 | tf_op jit(solution)/shard_map/ppermute | solution.py:877
  127.4 105.8 %collective-permute-start.10 = (bf16[512,2048]{1,0:T(8,128)(2,1)}, bf16[512,2048]{1,0:T(8,128)(2,1)}, u32[]{:S(2)}, u32[]{:S(2)}) collective-permute-start(bf16[512,2048]{1,0:T(8,128)(2,1)} %get-tuple-element.221.refs_1_.refs_3_), channel_id=1, source_target_pairs={{0,2},{1,3},{2,0},{3,1},{4,6},{5,7},{6,4},{7,5},{8,10},{9,11},{10,... | collective-permute-start | bytes 6291464 | tf_op jit(solution)/shard_map/ppermute | solution.py:877
  128.8 104.4 %collective-permute-start.11 = (bf16[512,2048]{1,0:T(8,128)(2,1)}, bf16[512,2048]{1,0:T(8,128)(2,1)}, u32[]{:S(2)}, u32[]{:S(2)}) collective-permute-start(bf16[512,2048]{1,0:T(8,128)(2,1)} %get-tuple-element.221.refs_1_.refs_3_), channel_id=1, source_target_pairs={{0,4},{1,5},{2,6},{3,7},{4,0},{5,1},{6,2},{7,3},{8,12},{9,13},{10,... | collective-permute-start | bytes 6291464 | tf_op jit(solution)/shard_map/ppermute | solution.py:877
  176.2 53.7 %all-to-all-start = ((bf16[8,512,256]{2,1,0:T(8,128)(2,1)}), bf16[8,512,256]{2,1,0:T(8,128)(2,1)}, u32[]{:S(2)}, u32[]{:S(2)}) async-start(bf16[8,512,256]{2,1,0:T(8,128)(2,1)} %bitcast.30), calls=%async_computation | async-start | bytes 4194304 | tf_op jit(solution)/shard_map/all_to_all | solution.py:1037
  181.1 74.6 %collective-permute-start.14 = (bf16[1024,2048]{1,0:T(8,128)(2,1)}, bf16[1024,2048]{1,0:T(8,128)(2,1)}, u32[]{:S(2)}, u32[]{:S(2)}) collective-permute-start(bf16[1024,2048]{1,0:T(8,128)(2,1)} %refs_4_.5), channel_id=1, source_target_pairs={{0,1},{1,0},{2,3},{3,2},{4,5},{5,4},{6,7},{7,6},{8,9},{9,8},{10,11... | collective-permute-start | bytes 12582920 | tf_op jit(solution)/shard_map/ppermute | solution.py:877
  181.6 74.2 %collective-permute-start.15 = (bf16[1024,2048]{1,0:T(8,128)(2,1)}, bf16[1024,2048]{1,0:T(8,128)(2,1)}, u32[]{:S(2)}, u32[]{:S(2)}) collective-permute-start(bf16[1024,2048]{1,0:T(8,128)(2,1)} %own.1), channel_id=1, source_target_pairs={{0,1},{1,0},{2,3},{3,2},{4,5},{5,4},{6,7},{7,6},{8,9},{9,8},{10,11... | collective-permute-start | bytes 12582920 | tf_op jit(solution)/shard_map/ppermute | solution.py:877
  251.3 46.9 %collective-permute-start.12 = (bf16[512,2048]{1,0:T(8,128)(2,1)}, bf16[512,2048]{1,0:T(8,128)(2,1)}, u32[]{:S(2)}, u32[]{:S(2)}) collective-permute-start(bf16[512,2048]{1,0:T(8,128)(2,1)} %add_convert_fusion.2.refs_0_.refs_3_), channel_id=1, source_target_pairs={{0,2},{1,3},{2,0},{3,1},{4,6},{5,7},{6,4},{7,5},{8,10},{9,11},{10,... | collective-permute-start | bytes 6291464 | tf_op jit(solution)/shard_map/ppermute | solution.py:877
  252.4 47.3 %collective-permute-start.13 = (bf16[512,2048]{1,0:T(8,128)(2,1)}, bf16[512,2048]{1,0:T(8,128)(2,1)}, u32[]{:S(2)}, u32[]{:S(2)}) collective-permute-start(bf16[512,2048]{1,0:T(8,128)(2,1)} %add_convert_fusion.2.refs_0_.refs_3_), channel_id=1, source_target_pairs={{0,4},{1,5},{2,6},{3,7},{4,0},{5,1},{6,2},{7,3},{8,12},{9,13},{10,... | collective-permute-start | bytes 6291464 | tf_op jit(solution)/shard_map/ppermute | solution.py:877
  301.9 56.5 %collective-permute-start.16 = (bf16[256,2048]{1,0:T(8,128)(2,1)}, bf16[256,2048]{1,0:T(8,128)(2,1)S(1)}, u32[]{:S(2)}, u32[]{:S(2)}) collective-permute-start(bf16[256,2048]{1,0:T(8,128)(2,1)} %slice.219), channel_id=1, source_target_pairs={{0,2},{1,3},{2,0},{3,1},{4,6},{5,7},{6,4},{7,5},{8,10},{9,11},{10,... | collective-permute-start | bytes 3145736 | tf_op jit(solution)/shard_map/ppermute | solution.py:877
  303.5 55.7 %collective-permute-start.17 = (bf16[256,2048]{1,0:T(8,128)(2,1)S(1)}, bf16[256,2048]{1,0:T(8,128)(2,1)S(1)}, u32[]{:S(2)}, u32[]{:S(2)}) collective-permute-start(bf16[256,2048]{1,0:T(8,128)(2,1)S(1)} %slice.220), channel_id=1, source_target_pairs={{0,4},{1,5},{2,6},{3,7},{4,0},{5,1},{6,2},{7,3},{8,12},{9,13},{10,... | collective-permute-start | bytes 3145736 | tf_op jit(solution)/shard_map/ppermute | solution.py:877
  304.1 55.1 %collective-permute-start.18 = (bf16[256,2048]{1,0:T(8,128)(2,1)S(1)}, bf16[256,2048]{1,0:T(8,128)(2,1)S(1)}, u32[]{:S(2)}, u32[]{:S(2)}) collective-permute-start(bf16[256,2048]{1,0:T(8,128)(2,1)S(1)} %slice.221), channel_id=1, source_target_pairs={{0,2},{1,3},{2,0},{3,1},{4,6},{5,7},{6,4},{7,5},{8,10},{9,11},{10,... | collective-permute-start | bytes 3145736 | tf_op jit(solution)/shard_map/ppermute | solution.py:877
  308.2 51.1 %collective-permute-start.19 = (bf16[256,2048]{1,0:T(8,128)(2,1)}, bf16[256,2048]{1,0:T(8,128)(2,1)S(1)}, u32[]{:S(2)}, u32[]{:S(2)}) collective-permute-start(bf16[256,2048]{1,0:T(8,128)(2,1)} %slice.222), channel_id=1, source_target_pairs={{0,4},{1,5},{2,6},{3,7},{4,0},{5,1},{6,2},{7,3},{8,12},{9,13},{10,... | collective-permute-start | bytes 3145736 | tf_op jit(solution)/shard_map/ppermute | solution.py:877
  358.4 30.5 %collective-permute-start.22 = (bf16[256,2048]{1,0:T(8,128)(2,1)S(1)}, bf16[256,2048]{1,0:T(8,128)(2,1)S(1)}, u32[]{:S(2)}, u32[]{:S(2)}) collective-permute-start(bf16[256,2048]{1,0:T(8,128)(2,1)S(1)} %get-tuple-element.245), channel_id=1, source_target_pairs={{0,2},{1,3},{2,0},{3,1},{4,6},{5,7},{6,4},{7,5},{8,10},{9,11},{10,... | collective-permute-start | bytes 3145736 | tf_op jit(solution)/shard_map/ppermute | solution.py:877
  358.5 30.4 %collective-permute-start.23 = (bf16[256,2048]{1,0:T(8,128)(2,1)S(1)}, bf16[256,2048]{1,0:T(8,128)(2,1)S(1)}, u32[]{:S(2)}, u32[]{:S(2)}) collective-permute-start(bf16[256,2048]{1,0:T(8,128)(2,1)S(1)} %get-tuple-element.244), channel_id=1, source_target_pairs={{0,4},{1,5},{2,6},{3,7},{4,0},{5,1},{6,2},{7,3},{8,12},{9,13},{10,... | collective-permute-start | bytes 3145736 | tf_op jit(solution)/shard_map/ppermute | solution.py:877
  372.4 42.9 %collective-permute-start.20 = (bf16[256,2048]{1,0:T(8,128)(2,1)}, bf16[256,2048]{1,0:T(8,128)(2,1)}, u32[]{:S(2)}, u32[]{:S(2)}) collective-permute-start(bf16[256,2048]{1,0:T(8,128)(2,1)} %get-tuple-element.252), channel_id=1, source_target_pairs={{0,2},{1,3},{2,0},{3,1},{4,6},{5,7},{6,4},{7,5},{8,10},{9,11},{10,... | collective-permute-start | bytes 3145736 | tf_op jit(solution)/shard_map/ppermute | solution.py:877
  386.9 28.4 %collective-permute-start.21 = (bf16[256,2048]{1,0:T(8,128)(2,1)}, bf16[256,2048]{1,0:T(8,128)(2,1)}, u32[]{:S(2)}, u32[]{:S(2)}) collective-permute-start(bf16[256,2048]{1,0:T(8,128)(2,1)} %get-tuple-element.251), channel_id=1, source_target_pairs={{0,4},{1,5},{2,6},{3,7},{4,0},{5,1},{6,2},{7,3},{8,12},{9,13},{10,... | collective-permute-start | bytes 3145736 | tf_op jit(solution)/shard_map/ppermute | solution.py:877
  415.2 40.6 %collective-permute-start.27 = (bf16[1024,2048]{1,0:T(8,128)(2,1)}, bf16[1024,2048]{1,0:T(8,128)(2,1)}, u32[]{:S(2)}, u32[]{:S(2)}) collective-permute-start(bf16[1024,2048]{1,0:T(8,128)(2,1)} %get-tuple-element.138), channel_id=1, source_target_pairs={{0,1},{1,0},{2,3},{3,2},{4,5},{5,4},{6,7},{7,6},{8,9},{9,8},{10,11... | collective-permute-start | bytes 12582920 | tf_op jit(solution)/shard_map/ppermute | solution.py:877
  419.0 25.8 %collective-permute-start.25 = (bf16[256,2048]{1,0:T(8,128)(2,1)}, bf16[256,2048]{1,0:T(8,128)(2,1)S(1)}, u32[]{:S(2)}, u32[]{:S(2)}) collective-permute-start(bf16[256,2048]{1,0:T(8,128)(2,1)} %get-tuple-element.243), channel_id=1, source_target_pairs={{0,4},{1,5},{2,6},{3,7},{4,0},{5,1},{6,2},{7,3},{8,12},{9,13},{10,... | collective-permute-start | bytes 3145736 | tf_op jit(solution)/shard_map/ppermute | solution.py:877
  419.1 25.7 %collective-permute-start.26 = (bf16[256,2048]{1,0:T(8,128)(2,1)}, bf16[256,2048]{1,0:T(8,128)(2,1)S(1)}, u32[]{:S(2)}, u32[]{:S(2)}) collective-permute-start(bf16[256,2048]{1,0:T(8,128)(2,1)} %get-tuple-element.242), channel_id=1, source_target_pairs={{0,2},{1,3},{2,0},{3,1},{4,6},{5,7},{6,4},{7,5},{8,10},{9,11},{10,... | collective-permute-start | bytes 3145736 | tf_op jit(solution)/shard_map/ppermute | solution.py:877
  444.2 37.0 %collective-permute-start.24 = (bf16[1024,2048]{1,0:T(8,128)(2,1)}, bf16[1024,2048]{1,0:T(8,128)(2,1)}, u32[]{:S(2)}, u32[]{:S(2)}) collective-permute-start(bf16[1024,2048]{1,0:T(8,128)(2,1)} %get-tuple-element.143), channel_id=1, source_target_pairs={{0,1},{1,0},{2,3},{3,2},{4,5},{5,4},{6,7},{7,6},{8,9},{9,8},{10,11... | collective-permute-start | bytes 12582920 | tf_op jit(solution)/shard_map/ppermute | solution.py:877
  476.5 31.4 %all-to-all-start.1 = ((bf16[512,8,256]{2,0,1:T(8,128)(2,1)}), bf16[512,8,256]{2,0,1:T(8,128)(2,1)}, u32[]{:S(2)}, u32[]{:S(2)}) async-start(bf16[512,8,256]{2,0,1:T(8,128)(2,1)} %bitcast.39), calls=%async_computation.1 | async-start | bytes 4194304 | tf_op jit(solution)/shard_map/all_to_all | solution.py:1090
  481.2 301.1 %all-reduce.7.cloned.1.call-start = ((), (), s32[]{:S(2)}) async-start(), calls=%async_computation.4 | async-start | bytes 16777216 | tf_op jit(solution)/shard_map/psum | solution.py:1095
  489.0 474.1 %all-reduce.5.cloned.1.call-start = ((), (), s32[]{:S(2)}) async-start(), calls=%async_computation.3 | async-start | bytes 8388608 | tf_op jit(solution)/shard_map/psum | solution.py:1139
  564.6 25.9 %collective-permute-start.31 = (bf16[2048,768]{1,0:T(8,128)(2,1)}, bf16[2048,768]{1,0:T(8,128)(2,1)}, u32[]{:S(2)}, u32[]{:S(2)}) collective-permute-start(bf16[2048,768]{1,0:T(8,128)(2,1)} %get-tuple-element.192), channel_id=1, source_target_pairs={{0,1},{1,0},{2,3},{3,2},{4,5},{5,4},{6,7},{7,6},{8,9},{9,8},{10,11... | collective-permute-start | bytes 9437192 | tf_op jit(solution)/shard_map/ppermute | solution.py:877
  603.3 49.4 %collective-permute-start.36 = (bf16[768,2048]{1,0:T(8,128)(2,1)}, bf16[768,2048]{1,0:T(8,128)(2,1)S(1)}, u32[]{:S(2)}, u32[]{:S(2)}) collective-permute-start(bf16[768,2048]{1,0:T(8,128)(2,1)} %shard_map.323), channel_id=1, source_target_pairs={{0,1},{1,0},{2,3},{3,2},{4,5},{5,4},{6,7},{7,6},{8,9},{9,8},{10,11... | collective-permute-start | bytes 9437192 | tf_op jit(solution)/shard_map/ppermute | solution.py:877
  603.7 25.3 %collective-permute-start.30 = (bf16[256,2048]{1,0:T(8,128)(2,1)S(1)}, bf16[256,2048]{1,0:T(8,128)(2,1)S(1)}, u32[]{:S(2)}, u32[]{:S(2)}) collective-permute-start(bf16[256,2048]{1,0:T(8,128)(2,1)S(1)} %pad_maximum_fusion.4), channel_id=1, source_target_pairs={{0,4},{1,5},{2,6},{3,7},{4,0},{5,1},{6,2},{7,3},{8,12},{9,13},{10,... | collective-permute-start | bytes 3145736 | tf_op jit(solution)/shard_map/ppermute | solution.py:877
  605.4 24.9 %collective-permute-start.29 = (bf16[256,2048]{1,0:T(8,128)(2,1)S(1)}, bf16[256,2048]{1,0:T(8,128)(2,1)S(1)}, u32[]{:S(2)}, u32[]{:S(2)}) collective-permute-start(bf16[256,2048]{1,0:T(8,128)(2,1)S(1)} %pad_maximum_fusion.3), channel_id=1, source_target_pairs={{0,2},{1,3},{2,0},{3,1},{4,6},{5,7},{6,4},{7,5},{8,10},{9,11},{10,... | collective-permute-start | bytes 3145736 | tf_op jit(solution)/shard_map/ppermute | solution.py:877
  669.0 22.9 %collective-permute-start.38 = (bf16[256,2048]{1,0:T(8,128)(2,1)S(1)}, bf16[256,2048]{1,0:T(8,128)(2,1)S(1)}, u32[]{:S(2)}, u32[]{:S(2)}) collective-permute-start(bf16[256,2048]{1,0:T(8,128)(2,1)S(1)} %get-tuple-element.171), channel_id=1, source_target_pairs={{1,0},{4,1},{7,2},{2,3},{5,4},{0,5},{3,6},{6,7},{9,8},{12,9},{15,1... | collective-permute-start | bytes 3145736 | tf_op jit(solution)/shard_map/ppermute | solution.py:1134
  670.8 115.0 %collective-permute-start.32 = (bf16[512,2048]{1,0:T(8,128)(2,1)}, bf16[512,2048]{1,0:T(8,128)(2,1)}, u32[]{:S(2)}, u32[]{:S(2)}) collective-permute-start(bf16[512,2048]{1,0:T(8,128)(2,1)} %get-tuple-element.166), channel_id=1, source_target_pairs={{0,2},{1,3},{2,0},{3,1},{4,6},{5,7},{6,4},{7,5},{8,10},{9,11},{10,... | collective-permute-start | bytes 6291464 | tf_op jit(solution)/shard_map/ppermute | solution.py:877
  672.0 113.8 %collective-permute-start.33 = (bf16[512,2048]{1,0:T(8,128)(2,1)}, bf16[512,2048]{1,0:T(8,128)(2,1)}, u32[]{:S(2)}, u32[]{:S(2)}) collective-permute-start(bf16[512,2048]{1,0:T(8,128)(2,1)} %get-tuple-element.167), channel_id=1, source_target_pairs={{0,4},{1,5},{2,6},{3,7},{4,0},{5,1},{6,2},{7,3},{8,12},{9,13},{10,... | collective-permute-start | bytes 6291464 | tf_op jit(solution)/shard_map/ppermute | solution.py:877
  674.0 108.3 %collective-permute-start.39 = (bf16[256,2048]{1,0:T(8,128)(2,1)}, bf16[256,2048]{1,0:T(8,128)(2,1)}, u32[]{:S(2)}, u32[]{:S(2)}) collective-permute-start(bf16[256,2048]{1,0:T(8,128)(2,1)} %get-tuple-element.172), channel_id=1, source_target_pairs={{2,0},{5,1},{0,2},{3,3},{6,4},{1,5},{4,6},{7,7},{10,8},{13,9},{8,1... | collective-permute-start | bytes 3145736 | tf_op jit(solution)/shard_map/ppermute | solution.py:1134
  676.6 105.7 %collective-permute-start.34 = (bf16[128,2048]{1,0:T(8,128)(2,1)}, bf16[128,2048]{1,0:T(8,128)(2,1)}, u32[]{:S(2)}, u32[]{:S(2)}) collective-permute-start(bf16[128,2048]{1,0:T(8,128)(2,1)} %get-tuple-element.237), channel_id=1, source_target_pairs={{0,4},{1,5},{2,6},{3,7},{4,0},{5,1},{6,2},{7,3},{8,12},{9,13},{10,... | collective-permute-start | bytes 1572872 | tf_op jit(solution)/shard_map/ppermute | solution.py:877
  692.8 89.5 %collective-permute-start.35 = (bf16[128,2048]{1,0:T(8,128)(2,1)}, bf16[128,2048]{1,0:T(8,128)(2,1)}, u32[]{:S(2)}, u32[]{:S(2)}) collective-permute-start(bf16[128,2048]{1,0:T(8,128)(2,1)} %get-tuple-element.236), channel_id=1, source_target_pairs={{0,2},{1,3},{2,0},{3,1},{4,6},{5,7},{6,4},{7,5},{8,10},{9,11},{10,... | collective-permute-start | bytes 1572872 | tf_op jit(solution)/shard_map/ppermute | solution.py:877
  790.4 26.3 %collective-permute-start.42 = (bf16[256,2048]{1,0:T(8,128)(2,1)}, bf16[256,2048]{1,0:T(8,128)(2,1)S(1)}, u32[]{:S(2)}, u32[]{:S(2)}) collective-permute-start(bf16[256,2048]{1,0:T(8,128)(2,1)} %get-tuple-element.233), channel_id=1, source_target_pairs={{0,4},{1,5},{2,6},{3,7},{4,0},{5,1},{6,2},{7,3},{8,12},{9,13},{10,... | collective-permute-start | bytes 3145736 | tf_op jit(solution)/shard_map/ppermute | solution.py:877
  791.9 26.4 %collective-permute-start.43 = (bf16[256,2048]{1,0:T(8,128)(2,1)}, bf16[256,2048]{1,0:T(8,128)(2,1)}, u32[]{:S(2)}, u32[]{:S(2)}) collective-permute-start(bf16[256,2048]{1,0:T(8,128)(2,1)} %get-tuple-element.232), channel_id=1, source_target_pairs={{0,2},{1,3},{2,0},{3,1},{4,6},{5,7},{6,4},{7,5},{8,10},{9,11},{10,... | collective-permute-start | bytes 3145736 | tf_op jit(solution)/shard_map/ppermute | solution.py:877
  799.5 63.8 %collective-permute-start.40 = (bf16[512,2048]{1,0:T(8,128)(2,1)}, bf16[512,2048]{1,0:T(8,128)(2,1)}, u32[]{:S(2)}, u32[]{:S(2)}) collective-permute-start(bf16[512,2048]{1,0:T(8,128)(2,1)} %copy-done.20), channel_id=1, source_target_pairs={{0,2},{1,3},{2,0},{3,1},{4,6},{5,7},{6,4},{7,5},{8,10},{9,11},{10,... | collective-permute-start | bytes 6291464 | tf_op jit(solution)/shard_map/ppermute | solution.py:877
  800.1 63.1 %collective-permute-start.41 = (bf16[512,2048]{1,0:T(8,128)(2,1)}, bf16[512,2048]{1,0:T(8,128)(2,1)}, u32[]{:S(2)}, u32[]{:S(2)}) collective-permute-start(bf16[512,2048]{1,0:T(8,128)(2,1)} %copy-done.19), channel_id=1, source_target_pairs={{0,4},{1,5},{2,6},{3,7},{4,0},{5,1},{6,2},{7,3},{8,12},{9,13},{10,... | collective-permute-start | bytes 6291464 | tf_op jit(solution)/shard_map/ppermute | solution.py:877
  827.9 39.8 %collective-permute-start.47 = (f32[24576]{0:T(1024)S(1)}, f32[24576]{0:T(1024)S(1)}, u32[]{:S(2)}, u32[]{:S(2)}) collective-permute-start(f32[24576]{0:T(1024)S(1)} %add.282), channel_id=1, source_target_pairs={{0,2},{1,3},{2,0},{3,1},{4,6},{5,7},{6,4},{7,5},{8,10},{9,11},{10,... | collective-permute-start | bytes 294920 | tf_op jit(solution)/shard_map/ppermute | solution.py:877
  829.4 38.2 %collective-permute-start.48 = (f32[24576]{0:T(1024)S(1)}, f32[24576]{0:T(1024)S(1)}, u32[]{:S(2)}, u32[]{:S(2)}) collective-permute-start(f32[24576]{0:T(1024)S(1)} %add.282), channel_id=1, source_target_pairs={{0,4},{1,5},{2,6},{3,7},{4,0},{5,1},{6,2},{7,3},{8,12},{9,13},{10,... | collective-permute-start | bytes 294920 | tf_op jit(solution)/shard_map/ppermute | solution.py:877
  830.0 37.7 %collective-permute-start.49 = (f32[24576]{0:T(1024)S(1)}, f32[24576]{0:T(1024)S(1)}, u32[]{:S(2)}, u32[]{:S(2)}) collective-permute-start(f32[24576]{0:T(1024)S(1)} %add.282), channel_id=1, source_target_pairs={{0,6},{1,7},{2,4},{3,5},{4,2},{5,3},{6,0},{7,1},{8,14},{9,15},{10,... | collective-permute-start | bytes 294920 | tf_op jit(solution)/shard_map/ppermute | solution.py:877
  865.6 28.2 %collective-permute-start.44 = (bf16[256,2048]{1,0:T(8,128)(2,1)S(1)}, bf16[256,2048]{1,0:T(8,128)(2,1)S(1)}, u32[]{:S(2)}, u32[]{:S(2)}) collective-permute-start(bf16[256,2048]{1,0:T(8,128)(2,1)S(1)} %get-tuple-element.229), channel_id=1, source_target_pairs={{0,4},{1,5},{2,6},{3,7},{4,0},{5,1},{6,2},{7,3},{8,12},{9,13},{10,... | collective-permute-start | bytes 3145736 | tf_op jit(solution)/shard_map/ppermute | solution.py:877
  866.2 27.6 %collective-permute-start.45 = (bf16[256,2048]{1,0:T(8,128)(2,1)S(1)}, bf16[256,2048]{1,0:T(8,128)(2,1)S(1)}, u32[]{:S(2)}, u32[]{:S(2)}) collective-permute-start(bf16[256,2048]{1,0:T(8,128)(2,1)S(1)} %get-tuple-element.228), channel_id=1, source_target_pairs={{0,2},{1,3},{2,0},{3,1},{4,6},{5,7},{6,4},{7,5},{8,10},{9,11},{10,... | collective-permute-start | bytes 3145736 | tf_op jit(solution)/shard_map/ppermute | solution.py:877
  (68 other events, 900.9 us)
Sparse Core Ops, SparseCore 0:
  117.0 86.3 all-gather.1
  489.2 293.0 all-reduce.6
  800.8 162.3 all-reduce.4
